TPU v7x, 32 devices: a whole 2x2x4 slice. The times are simulated.
32 devices in a mesh: section: 2 (over x), dp: 4 (over y, core), mp: 4 (over z).
Axes of the slice: x: 2, y: 2, z: 4, core: 2. Of those that a mesh axis runs over, the one named last changes fastest.
Arguments:
- layer_in: bfloat16 [2, 8, 1024, 512], P('section', 'dp', 'mp'), may hold values from -6 to 6
- segment_ids: int32 [2, 8, 1024], P(None, 'dp'), may hold values from 0 to 3, never falling along the last dimension, each value on 1 to 769 neighbouring positions
- out_grads: bfloat16 [2, 8, 1024, 512], P('section', 'dp', 'mp'), may hold values from -6 to 6
- w_qkv: bfloat16 [2, 512, 3, 512], P('section', 'dp', None, 'mp'), may hold values from -0.25 to 0.25
- w_out: bfloat16 [2, 512, 512], P('section', 'mp', 'dp'), may hold values from -2 to 2
- w_up: bfloat16 [2, 512, 2048], P('section', 'dp', 'mp'), may hold values from -0.25 to 0.25
- w_down: bfloat16 [2, 2048, 512], P('section', 'mp', 'dp'), may hold values from -0.125 to 0.125
- norm_gain: float32 [2, 3, 512], P('section', None, ('dp', 'mp')), may hold values from 0.5 to 1.5
- norm_bias: float32 [2, 3, 512], P('section', None, ('dp', 'mp')), may hold values from -1.2 to 1.2
- w_qc: bfloat16 [512, 512], P('dp', ('section', 'mp')), may hold values from -0.25 to 0.25
- w_kvc: bfloat16 [512, 2, 512], P('dp', None, ('section', 'mp')), may hold values from -0.25 to 0.25
- w_oc: bfloat16 [512, 512], P(('section', 'mp'), 'dp'), may hold values from -2 to 2
Outputs:
- section_out: bfloat16 [2, 8, 1024, 512], P('section', 'dp', 'mp')
- in_grads: bfloat16 [2, 8, 1024, 512], P('section', 'dp', 'mp')
- grad_qkv: float32 [2, 512, 3, 512], P('section', 'dp', None, 'mp')
- grad_out: float32 [2, 512, 512], P('section', 'mp', 'dp')
- grad_up: float32 [2, 512, 2048], P('section', 'dp', 'mp')
- grad_down: float32 [2, 2048, 512], P('section', 'mp', 'dp')
- grad_gain: float32 [2, 3, 512], P('section', None, ('dp', 'mp'))
- grad_bias: float32 [2, 2, 512], P('section', None, ('dp', 'mp'))
- grad_ffn_bias: float32 [2, 512], P('section', ('dp', 'mp'))
- grad_qc: float32 [512, 512], P('dp', ('section', 'mp'))
- grad_kvc: float32 [512, 2, 512], P('dp', None, ('section', 'mp'))
- grad_oc: float32 [512, 512], P(('section', 'mp'), 'dp')
Inputs may be any that keep to these rules, and one draw needn't show every extreme that they name: `segment_ids`: in every row of both layers the segment numbers start at 0 and never fall, all 4 occur, and one segment has 769 positions.
All inputs are finite; a program needn't handle non-finite values.
Results may differ from a plain program's by a relative error of at most 0.035.
Values may be sent and summed in bfloat16 or wider, within the bound.
No kernel may reach another device: no remote copies, remote signals or barrier semaphores. Data moves between devices by JAX's collectives and lax.ppermute only.
A program may use at most 192 MiB of HBM per device.

v0:
```python
import functools

import jax
import jax.numpy as jnp
from jax import lax
from jax.experimental import pallas as pl
from jax.experimental.pallas import tpu as pltpu
from jax.sharding import PartitionSpec as P

HD = 64
PAIR = 2 * HD
EPS = 1e-05
BIG = 1e30
FACTOR = HD**-0.5
LOG2E = 1.4426950408889634
BF = jnp.bfloat16
F32 = jnp.float32
PAD = 16
VMEM_MIB = {"self_fwd": 56, "feed_fwd": 22, "decoder": 56, "feed_bwd": 56, "self_bwd": 56, "last": 56}


def swap(block, axis, bit):
    count = lax.axis_size(axis)
    return lax.ppermute(block, axis, [(i, i ^ bit) for i in range(count)])


def together(*values):
    return lax.optimization_barrier(values)


def oneway(block, axis, source, target):
    return lax.ppermute(block, axis, [(source, target)])


def dp_bits():
    count = lax.axis_size("dp")
    return [1 << b for b in range(1, count.bit_length() - 1)]


def relative_order():
    order = [0]
    for bit in dp_bits():
        order = order + [a ^ bit for a in order]
    return order + [a ^ 1 for a in order]


def after(x, *others):
    return lax.optimization_barrier((x, others))[0]


def decoder_swap(block, axis, bit):
    count = lax.axis_size(axis)
    pairs = [(count + i, count + (i ^ bit)) for i in range(count)]
    return lax.ppermute(block, ("section", axis), pairs)


def doubled(arrays, bits, move=swap):
    for bit in bits:
        arrays = arrays + [(move(x, "dp", bit), a ^ bit) for x, a in arrays]
    return arrays


def add(a, b):
    return (a.astype(F32) + b.astype(F32)).astype(BF)


def halves(x, axis=0):
    middle = x.shape[axis] // 2
    return lax.slice_in_dim(x, 0, middle, axis=axis), lax.slice_in_dim(x, middle, None, axis=axis)


def fold(keep, got, axis=0):
    (k1, k2), (g1, g2) = halves(keep, axis), halves(got, axis)
    return add(k1, g1), add(k2, g2)


def fold_dp(keep, got, move=swap):
    for bit in dp_bits()[::-1]:
        keep, send = fold(keep, got)
        got = move(send, "dp", bit)
    return keep, got


def fold_dp_rest(keep, got, move=swap):
    for bit in dp_bits()[-2::-1]:
        keep, send = fold(keep, got)
        got = move(send, "dp", bit)
    return keep, got


def fold_mp(keep, got, bit, move=swap):
    keep, send = fold(keep, got, 1)
    return keep, move(send, "mp", bit)


def total(keep, got):
    return keep[0, 0].astype(F32) + got[0, 0].astype(F32)


def rows_in(local):
    rows, span, width = local.shape
    parts = local.reshape(rows, 2, span // 2, width)
    first = (lax.axis_index("dp") & 1) == 0
    keep = jnp.where(first, parts[:, 0], parts[:, 1])
    got = swap(jnp.where(first, parts[:, 1], parts[:, 0]), "dp", 1)
    chip = jnp.where(first, jnp.concatenate([keep, got]), jnp.concatenate([got, keep]))
    return chip


def rows_out(own):
    ways = lax.axis_size("mp")
    return lax.all_to_all(own.reshape(ways, -1, own.shape[1]), "mp", 0, 0, tiled=True)


def rows_placed(chip):
    rows = chip.shape[0] // 2
    first = (lax.axis_index("dp") & 1) == 0
    keep = jnp.where(first, chip[:rows], chip[rows:])
    got = swap(jnp.where(first, chip[rows:], chip[:rows]), "dp", 1)
    return jnp.where(first, jnp.concatenate([keep, got], axis=1), jnp.concatenate([got, keep], axis=1))[None]


def xor_order(x, me):
    count = x.shape[0]
    bit = 1
    while bit < count:
        flipped = x.reshape((count // (2 * bit), 2, bit) + x.shape[1:])[:, ::-1].reshape(x.shape)
        x = jnp.where((me & bit) > 0, flipped, x)
        bit *= 2
    return x


def mm(a, b):
    return jnp.dot(a, b, preferred_element_type=F32)


def nt(a, b):
    return lax.dot_general(a, b, (((1,), (1,)), ((), ())), preferred_element_type=F32)


def stats(states):
    average = jnp.mean(states, axis=-1, keepdims=True)
    centred = states - average
    inv = lax.rsqrt(jnp.mean(centred * centred, axis=-1, keepdims=True) + EPS)
    return centred * inv, inv


def norm_fwd(states, gain, bias):
    hat, _ = stats(states)
    return (hat * gain + bias).astype(BF)


def norm_bwd(states, gain, grad):
    hat, inv = stats(states)
    e = grad * gain
    dx = inv * (
        e - jnp.mean(e, axis=-1, keepdims=True) - hat * jnp.mean(e * hat, axis=-1, keepdims=True)
    )
    return dx, jnp.sum(grad * hat, axis=0, keepdims=True), jnp.sum(grad, axis=0, keepdims=True)


def gelu_parts(pre):
    size = jnp.abs(pre)
    bell = jnp.exp2(pre * pre * (-0.5 * LOG2E))
    t = 1.0 / (1.0 + (0.3275911 * 0.5**0.5) * size)
    poly = 1.061405429 * t - 1.453152027
    poly = poly * t + 1.421413741
    poly = poly * t - 0.284496736
    poly = poly * t + 0.254829592
    tail = 0.5 * poly * t * bell
    return jnp.where(pre >= 0, 1.0 - tail, tail), 0.3989422804014327 * bell


def lanes(rows):
    return lax.broadcasted_iota(jnp.int32, (rows, PAIR), 1)


def head_part(h, real, other):
    lane = lanes(real.shape[0])
    mine = (lane >= HD) if h else (lane < HD)
    return jnp.where(mine, real.astype(F32), other).astype(BF)


def query_code(code):
    return code.astype(F32)


def key_code(code):
    lane = lanes(code.shape[0])
    return jnp.where((lane & (HD - 1)) < 4, (code.astype(F32) - 1.0) * BIG, 0.0)


def start(copies):
    for copy in copies:
        copy.start()
    return copies


def wait(copies):
    for copy in copies:
        copy.wait()


def moves(pairs, sems):
    return [pltpu.make_async_copy(a, b, sems.at[n]) for n, (a, b) in enumerate(pairs)]


def load_weights(me, refs, pieces, target, sems):
    blk = target.shape[1] // len({piece[4] for piece in pieces})
    copies = []
    for n, (ref, index, first, pairs, a, columns) in enumerate(pieces):
        rows = pl.ds(pl.multiple_of((me ^ a) * blk, blk), blk)
        place = target.at[pl.ds(first, pairs), rows, columns]
        copies.append(pltpu.make_async_copy(refs[ref].at[index], place, sems.at[n]))
    return start(copies)


def kernel_order(count):
    order = [0]
    bit = 2
    while bit < count:
        order = order + [a ^ bit for a in order]
        bit *= 2
    return order + [a ^ 1 for a in order]


def store_grad(me, staged, b, keep, send, sems):
    count = 2 * keep.shape[0]
    blk = staged.shape[1] // count
    copies = []
    for n, a in enumerate(kernel_order(count)):
        target = keep.at[n] if n < count // 2 else send.at[n - count // 2]
        rows = pl.ds(pl.multiple_of((me ^ a) * blk, blk), blk)
        copies.append(
            pltpu.make_async_copy(staged.at[b, rows, :], target.at[b], sems.at[b, n])
        )
    return copies


def attend_pair(q, k, v, code_q, code_k, b, logs):
    rows = q.shape[0]
    wide_v = jnp.concatenate([v, jnp.ones_like(v)], axis=1)
    scale = FACTOR * LOG2E
    outs = []
    for h in range(2):
        qa = head_part(h, q, query_code(code_q))
        ka = head_part(h, k, key_code(code_k))
        s = nt(qa, ka)
        top = jnp.max(s, axis=1, keepdims=True)
        p = jnp.exp2((s - top) * scale).astype(BF)
        o = mm(p, wide_v)
        total = o[:, PAIR:]
        outs.append(o[:, :PAIR] / total)
        logs[...] = jnp.where(lanes(rows) == 2 * b + h, top * scale + jnp.log2(total), logs[...])
    return jnp.where(lanes(rows) < HD, outs[0], outs[1])


def attend_pair_back(q, k, v, att, do, code_q, code_k, logs_ref, b):
    rows = q.shape[0]
    scale = FACTOR * LOG2E
    k_t = k.T
    prod = do.astype(F32) * att
    high = prod.astype(BF)
    low = (prod - high.astype(F32)).astype(BF)
    row = lax.broadcasted_iota(jnp.int32, (8, PAIR), 0)
    lane = lax.broadcasted_iota(jnp.int32, (8, PAIR), 1)
    pick = jnp.where((lane // HD) == row, 1.0, 0.0).astype(BF)
    delta = nt(pick, high) + nt(pick, low)
    dk = dv = 0.0
    dq_t = []
    for h in range(2):
        qa = head_part(h, q, query_code(code_q))
        ka = head_part(h, k, key_code(code_k))
        qm = head_part(h, q, 0.0)
        dm = head_part(h, do, 0.0)
        log = logs_ref[pl.ds(2 * b + h, 1), :]
        p_t = jnp.exp2(nt(ka, qa) * scale - log)
        ds_t = (p_t * (nt(v, dm) - delta[h : h + 1])).astype(BF)
        dv = dv + mm(p_t.astype(BF), dm)
        dk = dk + mm(ds_t, qm)
        dq_t.append(mm(k_t, ds_t))
    sub = lax.broadcasted_iota(jnp.int32, (PAIR, rows), 0)
    dq = jnp.where(sub < HD, dq_t[0], dq_t[1]).T
    return (dq * FACTOR).astype(BF), (dk * FACTOR).astype(BF), dv.astype(BF)


def columns(wbuf, pairs, at):
    return jnp.concatenate([wbuf[b, :, at * PAIR : (at + 1) * PAIR] for b in pairs], axis=1)


def lane_pairs(x, count):
    return [x[:, n * PAIR : (n + 1) * PAIR] for n in range(count)]


def attention_fwd(pairs, q_src, kv_src, code_q, code_k, wbuf, q_buf, k_buf, v_buf, att_buf, logs, total, emit):
    count = len(pairs)
    logs[...] = jnp.zeros_like(logs)
    queries = mm(q_src[...], columns(wbuf, pairs, 0)).astype(BF)
    for n, q in enumerate(lane_pairs(queries, count)):
        q_buf[n] = q
    for n, b in enumerate(pairs):
        kv = mm(kv_src[...], wbuf[b, :, PAIR : 3 * PAIR]).astype(BF)
        k_buf[n] = kv[:, :PAIR]
        v_buf[n] = kv[:, PAIR:]
        att_buf[n] = attend_pair(
            q_buf[n], k_buf[n], v_buf[n], code_q[...], code_k[...], n, logs
        )
        emit(n)
    attended = jnp.concatenate([att_buf[n].astype(BF) for n in range(count)], axis=1)
    total[...] += nt(attended, columns(wbuf, pairs, 3))


def attention_bwd(me, pairs, low, low_t, q_src_t, kv_src_t, code_q, code_k, wbuf, q_buf, k_buf, v_buf, att_buf, logs, do_buf, d_q_src, d_kv_src, staged, store):
    count = len(pairs)
    for n, do in enumerate(lane_pairs(mm(low[...], columns(wbuf, pairs, 3)).astype(BF), count)):
        do_buf[n] = do
    attended = jnp.concatenate([att_buf[n].astype(BF) for n in range(count)], axis=1)
    for n, part in enumerate(lane_pairs(mm(low_t[...], attended).astype(BF), count)):
        staged[n, :, 3 * PAIR :] = part
    dqs = []
    for n, b in enumerate(pairs):
        dq, dk, dv = attend_pair_back(
            q_buf[n], k_buf[n], v_buf[n], att_buf[n], do_buf[n], code_q[...], code_k[...], logs, n
        )
        dqs.append(dq)
        dkv = jnp.concatenate([dk, dv], axis=1)
        staged[n, :, PAIR : 3 * PAIR] = mm(kv_src_t[...], dkv).astype(BF)
        part = nt(dkv, wbuf[b, :, PAIR : 3 * PAIR])
        d_kv_src[...] = part if n == 0 else d_kv_src[...] + part
    dq = jnp.concatenate(dqs, axis=1)
    for n, part in enumerate(lane_pairs(mm(q_src_t[...], dq).astype(BF), count)):
        staged[n, :, :PAIR] = part
    copies = []
    for n in range(count):
        copies += start(store(n))
    d_q_src[...] = nt(dq, columns(wbuf, pairs, 0))
    return copies


def self_fwd_kernel(pieces, n_weights, ints, x_own, x_other, code_in, *refs):
    weights, refs = refs[:n_weights], refs[n_weights:]
    q_ref, k_ref, v_ref, att_ref, logs_ref, mid_ref, normed_t_ref, norms = refs[:8]
    wbuf, own, other, code, normed, mid, q_buf, k_buf, v_buf, att_buf, logs, logs_t, turned, lines, wsems, sems, osems, lsems = refs[8:]
    me = ints[0]
    half = own.shape[0]
    loads = start(moves([(x_own, own), (x_other, other), (code_in, code)], sems))
    blk = wbuf.shape[1] // n_weights
    line_copies = start(
        moves([(w.at[:, pl.ds(blk, PAD), :], lines.at[n]) for n, w in enumerate(weights)], lsems)
    )
    weight_copies = load_weights(me, weights, pieces, wbuf, wsems)
    wait(line_copies)
    parts = jnp.sum(lines[...].astype(F32), axis=(0, 1))
    norms[...] = parts[:8] + parts[8:]
    wait(loads)
    states = own[...].astype(F32)
    mid[...] = states
    normed[:half] = norm_fwd(states, norms[0:1], norms[3:4])
    normed[half:] = norm_fwd(other[...].astype(F32), norms[0:1], norms[3:4])
    wait(weight_copies)
    outs = []

    def emit(n):
        sources = [(q_buf, q_ref), (k_buf, k_ref), (v_buf, v_ref), (att_buf, att_ref)]
        outs.extend(start(moves([(a.at[n], b.at[n]) for a, b in sources], osems.at[n])))

    pairs = list(range(wbuf.shape[0]))
    attention_fwd(
        pairs, normed.at[:half], normed, code.at[:half], code, wbuf, q_buf, k_buf, v_buf, att_buf, logs, mid, emit
    )
    outs.extend(start(moves([(mid, mid_ref)], osems.at[len(pairs)])))
    logs_t[...] = logs[...].T[: logs_t.shape[0]]
    turned[...] = normed[...].T
    outs.extend(start(moves([(logs_t, logs_ref), (turned, normed_t_ref)], osems.at[len(pairs) + 1])))
    wait(outs)


def self_bwd_kernel(pieces, n_weights, pairs, ints, d_mid_in, code_in, q_in, k_in, v_in, att_in, logs_in, normed_t_in, *refs):
    weights, refs = refs[:n_weights], refs[n_weights:]
    d_own_ref, d_other_ref, keep, send = refs[:4]
    wbuf, d_mid, code, q_buf, k_buf, v_buf, att_buf, logs, normed_t, low, low_t, do_buf, d_q, d_kv, d_other, staged, wsems, sems, gsems = refs[4:]
    me = ints[0]
    half = d_mid.shape[0]
    loads = start(
        moves(
            [(d_mid_in, d_mid), (code_in, code), (q_in, q_buf), (k_in, k_buf), (v_in, v_buf), (att_in, att_buf), (logs_in, logs), (normed_t_in, normed_t)],
            sems,
        )
    )
    weight_copies = load_weights(me, weights, pieces, wbuf, wsems)
    wait(loads[:1])
    low[...] = d_mid[...].astype(BF)
    low_t[...] = low[...].T
    wait(loads[1:])
    wait(weight_copies)

    def store(n):
        return store_grad(me, staged, n, keep, send, gsems)

    copies = attention_bwd(
        me, pairs, low, low_t, normed_t.at[:, :half], normed_t, code.at[:half], code, wbuf, q_buf, k_buf, v_buf, att_buf, logs, do_buf, d_q, d_kv, staged, store
    )
    d_other[...] = d_kv[half:].astype(BF)
    outs = start(moves([(d_other, d_other_ref)], sems.at[pl.ds(0, 1)]))
    d_q[...] += d_kv[:half]
    outs += start(moves([(d_q, d_own_ref)], sems.at[pl.ds(1, 1)]))
    wait(outs + copies)


def feed_fwd_kernel(pieces, n_weights, ints, mid_in, norms, *refs):
    weights, refs = refs[:n_weights], refs[n_weights:]
    out_ref, memory_ref, hidden_ref, slope_ref = refs[:4]
    both, mid, out, memory, hidden_buf, slope_buf, normed, wsems, sems, osems = refs[4:]
    me = ints[0]

    @pl.when(ints[1] == 1)
    def _():
        loads = start(moves([(mid_in, mid)], sems))
        weight_copies = load_weights(me, weights, pieces, both, wsems)
        wait(loads)
        normed[...] = norm_fwd(mid[...], norms[1:2], norms[4:5])
        wait(weight_copies)
        outs = []
        ways, _, unit = both.shape
        unit = unit // 2
        for b in range(ways):
            pre = mm(normed[...], both[b, :, :unit])
            cdf, density = gelu_parts(pre)
            hidden_buf[b] = (pre * cdf).astype(BF)
            slope_buf[b] = (cdf + pre * density).astype(BF)
            base = mid[...] if b == 0 else out[...]
            out[...] = base + nt(hidden_buf[b], both[b, :, unit:])
            outs += start(
                moves([(hidden_buf.at[b], hidden_ref.at[b]), (slope_buf.at[b], slope_ref.at[b])], osems.at[b])
            )
        outs += start(moves([(out, out_ref)], osems.at[ways]))
        memory[...] = norm_fwd(out[...], norms[2:3], norms[5:6])
        outs += start(moves([(memory, memory_ref)], sems))
        wait(outs)


def decoder_kernel(pieces, n_weights, ints, mid_in, mem_own, mem_other, code_q_in, code_k_in, cots_in, norms, *refs):
    weights, refs = refs[:n_weights], refs[n_weights:]
    decoded_ref, d_mid_ref, mem_keep, mem_send, small, keep_u, send_u, keep_d, send_d, keep3, send3 = refs[:11]
    (
        wbuf, both, mid, mem, code_q, code_k, cots, cross_in, q_buf, k_buf, v_buf, att_buf, logs, logs_t,
        joined, out, decoded, normed, normed_t, low, low_t, mem_t, do_buf, d_norm, d_q, d_kv, d_mem,
        staged_u, staged_d, staged3, wsems, sems, osems, gsems_u, gsems_d, gsems3,
    ) = refs[11:]
    me = ints[0]
    half = mid.shape[0]

    @pl.when(ints[1] == 0)
    def _():
        loads = start(
            moves(
                [(mid_in, mid), (mem_own, mem.at[:half]), (mem_other, mem.at[half:]), (code_q_in, code_q), (code_k_in, code_k), (cots_in, cots)],
                sems,
            )
        )
        crosses = load_weights(me, weights, pieces[0], wbuf, wsems.at[0])
        feeds = load_weights(me, weights, pieces[1], both, wsems.at[1])
        pairs = list(range(wbuf.shape[0]))
        wait(loads[:1])
        joined[...] = mid[...]
        cross_in[...] = norm_fwd(mid[...], norms[2:3], norms[5:6])
        wait(loads[1:])
        wait(crosses)
        attention_fwd(
            pairs, cross_in, mem, code_q, code_k, wbuf, q_buf, k_buf, v_buf, att_buf, logs, joined, lambda n: None
        )
        logs_t[...] = logs[...].T[: logs_t.shape[0]]
        wait(feeds)
        normed[...] = norm_fwd(joined[...], norms[1:2], norms[4:5])
        normed_t[...] = normed[...].T
        low_t[...] = cots[...].T
        unit = both.shape[2] // 2
        copies = []
        for b in pairs:
            pre = mm(normed[...], both[b, :, :unit])
            cdf, density = gelu_parts(pre)
            hidden = (pre * cdf).astype(BF)
            base = joined[...] if b == 0 else out[...]
            out[...] = base + nt(hidden, both[b, :, unit:])
            d_pre = (mm(cots[...], both[b, :, unit:]) * (cdf + pre * density)).astype(BF)
            staged_u[b] = mm(normed_t[...], d_pre).astype(BF)
            copies += start(store_grad(me, staged_u, b, keep_u, send_u, gsems_u))
            staged_d[b] = mm(low_t[...], hidden).astype(BF)
            copies += start(store_grad(me, staged_d, b, keep_d, send_d, gsems_d))
            part = nt(d_pre, both[b, :, :unit])
            d_norm[...] = part if b == 0 else d_norm[...] + part
        decoded[...] = out[...].astype(BF)
        outs = start(moves([(decoded, decoded_ref)], osems))
        dx, d_gain1, d_bias1 = norm_bwd(joined[...], norms[1:2], d_norm[...])
        joined[...] = cots[...].astype(F32) + dx
        def store3(n):
            return store_grad(me, staged3, n, keep3, send3, gsems3)

        low[...] = joined[...].astype(BF)
        low_t[...] = low[...].T
        mem_t[...] = mem[...].T
        normed_t[...] = cross_in[...].T
        copies += attention_bwd(
            me, pairs, low, low_t, normed_t, mem_t, code_q, code_k, wbuf, q_buf, k_buf, v_buf, att_buf, logs_t, do_buf, d_q, d_kv, staged3, store3
        )
        d_mem[...] = d_kv[...].astype(BF)
        outs += start(
            moves([(d_mem.at[half:], mem_send), (d_mem.at[:half], mem_keep)], osems.at[pl.ds(1, 2)])
        )
        dx, d_gain2, d_bias2 = norm_bwd(mid[...], norms[2:3], d_q[...])
        out[...] = joined[...] + dx
        outs += start(moves([(out, d_mid_ref)], osems.at[pl.ds(3, 1)]))
        small[0:1] = d_gain1
        small[1:2] = d_gain2
        small[2:3] = d_bias1
        small[3:4] = d_bias2
        wait(outs + copies)


def feed_bwd_kernel(pieces, n_weights, ints, encoded_in, mid_in, d_mem_in, cots_in, norms, hidden_in, slope_in, small_in, d_mid_in, keep_u_in, send_u_in, keep_d_in, send_d_in, *refs):
    weights, refs = refs[:n_weights], refs[n_weights:]
    small, d_mid_ref, keep_u, send_u, keep_d, send_d = refs[:6]
    (
        both, encoded, mid, d_mem, cots, hidden, slope, normed_t, low, low_t, d_out, d_norm, staged_u, staged_d, wsems, sems, gsems_u, gsems_d,
    ) = refs[6:]
    me = ints[0]

    @pl.when(ints[1] == 0)
    def _():
        small[...] = small_in[...]

    @pl.when(ints[1] == 1)
    def _():
        loads = start(
            moves(
                [(encoded_in, encoded), (d_mem_in, d_mem), (cots_in, cots), (mid_in, mid), (hidden_in, hidden), (slope_in, slope)],
                sems,
            )
        )
        weight_copies = load_weights(me, weights, pieces, both, wsems)
        wait(loads[:3])
        grad = d_mem[...].astype(F32) + cots[...].astype(F32)
        dx, d_gain, d_bias = norm_bwd(encoded[...], norms[2:3], grad)
        small[1:2] = d_gain
        small[3:4] = d_bias
        d_out[...] = dx
        low[...] = dx.astype(BF)
        low_t[...] = low[...].T
        wait(loads[3:])
        normed_t[...] = norm_fwd(mid[...], norms[1:2], norms[4:5]).T
        wait(weight_copies)
        ways, _, unit = both.shape
        unit = unit // 2
        copies = []
        for b in range(ways):
            d_pre = (mm(low[...], both[b, :, unit:]) * slope[b].astype(F32)).astype(BF)
            staged_u[b] = mm(normed_t[...], d_pre).astype(BF)
            copies += start(store_grad(me, staged_u, b, keep_u, send_u, gsems_u))
            staged_d[b] = mm(low_t[...], hidden[b]).astype(BF)
            copies += start(store_grad(me, staged_d, b, keep_d, send_d, gsems_d))
            part = nt(d_pre, both[b, :, :unit])
            d_norm[...] = part if b == 0 else d_norm[...] + part
        dx, d_gain1, d_bias1 = norm_bwd(mid[...], norms[1:2], d_norm[...])
        d_out[...] += dx
        outs = start(moves([(d_out, d_mid_ref)], sems))
        small[0:1] = d_gain1
        small[2:3] = d_bias1
        wait(outs + copies)


def last_kernel(d_own, d_got, x_own, d_mid, norms, dx_ref, small):
    grad = d_own[...] + d_got[...].astype(F32)
    dx, d_gain, d_bias = norm_bwd(x_own[...].astype(F32), norms[0:1], grad)
    dx_ref[...] = (d_mid[...] + dx).astype(BF)
    small[0:1] = d_gain
    small[1:2] = d_bias


VM = pl.BlockSpec(memory_space=pltpu.VMEM)
SM = pl.BlockSpec(memory_space=pltpu.SMEM)
AN = pl.BlockSpec(memory_space=pl.ANY)


def call(kernel, name, ins, outs, scratch, flops, **more):
    return pl.pallas_call(
        kernel,
        name=name,
        in_specs=[spec for _, spec in ins],
        out_shape=[jax.ShapeDtypeStruct(shape, dtype) for shape, dtype, _ in outs],
        out_specs=[spec for _, _, spec in outs],
        scratch_shapes=scratch,
        compiler_params=pltpu.CompilerParams(vmem_limit_bytes=VMEM_MIB[name] << 20),
        cost_estimate=pl.CostEstimate(flops=flops, bytes_accessed=8 << 20, transcendentals=0),
        **more,
    )(*[array for array, _ in ins])


def on_device(layer_in, segment_ids, out_grads, w_qkv, w_out, w_up, w_down, norm_gain, norm_bias, w_qc, w_kvc, w_oc):
    encoder = lax.axis_index("section") == 0
    me = lax.axis_index("dp")
    core = me & 1
    place = lax.axis_index("mp")
    ways = lax.axis_size("mp")
    count = lax.axis_size("dp")
    rows = layer_in.shape[1]
    width = layer_in.shape[3]
    blk = w_qkv.shape[1]
    half = 2 * layer_in.shape[2]
    length = 2 * half
    assert rows == 2 and ways == 4 and length == segment_ids.shape[2]
    ints = jnp.stack([me, encoder.astype(jnp.int32), place])

    each = norm_gain.shape[2]
    spread = jnp.tile(jnp.concatenate([norm_gain[0], norm_bias[0]]), (1, width // each))
    spread = jnp.where(jnp.arange(width) // each == me * ways + place, spread, 0.0)
    high = spread.astype(BF)
    low = (spread - high.astype(F32)).astype(BF)
    gap = jnp.zeros((2, width), BF)
    shard1 = jnp.concatenate([w_qkv[0].reshape(blk, -1), w_out[0].T], axis=1)
    shard1 = jnp.concatenate([shard1, high, gap, low, gap])
    bits, core_bit = dp_bits(), [1]
    unit = w_up.shape[2]
    shard2 = jnp.concatenate([w_up[0], w_down[0].T], axis=1)
    mine3 = jnp.stack([w_qc, w_kvc[:, 0], w_kvc[:, 1], w_oc.T], axis=1)
    theirs3 = oneway(mine3, "section", 0, 1)
    pair1 = jnp.stack([shard1, swap(shard1, "mp", 2)])
    own2, held2 = shard2[None], [0]
    for bit in bits:
        own2 = jnp.concatenate([own2, swap(own2, "dp", bit)])
        held2 = held2 + [a ^ bit for a in held2]
    up_pair = jnp.stack([w_up[0], swap(w_up[0], "mp", 2)])
    x_own = lax.all_to_all(rows_in(layer_in[0]), "mp", 0, 0, tiled=True).reshape(-1, width)
    cots = lax.all_to_all(after(rows_in(out_grads[0]), x_own), "mp", 0, 0, tiled=True).reshape(-1, width)
    pair1 = after(pair1, x_own)
    all1 = jnp.concatenate([pair1, swap(pair1, "mp", 1)])
    own3 = after(jnp.concatenate([theirs3, mine3], axis=2).reshape(1, blk, -1), pair1)
    for bit in bits:
        own3 = jnp.concatenate([own3, decoder_swap(own3, "dp", bit)])
    w1 = doubled([(all1, 0)], bits)
    up_pair, own2 = after((up_pair, own2), all1)
    up_rest = jnp.concatenate([up_pair[1:], swap(up_pair, "mp", 1)])
    down_own = own2[:, :, unit:]
    down_pair = jnp.stack([down_own, swap(down_own, "mp", 2)])
    up_rest, down_pair = after((up_rest, down_pair), *[w for w, _ in w1])
    w1 = doubled(w1, core_bit)
    x_other = swap(x_own, "dp", 1)

    other_segs = swap(segment_ids, "dp", 1)
    segs = jnp.where(core == (place >> 1), segment_ids, other_segs)
    segs = jnp.where((place & 1) == 0, segs[:, 0], segs[:, 1])
    segs = segs.reshape(2, ways, 2, -1).transpose(0, 2, 1, 3)
    segs = jnp.where(core == 0, segs, segs[:, ::-1]).reshape(2, length)
    lane = jnp.arange(PAIR) & (HD - 1)
    codes = (segs[:, :, None] == lane[None, None, :]).astype(BF)
    code_own = jnp.where(encoder, codes[0], codes[1])

    middle = ways // 2
    dma = pltpu.SemaphoreType.DMA

    def buf(*shape):
        return pltpu.VMEM(shape, BF)

    def fbuf(*shape):
        return pltpu.VMEM(shape, F32)

    def hbm(*arrays):
        return [(a, AN) for a in arrays]

    wbuf = buf(ways, width, 4 * PAIR)
    rows1, every = (pl.ds(0, ways), pl.ds(0, blk)), pl.ds(0, 4 * PAIR)
    pieces1 = [(n, rows1, 0, ways, a, every) for n, (_, a) in enumerate(w1)]

    weights1 = [w for w, _ in w1]

    def kept_shapes(count):
        return [
            ((count, half, PAIR), BF, AN),
            ((count, length, PAIR), BF, AN),
            ((count, length, PAIR), BF, AN),
            ((count, half, PAIR), F32, AN),
            ((8, half), F32, AN),
        ]

    def kept_bufs(count):
        return [buf(count, half, PAIR), buf(count, length, PAIR), buf(count, length, PAIR), fbuf(count, half, PAIR)]

    def grads(pairs, columns):
        return [((count // 2, pairs, blk, columns), BF, AN)] * 2

    state, state_low = ((half, width), F32, AN), ((half, width), BF, AN)

    x_other, cots = together(x_other, cots)
    up_rests = doubled([(up_rest, 0)], bits)
    down_rest = jnp.concatenate([down_pair[1:], swap(down_pair, "mp", 1)])
    pair3 = jnp.stack([own3, decoder_swap(own3, "mp", 2)])
    *kept, mid, normed_t, norms = call(
        functools.partial(self_fwd_kernel, pieces1, len(weights1)),
        "self_fwd",
        [(ints, SM)] + hbm(x_own, x_other, code_own, *weights1),
        kept_shapes(ways) + [state, ((width, length), BF, AN), ((8, width), F32, VM)],
        [wbuf, buf(half, width), buf(half, width), buf(length, PAIR), buf(length, width), fbuf(half, width)]
        + kept_bufs(ways)
        + [fbuf(half, PAIR), fbuf(8, half), buf(width, length), buf(count, ways, PAD, width)]
        + [dma((count,)), dma((3,)), dma((ways + 2, 4)), dma((count,))],
        5 << 30,
    )
    mid, pair3, own2, down_rest, *arrays = together(mid, pair3, own2, down_rest, *[w for w, _ in up_rests])
    up_rests = [(w, a) for w, (_, a) in zip(arrays, up_rests)]
    weights2 = [w for w, _ in doubled([(own2, 0), (down_rest, 0)] + up_rests, core_bit)]
    pieces2 = []
    others, low, high = pl.ds(0, ways - 1), pl.ds(0, unit), pl.ds(unit, unit)
    for n in range(2):
        base = n * (2 + len(up_rests))
        for at, a in enumerate(held2):
            pieces2.append((base, (pl.ds(at, 1),), 0, 1, a ^ n, pl.ds(0, 2 * unit)))
            pieces2.append((base + 1, (others, at), 1, ways - 1, a ^ n, high))
        for at, (_, a) in enumerate(up_rests):
            pieces2.append((base + 2 + at, (others,), 1, ways - 1, a ^ n, low))
    all3 = jnp.concatenate([pair3, decoder_swap(pair3, "mp", 1)])
    wbuf2 = buf(ways, width, 2 * unit)
    encoded, memory, hidden, slope = call(
        functools.partial(feed_fwd_kernel, pieces2, len(weights2)),
        "feed_fwd",
        [(ints, SM)] + hbm(mid) + [(norms, VM)] + hbm(*weights2),
        [state, state_low] + [((ways, half, unit), BF, AN)] * 2,
        [wbuf2, fbuf(half, width), fbuf(half, width), buf(half, width), buf(ways, half, unit), buf(ways, half, unit)]
        + [buf(half, width), dma((3 * count,)), dma((1,)), dma((ways + 1, 2))],
        5 << 30,
    )
    mem_own = oneway(memory, "section", 0, 1)
    mem_other = swap(mem_own, "dp", 1)
    w3 = doubled([(after(all3, mem_own), 0)], core_bit, decoder_swap)
    weights3 = [w for w, _ in w3]
    pieces3 = [(n, (pl.ds(0, ways), at), 0, ways, a ^ n, every) for n in range(2) for at, a in enumerate(held2)]
    dec_pieces = (pieces3, [(len(weights3) + piece[0],) + piece[1:] for piece in pieces2])
    decoded, d_mid, mem_keep, mem_send, small, keep_u, send_u, keep_d, send_d, keep3, send3 = call(
        functools.partial(decoder_kernel, dec_pieces, len(weights3) + len(weights2)),
        "decoder",
        [(ints, SM)] + hbm(mid, mem_own, mem_other, codes[1, :half], codes[0], cots) + [(norms, VM)] + hbm(*weights3, *weights2),
        [state_low, state, state_low, state_low, ((4, width), F32, VM)] + grads(ways, unit) * 2
        + grads(ways, 4 * PAIR),
        [wbuf, wbuf2, fbuf(half, width), buf(length, width), buf(half, PAIR), buf(length, PAIR), buf(half, width)]
        + [buf(half, width)]
        + kept_bufs(ways)
        + [fbuf(half, PAIR), fbuf(8, half), fbuf(half, width), fbuf(half, width), buf(half, width), buf(half, width)]
        + [buf(width, half), buf(half, width), buf(width, half), buf(width, length), buf(ways, half, PAIR)]
        + [fbuf(half, width), fbuf(half, width), fbuf(length, width), buf(length, width)]
        + [buf(ways, width, unit), buf(ways, width, unit), buf(ways, width, 4 * PAIR), dma((2, 3 * count)), dma((6,))]
        + [dma((4,)), dma((ways, count)), dma((ways, count)), dma((ways, count))],
        40 << 30,
    )
    mem_sum = add(mem_keep, swap(mem_send, "dp", 1))
    d_mem = oneway(mem_sum, "section", 1, 0)
    got3 = decoder_swap(after(send3, mem_sum), "dp", 1)
    section_out = rows_out(jnp.where(encoder, memory, after(decoded, mem_sum)))
    d_mem, got3, section_out = together(d_mem, got3, section_out)
    bit = bits[-1]
    keep3, send3 = fold(keep3, got3)
    small, d_mid, keep_u, send_u, keep_d, send_d = call(
        functools.partial(feed_bwd_kernel, pieces2, len(weights2)),
        "feed_bwd",
        [(ints, SM)] + hbm(encoded, mid, d_mem, cots) + [(norms, VM)] + hbm(hidden, slope) + [(small, VM)]
        + hbm(d_mid, keep_u, send_u, keep_d, send_d, *weights2),
        [((4, width), F32, VM), state] + grads(ways, unit) * 2,
        [wbuf2, fbuf(half, width), fbuf(half, width), buf(half, width), buf(half, width)]
        + [buf(ways, half, unit), buf(ways, half, unit), buf(width, half), buf(half, width), buf(width, half)]
        + [fbuf(half, width), fbuf(half, width), buf(ways, width, unit), buf(ways, width, unit), dma((3 * count,)), dma((6,))]
        + [dma((ways, count)), dma((ways, count))],
        8 << 30,
        input_output_aliases={9: 1, 10: 2, 11: 3, 12: 4, 13: 5},
    )
    got_u, got_d = swap(send_u, "dp", 1), swap(send_d, "dp", 1)
    got3 = decoder_swap(after(send3, d_mem), "dp", bit)

    def self_bwd(pairs, kept, d_mid):
        return call(
            functools.partial(self_bwd_kernel, pieces1, len(weights1), pairs),
            "self_bwd",
            [(ints, SM)] + hbm(d_mid, code_own, *kept, normed_t, *weights1),
            [state, state_low] + grads(len(pairs), 4 * PAIR),
            [wbuf, fbuf(half, width), buf(length, PAIR)]
            + kept_bufs(len(pairs))
            + [fbuf(8, half), buf(width, length), buf(half, width), buf(width, half), buf(len(pairs), half, PAIR)]
            + [fbuf(half, width), fbuf(length, width), buf(half, width), buf(len(pairs), width, 4 * PAIR)]
            + [dma((count,)), dma((8,)), dma((len(pairs), count))],
            10 << 30,
        )

    got_u, got_d, got3 = together(got_u, got_d, got3)
    keep_u, send_u = fold(keep_u, got_u)
    keep_d, send_d = fold(keep_d, got_d, 1)
    got_u, got_d = swap(send_u, "dp", bit), swap(send_d, "mp", 1)
    keep3, got3 = fold_dp_rest(keep3, got3, decoder_swap)
    keep3, send3 = fold(keep3, got3, 1)
    got3 = decoder_swap(send3, "mp", 1)
    d_own, d_other, keep1, send1 = self_bwd(list(range(ways)), kept, after(d_mid, send_u, send_d, send3))
    d_other, send1, got_u, got_d, got3 = together(d_other, send1, got_u, got_d, got3)
    got1 = swap(send1, "dp", 1)
    d_got = swap(d_other, "dp", 1)
    keep3, got3 = fold_mp(keep3, got3, 2, decoder_swap)
    keep1, send1 = fold(keep1, got1)
    keep_u, got_u, keep_d, got_d = after((keep_u, got_u, keep_d, got_d), send1)
    keep_d, send_d = fold(keep_d, got_d)
    got = swap(jnp.concatenate([send1, send_d], axis=1), "dp", bit)
    keep_u, got_u = fold_dp_rest(keep_u, got_u)
    keep_u, send_u = fold(keep_u, got_u, 1)
    got_u = swap(send_u, "mp", 1)
    d_own = after(d_own, send1, send_u, send_d)
    d_x, small0 = call(
        last_kernel,
        "last",
        [(a, VM) for a in (d_own, d_got, x_own, d_mid, norms)],
        [((half, width), BF, VM), ((2, width), F32, VM)],
        [],
        1 << 30,
    )
    in_grads = rows_out(d_x)
    d_x, small0, got, got_u, got3 = together(d_x, small0, got, got_u, got3)
    small = jnp.concatenate([small0[0:1], small[:2], small0[1:2], small[2:]])
    order = relative_order()
    small = small.reshape(6, count, ways, -1).transpose(1, 2, 0, 3)
    small = xor_order(small, me)
    small = xor_order(small.swapaxes(0, 1), place)
    small = jnp.stack([small[n] for n in (0, 2, 1, 3)], axis=1)
    small = jnp.stack([small[a] for a in order])
    for turn in [1] + bits[::-1]:
        small, send = halves(small)
        small = small + swap(send, "dp", turn)
    small = small.reshape(1, ways, 1, -1)
    small = jnp.pad(small, ((0, 0), (0, 0), (0, PAD - 1), (0, 4 * PAIR - small.shape[3])))
    keep1, got1 = fold_dp_rest(keep1, got[:, :ways])
    keep_d, got_d = fold_dp_rest(keep_d, got[:, ways:])
    keep1, send1 = fold(keep1, got1, 1)
    small_keep, small_send = halves(small.astype(BF), 1)
    send1 = jnp.concatenate([send1, small_send], axis=2)
    got1 = swap(send1, "mp", 1)
    keep1 = jnp.concatenate([keep1, small_keep], axis=2)
    r3 = total(keep3, got3).reshape(blk, 4, 2, -1)
    back = oneway(after(r3[:, :, 0].astype(BF), send1), "section", 1, 0)
    keep_u, send_u = fold(keep_u, got_u, 1)
    keep_d, send_d = fold(keep_d, got_d, 1)
    got = swap(jnp.concatenate([send_u, send_d], axis=1), "mp", 2)
    keep1, send1 = fold(keep1, got1, 1)
    got1 = swap(send1, "mp", 2)
    got, back, in_grads = after((got, back, in_grads), send1)
    got_u, got_d = halves(got, 1)
    r_up, r_down, r1 = total(keep_u, got_u), total(keep_d, got_d), total(keep1, got1)
    small, r1 = r1[blk, : 6 * each].reshape(6, each), r1[:blk]
    section_out, in_grads = rows_placed(section_out), rows_placed(in_grads)
    grad_qkv = r1[:, : 3 * PAIR].reshape(1, blk, 3, -1)
    grad_out = r1[:, 3 * PAIR :].T[None]
    grad_up = r_up[None]
    grad_down = r_down.T[None]
    r3 = jnp.where(encoder, back.astype(F32), r3[:, :, 1])
    grad_qc, grad_kvc, grad_oc = r3[:, 0], r3[:, 1:3], r3[:, 3].T
    grad_gain = small[None, :3]
    grad_bias = jnp.stack([small[3], small[5]])[None]
    grad_ffn = small[4][None]
    return (
        section_out,
        in_grads,
        grad_qkv,
        grad_out,
        grad_up,
        grad_down,
        grad_gain,
        grad_bias,
        grad_ffn,
        grad_qc,
        grad_kvc,
        grad_oc,
    )


def solution(mesh):
    placed = (
        P("section", "dp", "mp", None),
        P(None, "dp", None),
        P("section", "dp", "mp", None),
        P("section", "dp", None, "mp"),
        P("section", "mp", "dp"),
        P("section", "dp", "mp"),
        P("section", "mp", "dp"),
        P("section", None, ("dp", "mp")),
        P("section", None, ("dp", "mp")),
        P("dp", ("section", "mp")),
        P("dp", None, ("section", "mp")),
        P(("section", "mp"), "dp"),
    )
    return jax.shard_map(
        on_device,
        mesh=mesh,
        in_specs=placed,
        out_specs=(
            P("section", "dp", "mp", None),
            P("section", "dp", "mp", None),
            P("section", "dp", None, "mp"),
            P("section", "mp", "dp"),
            P("section", "dp", "mp"),
            P("section", "mp", "dp"),
            P("section", None, ("dp", "mp")),
            P("section", None, ("dp", "mp")),
            P("section", ("dp", "mp")),
            P("dp", ("section", "mp")),
            P("dp", None, ("section", "mp")),
            P(("section", "mp"), "dp"),
        ),
        check_vma=False,
    )
```

profile of v0, /device:TPU:3, one launch (start us, length us, event | category | flops | bytes accessed | tf_op | source)
XLA Modules:
  0.0 302.5 jit_solution(14534546672623164103)
XLA Ops:
  1.7 1.0 copy.53
  3.8 2.4 collective-permute-start.4
  6.2 1.1 select_bitcast_fusion.5
  7.2 1.0 collective-permute-start
  8.5 1.3 collective-permute-start.13
  11.2 1.3 collective-permute-start.9
  13.9 4.6 %all-to-all-start = ((bf16[4,128,512]{2,1,0:T(8,128)(2,1)}), bf16[4,128,512]{2,1,0:T(8,128)(2,1)S(1)}, u32[]{:S(2)}, u32[]{:S(2)}) async-start(bf16[4,128,512]{2,1,0:T(8,128)(2,1)} %maximum_select_fusion), calls=%async_computation | async-start | bytes 1048576 | tf_op jit(solution)/shard_map/all_to_all | solution.py:632
  18.8 13.8 %all-to-all-done = bf16[4,128,512]{2,1,0:T(8,128)(2,1)S(1)} async-done(((bf16[4,128,512]{2,1,0:T(8,128)(2,1)}), bf16[4,128,512]{2,1,0:T(8,128)(2,1)S(1)}, u32[]{:S(2)}, u32[]{:S(2)}) %all-to-all-start) | async-done | bytes 524320 | tf_op jit(solution)/shard_map/all_to_all | solution.py:632
  32.7 1.0 maximum_select_fusion.1
  33.8 2.1 collective-permute-start.10
  36.6 3.2 %collective-permute-done.5 = bf16[2,144,512]{2,1,0:T(8,128)(2,1)S(1)} collective-permute-done((bf16[2,144,512]{2,1,0:T(8,128)(2,1)S(1)}, bf16[2,144,512]{2,1,0:T(8,128)(2,1)S(1)}, u32[]{:S(2)}, u32[]{:S(2)}) %collective-permute-start.5) | collective-permute-done | bytes 294944 | tf_op jit(solution)/shard_map/ppermute | solution.py:24
  41.2 1.6 collective-permute-start.15
  42.8 3.0 collective-permute-start.1
  45.8 4.1 %all-to-all-start.1 = ((bf16[4,128,512]{2,1,0:T(8,128)(2,1)}), bf16[4,128,512]{2,1,0:T(8,128)(2,1)}, u32[]{:S(2)}, u32[]{:S(2)}) async-start(bf16[4,128,512]{2,1,0:T(8,128)(2,1)} %maximum_select_fusion.1), calls=%async_computation.1 | async-start | bytes 1048576 | tf_op jit(solution)/shard_map/all_to_all | solution.py:633
  50.0 4.4 %collective-permute-start.11 = (bf16[2,128,512]{2,1,0:T(8,128)(2,1)S(1)}, bf16[2,128,512]{2,1,0:T(8,128)(2,1)S(1)}, u32[]{:S(2)}, u32[]{:S(2)}) collective-permute-start(bf16[2,128,512]{2,1,0:T(8,128)(2,1)S(1)} %constant_dynamic-update-slice_fusion.2), channel_id=1, source_target_pairs={{16,18},{17,19},{18,16},{19,17},{20,22},{21,23},{22,20},{23,21},{2... | collective-permute-start | bytes 786440 | tf_op jit(solution)/shard_map/ppermute | solution.py:54
  54.4 1.1 collective-permute-start.7
  56.4 4.0 %collective-permute-start.8 = (bf16[4,144,512]{2,1,0:T(8,128)(2,1)}, bf16[4,144,512]{2,1,0:T(8,128)(2,1)}, u32[]{:S(2)}, u32[]{:S(2)}) collective-permute-start(bf16[4,144,512]{2,1,0:T(8,128)(2,1)} %collective-permute-done.6.refs_1_), channel_id=1, source_target_pairs={{0,4},{4,0},{8,12},{12,8},{1,5},{5,1},{9,13},{13,9},{2,6},{6,2},{1... | collective-permute-start | bytes 1769480 | tf_op jit(solution)/shard_map/ppermute | solution.py:24
  61.5 16.3 %collective-permute-done.11 = bf16[2,128,512]{2,1,0:T(8,128)(2,1)S(1)} collective-permute-done((bf16[2,128,512]{2,1,0:T(8,128)(2,1)S(1)}, bf16[2,128,512]{2,1,0:T(8,128)(2,1)S(1)}, u32[]{:S(2)}, u32[]{:S(2)}) %collective-permute-start.11) | collective-permute-done | bytes 262176 | tf_op jit(solution)/shard_map/ppermute | solution.py:54
  79.8 13.3 %self_fwd.1 = (bf16[4,512,128]{2,1,0:T(8,128)(2,1)}, bf16[4,1024,128]{2,1,0:T(8,128)(2,1)}, bf16[4,1024,128]{2,1,0:T(8,128)(2,1)}, f32[4,512,128]{2,1,0:T(8,128)...) custom-call(s32[3]{0:T(128)} %pad_add_fusion.ints, ...), custom_call_target="tpu_custom_call" | custom-call | flops 5368709120 | bytes 8388608 | tf_op jit(solution)/shard_map/self_fwd/pallas_call | solution.py:585
  93.1 2.0 collective-permute-start.19
  95.7 1.9 collective-permute-start.24
  99.7 1.2 copy-done.12
  102.0 1.0 copy-done.13
  103.0 1.4 collective-permute-start.22
  104.4 6.5 %collective-permute-done.24 = bf16[2,2,128,512]{3,2,1,0:T(8,128)(2,1)S(1)} collective-permute-done((bf16[2,2,128,512]{3,2,1,0:T(8,128)(2,1)}, bf16[2,2,128,512]{3,2,1,0:T(8,128)(2,1)S(1)}, u32[]{:S(2)}, u32[]{:S(2)}) %collective-permute-start.24) | collective-permute-done | bytes 524320 | tf_op jit(solution)/shard_map/ppermute | solution.py:54
  110.9 1.1 pad_maximum_fusion.refs_0_
  112.0 7.4 %collective-permute-done.22.mem_own = bf16[512,512]{1,0:T(8,128)(2,1)S(1)} collective-permute-done((bf16[512,512]{1,0:T(8,128)(2,1)S(1)}, bf16[512,512]{1,0:T(8,128)(2,1)S(1)}, u32[]{:S(2)}, u32[]{:S(2)}) %collective-permute-start.22) | collective-permute-done | bytes 524320 | tf_op jit(solution)/shard_map/ppermute | solution.py:32
  119.5 2.8 collective-permute-start.25
  123.7 1.5 collective-permute-done.23.mem_other
  126.1 1.0 copy-done.38
  127.0 39.7 %decoder.1 = (bf16[512,512]{1,0:T(8,128)(2,1)}, f32[512,512]{1,0:T(8,128)}, bf16[512,512]{1,0:T(8,128)(2,1)}, bf16[512,512]{1,0:T(8,128)(2,1)}, f32[4,512]{1,0:T...) custom-call(s32[3]{0:T(128)} %pad_add_fusion.ints, ...), custom_call_target="tpu_custom_call" | custom-call | flops 42949672960 | bytes 8388608 | tf_op jit(solution)/shard_map/decoder/pallas_call | solution.py:585
  167.2 1.8 collective-permute-done.26
  168.9 1.2 add_convert_fusion.8
  170.1 2.3 collective-permute-start.28
  172.4 1.9 broadcast_select_fusion
  174.3 3.5 %all-to-all-start.2 = ((bf16[4,128,512]{2,1,0:T(8,128)(2,1)}), bf16[4,128,512]{2,1,0:T(8,128)(2,1)S(1)}, u32[]{:S(2)}, u32[]{:S(2)}) async-start(bf16[4,128,512]{2,1,0:T(8,128)(2,1)} %bitcast.35), calls=%async_computation.2 | async-start | bytes 1048576 | tf_op jit(solution)/shard_map/all_to_all | solution.py:112
  177.8 1.3 collective-permute-start.27
  179.1 11.4 %collective-permute-done.27.d_mem_in = bf16[512,512]{1,0:T(8,128)(2,1)S(1)} collective-permute-done((bf16[512,512]{1,0:T(8,128)(2,1)S(1)}, bf16[512,512]{1,0:T(8,128)(2,1)S(1)}, u32[]{:S(2)}, u32[]{:S(2)}) %collective-permute-start.27) | collective-permute-done | bytes 524320 | tf_op jit(solution)/shard_map/ppermute | solution.py:32
  190.5 1.8 all-to-all-done.2
  192.2 1.9 feed_bwd.1
  194.1 1.0 collective-permute-start.30
  195.5 3.3 %collective-permute-start.32 = (bf16[1,4,128,512]{3,2,1,0:T(8,128)(2,1)S(1)}, bf16[1,4,128,512]{3,2,1,0:T(8,128)(2,1)S(1)}, u32[]{:S(2)}, u32[]{:S(2)}) collective-permute-start(bf16[1,4,128,512]{3,2,1,0:T(8,128)(2,1)S(1)} %get-tuple-element.132), channel_id=1, source_target_pairs={{16,24},{20,28},{24,16},{28,20},{17,25},{21,29},{25,17},{29,21},{1... | collective-permute-start | bytes 1572872 | tf_op jit(solution)/shard_map/ppermute | solution.py:54
  198.8 11.8 %collective-permute-done.32 = bf16[1,4,128,512]{3,2,1,0:T(8,128)(2,1)S(1)} collective-permute-done((bf16[1,4,128,512]{3,2,1,0:T(8,128)(2,1)S(1)}, bf16[1,4,128,512]{3,2,1,0:T(8,128)(2,1)S(1)}, u32[]{:S(2)}, u32[]{:S(2)}) %collective-permute-start.32) | collective-permute-done | bytes 524320 | tf_op jit(solution)/shard_map/ppermute | solution.py:54
  211.5 2.3 collective-permute-start.35
  214.1 1.3 collective-permute-start.34
  215.7 1.3 collective-permute-start.33
  217.0 21.2 %self_bwd.1 = (f32[512,512]{1,0:T(8,128)}, bf16[512,512]{1,0:T(8,128)(2,1)}, bf16[2,4,128,512]{3,2,1,0:T(8,128)(2,1)}, bf16[2,4,128,512]{3,2,1,0:T(8,128)(2,1)}) custom-call(s32[3]{0:T(128)} %pad_add_fusion.ints, f32[512,512]{1,0:T(8,128)} %get-tuple-element.138.d_mid_in.d_mid, bf16[1024,128]{1,0:T(8,128)(2,1)} %fusion.code_in, ...), custom_call_target="tpu_custom_call" | custom-call | flops 10737418240 | bytes 8388608 | tf_op jit(solution)/shard_map/self_bwd/pallas_call | solution.py:585
  239.2 2.1 collective-permute-start.36
  241.4 2.5 collective-permute-done.36
  243.8 1.5 add_convert_fusion
  248.6 4.0 %collective-permute-start.40 = (bf16[1,1,128,512]{3,2,1,0:T(8,128)(2,1)}, bf16[1,1,128,512]{3,2,1,0:T(8,128)(2,1)S(1)}, u32[]{:S(2)}, u32[]{:S(2)}) collective-permute-start(bf16[1,1,128,512]{3,2,1,0:T(8,128)(2,1)} %add_convert_fusion.24), channel_id=1, source_target_pairs={{16,18},{17,19},{18,16},{19,17},{20,22},{21,23},{22,20},{23,21},{2... | collective-permute-start | bytes 393224 | tf_op jit(solution)/shard_map/ppermute | solution.py:54
  252.6 1.0 maximum_select_fusion.2
  254.4 3.4 %last.1 = (bf16[512,512]{1,0:T(8,128)(2,1)}, f32[2,512]{1,0:T(2,128)}) custom-call(f32[512,512]{1,0:T(8,128)} %get-tuple-element.156.d_own, bf16[512,512]{1,0:T(8,128)(2,1)} %copy-done.42, bf16[512,512]{1,0:T(8,128)(2,1)} %bitcast.160, f32[512,512]{1,0:T(8,128)} %get-tuple-element.138.d_mid_in.d_mid, f32[8,512]{1,0:T(8,128)} %get-tuple-element.101.norms), custom_call_target="tpu_custom_call" | custom-call | flops 1073741824 | bytes 8388608 | tf_op jit(solution)/shard_map/last/pallas_call | solution.py:585
  257.9 3.6 %all-to-all-start.3 = ((bf16[4,128,512]{2,1,0:T(8,128)(2,1)}), bf16[4,128,512]{2,1,0:T(8,128)(2,1)S(1)}, u32[]{:S(2)}, u32[]{:S(2)}) async-start(bf16[4,128,512]{2,1,0:T(8,128)(2,1)} %bitcast.161), calls=%async_computation.3 | async-start | bytes 1048576 | tf_op jit(solution)/shard_map/all_to_all | solution.py:112
  261.5 3.9 %collective-permute-done.38 = bf16[1,6,128,512]{3,2,1,0:T(8,128)(2,1)S(1)} collective-permute-done((bf16[1,6,128,512]{3,2,1,0:T(8,128)(2,1)}, bf16[1,6,128,512]{3,2,1,0:T(8,128)(2,1)S(1)}, u32[]{:S(2)}, u32[]{:S(2)}) %collective-permute-start.38) | collective-permute-done | bytes 786464 | tf_op jit(solution)/shard_map/ppermute | solution.py:24
  266.6 1.3 collective-permute-start.42
  270.1 1.3 collective-permute-done.43
  272.1 1.9 collective-permute-start.41
  274.0 1.3 collective-permute-start.44
  275.3 11.8 %collective-permute-done.45 = bf16[1,2,144,512]{3,2,1,0:T(8,128)(2,1)S(1)} collective-permute-done((bf16[1,2,144,512]{3,2,1,0:T(8,128)(2,1)S(1)}, bf16[1,2,144,512]{3,2,1,0:T(8,128)(2,1)S(1)}, u32[]{:S(2)}, u32[]{:S(2)}) %collective-permute-start.45) | collective-permute-done | bytes 294944 | tf_op jit(solution)/shard_map/ppermute | solution.py:24
  288.5 1.7 add_bitcast_fusion.1
  291.0 1.4 collective-permute-start.46
  293.1 4.7 %collective-permute-done.47 = bf16[1,1,144,512]{3,2,1,0:T(8,128)(2,1)S(1)} collective-permute-done((bf16[1,1,144,512]{3,2,1,0:T(8,128)(2,1)}, bf16[1,1,144,512]{3,2,1,0:T(8,128)(2,1)S(1)}, u32[]{:S(2)}, u32[]{:S(2)}) %collective-permute-start.47) | collective-permute-done | bytes 147488 | tf_op jit(solution)/shard_map/ppermute | solution.py:24
  301.3 1.0 maximum_select_fusion.3
  (244 shorter events, 34.9 us)
Async XLA Ops:
  3.8 14.9 %collective-permute-start.4 = (bf16[144,512]{1,0:T(8,128)(2,1)S(1)}, bf16[144,512]{1,0:T(8,128)(2,1)S(1)}, u32[]{:S(2)}, u32[]{:S(2)}) collective-permute-start(bf16[144,512]{1,0:T(8,128)(2,1)S(1)} %concatenate.116), channel_id=1, source_target_pairs={{0,2},{1,3},{2,0},{3,1},{4,6},{5,7},{6,4},{7,5},{8,10},{9,11},{10,... | collective-permute-start | bytes 442376 | tf_op jit(solution)/shard_map/ppermute | solution.py:24
  7.2 5.3 %collective-permute-start = (bf16[2,128,512]{2,1,0:T(8,128)(2,1)S(1)}, bf16[2,128,512]{2,1,0:T(8,128)(2,1)S(1)}, u32[]{:S(2)}, u32[]{:S(2)}) collective-permute-start(bf16[2,128,512]{2,1,0:T(8,128)(2,1)S(1)} %get-tuple-element.219), channel_id=1, source_target_pairs={{0,4},{4,0},{8,12},{12,8},{1,5},{5,1},{9,13},{13,9},{2,6},{6,2},{1... | collective-permute-start | bytes 786440 | tf_op jit(solution)/shard_map/ppermute | solution.py:24
  8.3 10.4 %collective-permute-start.12 = (bf16[128,512]{1,0:T(8,128)(2,1)S(1)}, bf16[128,512]{1,0:T(8,128)(2,1)S(1)}, u32[]{:S(2)}, u32[]{:S(2)}) collective-permute-start(bf16[128,512]{1,0:T(8,128)(2,1)S(1)} %bitcast.166), channel_id=1, source_target_pairs={{0,2},{1,3},{2,0},{3,1},{4,6},{5,7},{6,4},{7,5},{8,10},{9,11},{10,... | collective-permute-start | bytes 393224 | tf_op jit(solution)/shard_map/ppermute | solution.py:24
  8.5 24.2 %collective-permute-start.13 = (bf16[1,128,1024]{2,1,0:T(8,128)(2,1)S(1)}, bf16[1,128,1024]{2,1,0:T(8,128)(2,1)S(1)}, u32[]{:S(2)}, u32[]{:S(2)}) collective-permute-start(bf16[1,128,1024]{2,1,0:T(8,128)(2,1)S(1)} %maximum_bitcast_fusion), channel_id=1, source_target_pairs={{0,8},{4,12},{8,0},{12,4},{1,9},{5,13},{9,1},{13,5},{2,10},{6,14},... | collective-permute-start | bytes 786440 | tf_op jit(solution)/shard_map/ppermute | solution.py:24
  9.8 1.5 collective-permute-start.3
  11.2 7.3 %collective-permute-start.9 = (bf16[128,4,64]{0,2,1:T(8,128)(2,1)S(1)}, bf16[128,4,64]{0,2,1:T(8,128)(2,1)S(1)}, u32[]{:S(2)}, u32[]{:S(2)}) collective-permute-start(bf16[128,4,64]{0,2,1:T(8,128)(2,1)S(1)} %pad_maximum_fusion.13), channel_id=1, source_target_pairs={{0,16},{1,17},{2,18},{3,19},{4,20},{5,21},{6,22},{7,23},{8,24},{9,... | collective-permute-start | bytes 196616 | tf_op jit(solution)/shard_map/ppermute | solution.py:32
  12.6 20.1 %collective-permute-start.2 = (bf16[2,128,512]{2,1,0:T(8,128)(2,1)S(1)}, bf16[2,128,512]{2,1,0:T(8,128)(2,1)S(1)}, u32[]{:S(2)}, u32[]{:S(2)}) collective-permute-start(bf16[2,128,512]{2,1,0:T(8,128)(2,1)S(1)} %get-tuple-element.217), channel_id=1, source_target_pairs={{0,4},{4,0},{8,12},{12,8},{1,5},{5,1},{9,13},{13,9},{2,6},{6,2},{1... | collective-permute-start | bytes 786440 | tf_op jit(solution)/shard_map/ppermute | solution.py:24
  13.9 18.8 %all-to-all-start = ((bf16[4,128,512]{2,1,0:T(8,128)(2,1)}), bf16[4,128,512]{2,1,0:T(8,128)(2,1)S(1)}, u32[]{:S(2)}, u32[]{:S(2)}) async-start(bf16[4,128,512]{2,1,0:T(8,128)(2,1)} %maximum_select_fusion), calls=%async_computation | async-start | bytes 1048576 | tf_op jit(solution)/shard_map/all_to_all | solution.py:632
  32.6 10.1 %copy-start.25 = (bf16[4,128,512]{2,1,0:T(8,128)(2,1)}, bf16[4,128,512]{2,1,0:T(8,128)(2,1)S(1)}, u32[]{:S(2)}) copy-start(bf16[4,128,512]{2,1,0:T(8,128)(2,1)S(1)} %all-to-all-done) | copy-start | bytes 1572868
  32.6 7.2 %collective-permute-start.5 = (bf16[2,144,512]{2,1,0:T(8,128)(2,1)S(1)}, bf16[2,144,512]{2,1,0:T(8,128)(2,1)S(1)}, u32[]{:S(2)}, u32[]{:S(2)}) collective-permute-start(bf16[2,144,512]{2,1,0:T(8,128)(2,1)S(1)} %pad_maximum_fusion.7), channel_id=1, source_target_pairs={{0,1},{1,0},{2,3},{3,2},{4,5},{5,4},{6,7},{7,6},{8,9},{9,8},{10,11... | collective-permute-start | bytes 884744 | tf_op jit(solution)/shard_map/ppermute | solution.py:24
  32.7 66.3 %copy-start = (bf16[2,128,1024]{2,1,0:T(8,128)(2,1)}, bf16[2,128,1024]{2,1,0:T(8,128)(2,1)S(1)}, u32[]{:S(2)}) copy-start(bf16[2,128,1024]{2,1,0:T(8,128)(2,1)S(1)} %pad_maximum_fusion.4.refs_0_.refs_2_) | copy-start | bytes 1572868
  33.8 16.2 %collective-permute-start.10 = (bf16[1,128,512]{2,1,0:T(8,128)(2,1)S(1)}, bf16[1,128,512]{2,1,0:T(8,128)(2,1)S(1)}, u32[]{:S(2)}, u32[]{:S(2)}) collective-permute-start(bf16[1,128,512]{2,1,0:T(8,128)(2,1)S(1)} %copy.70), channel_id=1, source_target_pairs={{16,24},{20,28},{24,16},{28,20},{17,25},{21,29},{25,17},{29,21},{1... | collective-permute-start | bytes 393224 | tf_op jit(solution)/shard_map/ppermute | solution.py:54
  40.6 15.0 %collective-permute-start.6 = (bf16[4,144,512]{2,1,0:T(8,128)(2,1)}, bf16[4,144,512]{2,1,0:T(8,128)(2,1)}, u32[]{:S(2)}, u32[]{:S(2)}) collective-permute-start(bf16[4,144,512]{2,1,0:T(8,128)(2,1)} %constant_dynamic-update-slice_fusion.refs_0_), channel_id=1, source_target_pairs={{0,8},{4,12},{8,0},{12,4},{1,9},{5,13},{9,1},{13,5},{2,10},{6,14},... | collective-permute-start | bytes 1769480 | tf_op jit(solution)/shard_map/ppermute | solution.py:24
  40.8 13.5 %collective-permute-start.14 = (bf16[2,128,512]{2,1,0:T(8,128)(2,1)S(1)}, bf16[2,128,512]{2,1,0:T(8,128)(2,1)S(1)}, u32[]{:S(2)}, u32[]{:S(2)}) collective-permute-start(bf16[2,128,512]{2,1,0:T(8,128)(2,1)S(1)} %pad_maximum_fusion.9), channel_id=1, source_target_pairs={{0,1},{1,0},{2,3},{3,2},{4,5},{5,4},{6,7},{7,6},{8,9},{9,8},{10,11... | collective-permute-start | bytes 786440 | tf_op jit(solution)/shard_map/ppermute | solution.py:24
  41.2 14.3 %collective-permute-start.15 = (bf16[2,128,512]{2,1,0:T(8,128)(2,1)S(1)}, bf16[2,128,512]{2,1,0:T(8,128)(2,1)S(1)}, u32[]{:S(2)}, u32[]{:S(2)}) collective-permute-start(bf16[2,128,512]{2,1,0:T(8,128)(2,1)S(1)} %get-tuple-element.215), channel_id=1, source_target_pairs={{0,2},{1,3},{2,0},{3,1},{4,6},{5,7},{6,4},{7,5},{8,10},{9,11},{10,... | collective-permute-start | bytes 786440 | tf_op jit(solution)/shard_map/ppermute | solution.py:24
  42.8 35.9 %collective-permute-start.1 = (bf16[512,512]{1,0:T(8,128)(2,1)S(1)}, bf16[512,512]{1,0:T(8,128)(2,1)}, u32[]{:S(2)}, u32[]{:S(2)}) collective-permute-start(bf16[512,512]{1,0:T(8,128)(2,1)S(1)} %bitcast.158), channel_id=1, source_target_pairs={{0,4},{4,0},{8,12},{12,8},{1,5},{5,1},{9,13},{13,9},{2,6},{6,2},{1... | collective-permute-start | bytes 1572872 | tf_op jit(solution)/shard_map/ppermute | solution.py:24
  45.8 32.9 %all-to-all-start.1 = ((bf16[4,128,512]{2,1,0:T(8,128)(2,1)}), bf16[4,128,512]{2,1,0:T(8,128)(2,1)}, u32[]{:S(2)}, u32[]{:S(2)}) async-start(bf16[4,128,512]{2,1,0:T(8,128)(2,1)} %maximum_select_fusion.1), calls=%async_computation.1 | async-start | bytes 1048576 | tf_op jit(solution)/shard_map/all_to_all | solution.py:633
  50.0 27.9 %collective-permute-start.11 = (bf16[2,128,512]{2,1,0:T(8,128)(2,1)S(1)}, bf16[2,128,512]{2,1,0:T(8,128)(2,1)S(1)}, u32[]{:S(2)}, u32[]{:S(2)}) collective-permute-start(bf16[2,128,512]{2,1,0:T(8,128)(2,1)S(1)} %constant_dynamic-update-slice_fusion.2), channel_id=1, source_target_pairs={{16,18},{17,19},{18,16},{19,17},{20,22},{21,23},{22,20},{23,21},{2... | collective-permute-start | bytes 786440 | tf_op jit(solution)/shard_map/ppermute | solution.py:54
  54.4 25.4 %collective-permute-start.7 = (bf16[4,144,512]{2,1,0:T(8,128)(2,1)}, bf16[4,144,512]{2,1,0:T(8,128)(2,1)}, u32[]{:S(2)}, u32[]{:S(2)}) collective-permute-start(bf16[4,144,512]{2,1,0:T(8,128)(2,1)} %constant_dynamic-update-slice_fusion.refs_0_), channel_id=1, source_target_pairs={{0,4},{4,0},{8,12},{12,8},{1,5},{5,1},{9,13},{13,9},{2,6},{6,2},{1... | collective-permute-start | bytes 1769480 | tf_op jit(solution)/shard_map/ppermute | solution.py:24
  55.5 43.5 %copy-start.2 = (bf16[3,128,512]{2,1,0:T(8,128)(2,1)}, bf16[3,128,512]{2,1,0:T(8,128)(2,1)S(1)}, u32[]{:S(2)}) copy-start(bf16[3,128,512]{2,1,0:T(8,128)(2,1)S(1)} %pad_maximum_fusion.6.refs_2_.refs_4_) | copy-start | bytes 1179652
  55.6 24.1 %collective-permute-start.16 = (bf16[2,2,128,512]{3,2,1,0:T(8,128)(2,1)S(1)}, bf16[2,2,128,512]{3,2,1,0:T(8,128)(2,1)S(1)}, u32[]{:S(2)}, u32[]{:S(2)}) collective-permute-start(bf16[2,2,128,512]{3,2,1,0:T(8,128)(2,1)S(1)} %pad_maximum_fusion.5), channel_id=1, source_target_pairs={{0,1},{1,0},{2,3},{3,2},{4,5},{5,4},{6,7},{7,6},{8,9},{9,8},{10,11... | collective-permute-start | bytes 1572872 | tf_op jit(solution)/shard_map/ppermute | solution.py:24
  56.4 23.4 %collective-permute-start.8 = (bf16[4,144,512]{2,1,0:T(8,128)(2,1)}, bf16[4,144,512]{2,1,0:T(8,128)(2,1)}, u32[]{:S(2)}, u32[]{:S(2)}) collective-permute-start(bf16[4,144,512]{2,1,0:T(8,128)(2,1)} %collective-permute-done.6.refs_1_), channel_id=1, source_target_pairs={{0,4},{4,0},{8,12},{12,8},{1,5},{5,1},{9,13},{13,9},{2,6},{6,2},{1... | collective-permute-start | bytes 1769480 | tf_op jit(solution)/shard_map/ppermute | solution.py:24
  60.7 18.9 %copy-start.14 = (bf16[2,1024,128]{2,1,0:T(8,128)(2,1)}, bf16[2,1024,128]{2,1,0:T(8,128)(2,1)S(1)}, u32[]{:S(2)}) copy-start(bf16[2,1024,128]{2,1,0:T(8,128)(2,1)S(1)} %compare_convert_fusion) | copy-start | bytes 1572868
  78.7 14.4 %collective-permute-start.17 = (bf16[3,128,512]{2,1,0:T(8,128)(2,1)S(1)}, bf16[3,128,512]{2,1,0:T(8,128)(2,1)S(1)}, u32[]{:S(2)}, u32[]{:S(2)}) collective-permute-start(bf16[3,128,512]{2,1,0:T(8,128)(2,1)S(1)} %pad_maximum_fusion.6.refs_2_.refs_4_), channel_id=1, source_target_pairs={{0,8},{4,12},{8,0},{12,4},{1,9},{5,13},{9,1},{13,5},{2,10},{6,14},... | collective-permute-start | bytes 1179656 | tf_op jit(solution)/shard_map/ppermute | solution.py:24
  79.8 19.2 %copy-start.1 = (bf16[3,2,128,512]{3,2,1,0:T(8,128)(2,1)}, bf16[3,2,128,512]{3,2,1,0:T(8,128)(2,1)S(1)}, u32[]{:S(2)}) copy-start(bf16[3,2,128,512]{3,2,1,0:T(8,128)(2,1)S(1)} %pad_maximum_fusion.1.refs_1_.refs_3_) | copy-start | bytes 2359300
  79.8 19.2 %copy-start.3 = (s32[3]{0:T(128)S(1)}, s32[3]{0:T(128)}, u32[]{:S(2)}) copy-start(s32[3]{0:T(128)} %pad_add_fusion.ints) | copy-start | bytes 40
  93.1 5.8 %collective-permute-start.19 = (bf16[3,2,128,512]{3,2,1,0:T(8,128)(2,1)S(1)}, bf16[3,2,128,512]{3,2,1,0:T(8,128)(2,1)S(1)}, u32[]{:S(2)}, u32[]{:S(2)}) collective-permute-start(bf16[3,2,128,512]{3,2,1,0:T(8,128)(2,1)S(1)} %pad_maximum_fusion.1.refs_1_.refs_3_), channel_id=1, source_target_pairs={{0,4},{4,0},{8,12},{12,8},{1,5},{5,1},{9,13},{13,9},{2,6},{6,2},{1... | collective-permute-start | bytes 2359304 | tf_op jit(solution)/shard_map/ppermute | solution.py:24
  95.1 3.8 %collective-permute-start.18 = (bf16[2,128,1024]{2,1,0:T(8,128)(2,1)S(1)}, bf16[2,128,1024]{2,1,0:T(8,128)(2,1)S(1)}, u32[]{:S(2)}, u32[]{:S(2)}) collective-permute-start(bf16[2,128,1024]{2,1,0:T(8,128)(2,1)S(1)} %pad_maximum_fusion.4.refs_0_.refs_2_), channel_id=1, source_target_pairs={{0,4},{4,0},{8,12},{12,8},{1,5},{5,1},{9,13},{13,9},{2,6},{6,2},{1... | collective-permute-start | bytes 1572872 | tf_op jit(solution)/shard_map/ppermute | solution.py:24
  95.2 3.1 %collective-permute-start.20 = (bf16[3,128,512]{2,1,0:T(8,128)(2,1)S(1)}, bf16[3,128,512]{2,1,0:T(8,128)(2,1)S(1)}, u32[]{:S(2)}, u32[]{:S(2)}) collective-permute-start(bf16[3,128,512]{2,1,0:T(8,128)(2,1)S(1)} %pad_maximum_fusion.6.refs_2_.refs_4_), channel_id=1, source_target_pairs={{0,4},{4,0},{8,12},{12,8},{1,5},{5,1},{9,13},{13,9},{2,6},{6,2},{1... | collective-permute-start | bytes 1179656 | tf_op jit(solution)/shard_map/ppermute | solution.py:24
  95.6 3.3 %collective-permute-start.21 = (bf16[3,128,512]{2,1,0:T(8,128)(2,1)S(1)}, bf16[3,128,512]{2,1,0:T(8,128)(2,1)S(1)}, u32[]{:S(2)}, u32[]{:S(2)}) collective-permute-start(bf16[3,128,512]{2,1,0:T(8,128)(2,1)S(1)} %collective-permute-done.17.refs_3_.refs_5_), channel_id=1, source_target_pairs={{0,4},{4,0},{8,12},{12,8},{1,5},{5,1},{9,13},{13,9},{2,6},{6,2},{1... | collective-permute-start | bytes 1179656 | tf_op jit(solution)/shard_map/ppermute | solution.py:24
  95.7 15.2 %collective-permute-start.24 = (bf16[2,2,128,512]{3,2,1,0:T(8,128)(2,1)}, bf16[2,2,128,512]{3,2,1,0:T(8,128)(2,1)S(1)}, u32[]{:S(2)}, u32[]{:S(2)}) collective-permute-start(bf16[2,2,128,512]{3,2,1,0:T(8,128)(2,1)} %pad_maximum_fusion.3), channel_id=1, source_target_pairs={{16,17},{17,16},{18,19},{19,18},{20,21},{21,20},{22,23},{23,22},{2... | collective-permute-start | bytes 1572872 | tf_op jit(solution)/shard_map/ppermute | solution.py:54
  103.0 16.5 %copy-start.10 = (bf16[4,512,512]{2,1,0:T(8,128)(2,1)}, bf16[4,512,512]{2,1,0:T(8,128)(2,1)S(1)}, u32[]{:S(2)}) copy-start(bf16[4,512,512]{2,1,0:T(8,128)(2,1)S(1)} %get-tuple-element.119.hidden_in) | copy-start | bytes 6291460
  103.0 63.7 %copy-start.11 = (bf16[4,512,512]{2,1,0:T(8,128)(2,1)}, bf16[4,512,512]{2,1,0:T(8,128)(2,1)S(1)}, u32[]{:S(2)}) copy-start(bf16[4,512,512]{2,1,0:T(8,128)(2,1)S(1)} %get-tuple-element.120.slope_in) | copy-start | bytes 6291460
  103.0 19.4 %copy-start.15 = (bf16[2,1024,128]{2,1,0:T(8,128)(2,1)S(1)}, bf16[2,1024,128]{2,1,0:T(8,128)(2,1)}, u32[]{:S(2)}) copy-start(bf16[2,1024,128]{2,1,0:T(8,128)(2,1)} %copy-done.14) | copy-start | bytes 1572868
  103.0 16.5 %collective-permute-start.22 = (bf16[512,512]{1,0:T(8,128)(2,1)S(1)}, bf16[512,512]{1,0:T(8,128)(2,1)S(1)}, u32[]{:S(2)}, u32[]{:S(2)}) collective-permute-start(bf16[512,512]{1,0:T(8,128)(2,1)S(1)} %get-tuple-element.106), channel_id=1, source_target_pairs={{0,16},{1,17},{2,18},{3,19},{4,20},{5,21},{6,22},{7,23},{8,24},{9,... | collective-permute-start | bytes 1572872 | tf_op jit(solution)/shard_map/ppermute | solution.py:32
  112.0 13.3 %copy-start.19 = (bf16[4,2,128,512]{3,2,1,0:T(8,128)(2,1)}, bf16[4,2,128,512]{3,2,1,0:T(8,128)(2,1)S(1)}, u32[]{:S(2)}) copy-start(bf16[4,2,128,512]{3,2,1,0:T(8,128)(2,1)S(1)} %pad_maximum_fusion.refs_0_) | copy-start | bytes 3145732
  119.5 5.8 %collective-permute-start.25 = (bf16[4,2,128,512]{3,2,1,0:T(8,128)(2,1)S(1)}, bf16[4,2,128,512]{3,2,1,0:T(8,128)(2,1)S(1)}, u32[]{:S(2)}, u32[]{:S(2)}) collective-permute-start(bf16[4,2,128,512]{3,2,1,0:T(8,128)(2,1)S(1)} %pad_maximum_fusion.refs_0_), channel_id=1, source_target_pairs={{16,20},{20,16},{24,28},{28,24},{17,21},{21,17},{25,29},{29,25},{1... | collective-permute-start | bytes 3145736 | tf_op jit(solution)/shard_map/ppermute | solution.py:54
  122.3 3.0 collective-permute-start.23
  166.7 2.2 collective-permute-start.26
  170.1 22.1 %collective-permute-start.28 = (bf16[2,4,128,512]{3,2,1,0:T(8,128)(2,1)}, bf16[2,4,128,512]{3,2,1,0:T(8,128)(2,1)S(1)}, u32[]{:S(2)}, u32[]{:S(2)}) collective-permute-start(bf16[2,4,128,512]{3,2,1,0:T(8,128)(2,1)} %get-tuple-element.113), channel_id=1, source_target_pairs={{16,20},{20,16},{24,28},{28,24},{17,21},{21,17},{25,29},{29,25},{1... | collective-permute-start | bytes 3145736 | tf_op jit(solution)/shard_map/ppermute | solution.py:54
  174.3 17.9 %all-to-all-start.2 = ((bf16[4,128,512]{2,1,0:T(8,128)(2,1)}), bf16[4,128,512]{2,1,0:T(8,128)(2,1)S(1)}, u32[]{:S(2)}, u32[]{:S(2)}) async-start(bf16[4,128,512]{2,1,0:T(8,128)(2,1)} %bitcast.35), calls=%async_computation.2 | async-start | bytes 1048576 | tf_op jit(solution)/shard_map/all_to_all | solution.py:112
  177.8 12.7 %collective-permute-start.27 = (bf16[512,512]{1,0:T(8,128)(2,1)S(1)}, bf16[512,512]{1,0:T(8,128)(2,1)S(1)}, u32[]{:S(2)}, u32[]{:S(2)}) collective-permute-start(bf16[512,512]{1,0:T(8,128)(2,1)S(1)} %add_convert_fusion.8), channel_id=1, source_target_pairs={{16,0},{17,1},{18,2},{19,3},{20,4},{21,5},{22,6},{23,7},{24,8},{25... | collective-permute-start | bytes 1572872 | tf_op jit(solution)/shard_map/ppermute | solution.py:32
  194.1 16.5 %collective-permute-start.30 = (bf16[2,4,128,512]{3,2,1,0:T(8,128)(2,1)}, bf16[2,4,128,512]{3,2,1,0:T(8,128)(2,1)S(1)}, u32[]{:S(2)}, u32[]{:S(2)}) collective-permute-start(bf16[2,4,128,512]{3,2,1,0:T(8,128)(2,1)} %get-tuple-element.128), channel_id=1, source_target_pairs={{0,4},{4,0},{8,12},{12,8},{1,5},{5,1},{9,13},{13,9},{2,6},{6,2},{1... | collective-permute-start | bytes 3145736 | tf_op jit(solution)/shard_map/ppermute | solution.py:24
  195.2 15.5 %collective-permute-start.31 = (bf16[2,4,128,512]{3,2,1,0:T(8,128)(2,1)}, bf16[2,4,128,512]{3,2,1,0:T(8,128)(2,1)S(1)}, u32[]{:S(2)}, u32[]{:S(2)}) collective-permute-start(bf16[2,4,128,512]{3,2,1,0:T(8,128)(2,1)} %get-tuple-element.129), channel_id=1, source_target_pairs={{0,4},{4,0},{8,12},{12,8},{1,5},{5,1},{9,13},{13,9},{2,6},{6,2},{1... | collective-permute-start | bytes 3145736 | tf_op jit(solution)/shard_map/ppermute | solution.py:24
  195.2 18.5 %copy-start.18 = (bf16[2,4,128,512]{3,2,1,0:T(8,128)(2,1)S(1)}, bf16[2,4,128,512]{3,2,1,0:T(8,128)(2,1)}, u32[]{:S(2)}) copy-start(bf16[2,4,128,512]{3,2,1,0:T(8,128)(2,1)} %get-tuple-element.135) | copy-start | bytes 3145732
  195.5 15.1 %collective-permute-start.32 = (bf16[1,4,128,512]{3,2,1,0:T(8,128)(2,1)S(1)}, bf16[1,4,128,512]{3,2,1,0:T(8,128)(2,1)S(1)}, u32[]{:S(2)}, u32[]{:S(2)}) collective-permute-start(bf16[1,4,128,512]{3,2,1,0:T(8,128)(2,1)S(1)} %get-tuple-element.132), channel_id=1, source_target_pairs={{16,24},{20,28},{24,16},{28,20},{17,25},{21,29},{25,17},{29,21},{1... | collective-permute-start | bytes 1572872 | tf_op jit(solution)/shard_map/ppermute | solution.py:54
  211.5 26.8 %collective-permute-start.35 = (bf16[1,2,128,512]{3,2,1,0:T(8,128)(2,1)S(1)}, bf16[1,2,128,512]{3,2,1,0:T(8,128)(2,1)S(1)}, u32[]{:S(2)}, u32[]{:S(2)}) collective-permute-start(bf16[1,2,128,512]{3,2,1,0:T(8,128)(2,1)S(1)} %get-tuple-element.207), channel_id=1, source_target_pairs={{16,17},{17,16},{18,19},{19,18},{20,21},{21,20},{22,23},{23,22},{2... | collective-permute-start | bytes 786440 | tf_op jit(solution)/shard_map/ppermute | solution.py:54
  214.1 24.2 %collective-permute-start.34 = (bf16[2,2,128,512]{3,2,1,0:T(8,128)(2,1)S(1)}, bf16[2,2,128,512]{3,2,1,0:T(8,128)(2,1)S(1)}, u32[]{:S(2)}, u32[]{:S(2)}) collective-permute-start(bf16[2,2,128,512]{3,2,1,0:T(8,128)(2,1)S(1)} %get-tuple-element.197), channel_id=1, source_target_pairs={{0,1},{1,0},{2,3},{3,2},{4,5},{5,4},{6,7},{7,6},{8,9},{9,8},{10,11... | collective-permute-start | bytes 1572872 | tf_op jit(solution)/shard_map/ppermute | solution.py:24
  215.7 22.6 %collective-permute-start.33 = (bf16[1,4,128,512]{3,2,1,0:T(8,128)(2,1)S(1)}, bf16[1,4,128,512]{3,2,1,0:T(8,128)(2,1)S(1)}, u32[]{:S(2)}, u32[]{:S(2)}) collective-permute-start(bf16[1,4,128,512]{3,2,1,0:T(8,128)(2,1)S(1)} %get-tuple-element.200), channel_id=1, source_target_pairs={{0,8},{4,12},{8,0},{12,4},{1,9},{5,13},{9,1},{13,5},{2,10},{6,14},... | collective-permute-start | bytes 1572872 | tf_op jit(solution)/shard_map/ppermute | solution.py:24
  239.2 4.6 %collective-permute-start.36 = (bf16[2,4,128,512]{3,2,1,0:T(8,128)(2,1)}, bf16[2,4,128,512]{3,2,1,0:T(8,128)(2,1)S(1)}, u32[]{:S(2)}, u32[]{:S(2)}) collective-permute-start(bf16[2,4,128,512]{3,2,1,0:T(8,128)(2,1)} %get-tuple-element.150), channel_id=1, source_target_pairs={{0,4},{4,0},{8,12},{12,8},{1,5},{5,1},{9,13},{13,9},{2,6},{6,2},{1... | collective-permute-start | bytes 3145736 | tf_op jit(solution)/shard_map/ppermute | solution.py:24
  246.5 19.0 %collective-permute-start.38 = (bf16[1,6,128,512]{3,2,1,0:T(8,128)(2,1)}, bf16[1,6,128,512]{3,2,1,0:T(8,128)(2,1)S(1)}, u32[]{:S(2)}, u32[]{:S(2)}) collective-permute-start(bf16[1,6,128,512]{3,2,1,0:T(8,128)(2,1)} %pad_maximum_fusion.2), channel_id=1, source_target_pairs={{0,8},{4,12},{8,0},{12,4},{1,9},{5,13},{9,1},{13,5},{2,10},{6,14},... | collective-permute-start | bytes 2359304 | tf_op jit(solution)/shard_map/ppermute | solution.py:24
  246.7 5.9 %collective-permute-start.29 = (bf16[2,128,512]{2,1,0:T(8,128)(2,1)S(1)}, bf16[2,128,512]{2,1,0:T(8,128)(2,1)S(1)}, u32[]{:S(2)}, u32[]{:S(2)}) collective-permute-start(bf16[2,128,512]{2,1,0:T(8,128)(2,1)S(1)} %get-tuple-element.213), channel_id=1, source_target_pairs={{0,4},{4,0},{8,12},{12,8},{1,5},{5,1},{9,13},{13,9},{2,6},{6,2},{1... | collective-permute-start | bytes 786440 | tf_op jit(solution)/shard_map/ppermute | solution.py:24
  247.4 6.2 %collective-permute-start.37 = (bf16[512,512]{1,0:T(8,128)(2,1)S(1)}, bf16[512,512]{1,0:T(8,128)(2,1)S(1)}, u32[]{:S(2)}, u32[]{:S(2)}) collective-permute-start(bf16[512,512]{1,0:T(8,128)(2,1)S(1)} %copy-done.39), channel_id=1, source_target_pairs={{0,4},{4,0},{8,12},{12,8},{1,5},{5,1},{9,13},{13,9},{2,6},{6,2},{1... | collective-permute-start | bytes 1572872 | tf_op jit(solution)/shard_map/ppermute | solution.py:24
  247.6 13.9 %collective-permute-start.39 = (bf16[1,2,128,512]{3,2,1,0:T(8,128)(2,1)S(1)}, bf16[1,2,128,512]{3,2,1,0:T(8,128)(2,1)S(1)}, u32[]{:S(2)}, u32[]{:S(2)}) collective-permute-start(bf16[1,2,128,512]{3,2,1,0:T(8,128)(2,1)S(1)} %get-tuple-element.205), channel_id=1, source_target_pairs={{0,1},{1,0},{2,3},{3,2},{4,5},{5,4},{6,7},{7,6},{8,9},{9,8},{10,11... | collective-permute-start | bytes 786440 | tf_op jit(solution)/shard_map/ppermute | solution.py:24
  248.6 12.9 %collective-permute-start.40 = (bf16[1,1,128,512]{3,2,1,0:T(8,128)(2,1)}, bf16[1,1,128,512]{3,2,1,0:T(8,128)(2,1)S(1)}, u32[]{:S(2)}, u32[]{:S(2)}) collective-permute-start(bf16[1,1,128,512]{3,2,1,0:T(8,128)(2,1)} %add_convert_fusion.24), channel_id=1, source_target_pairs={{16,18},{17,19},{18,16},{19,17},{20,22},{21,23},{22,20},{23,21},{2... | collective-permute-start | bytes 393224 | tf_op jit(solution)/shard_map/ppermute | solution.py:54
  257.9 10.0 %copy-start.30 = (bf16[1,2,128,512]{3,2,1,0:T(8,128)(2,1)S(1)}, bf16[1,2,128,512]{3,2,1,0:T(8,128)(2,1)}, u32[]{:S(2)}) copy-start(bf16[1,2,128,512]{3,2,1,0:T(8,128)(2,1)} %copy-done.28) | copy-start | bytes 786436
  257.9 29.9 %all-to-all-start.3 = ((bf16[4,128,512]{2,1,0:T(8,128)(2,1)}), bf16[4,128,512]{2,1,0:T(8,128)(2,1)S(1)}, u32[]{:S(2)}, u32[]{:S(2)}) async-start(bf16[4,128,512]{2,1,0:T(8,128)(2,1)} %bitcast.161), calls=%async_computation.3 | async-start | bytes 1048576 | tf_op jit(solution)/shard_map/all_to_all | solution.py:112
  266.6 2.1 collective-permute-start.42
  268.7 2.7 collective-permute-start.43
  271.5 15.6 %collective-permute-start.45 = (bf16[1,2,144,512]{3,2,1,0:T(8,128)(2,1)S(1)}, bf16[1,2,144,512]{3,2,1,0:T(8,128)(2,1)S(1)}, u32[]{:S(2)}, u32[]{:S(2)}) collective-permute-start(bf16[1,2,144,512]{3,2,1,0:T(8,128)(2,1)S(1)} %pad_maximum_fusion.8), channel_id=1, source_target_pairs={{0,1},{1,0},{2,3},{3,2},{4,5},{5,4},{6,7},{7,6},{8,9},{9,8},{10,11... | collective-permute-start | bytes 884744 | tf_op jit(solution)/shard_map/ppermute | solution.py:24
  272.1 15.7 %collective-permute-start.41 = (bf16[1,2,128,512]{3,2,1,0:T(8,128)(2,1)S(1)}, bf16[1,2,128,512]{3,2,1,0:T(8,128)(2,1)S(1)}, u32[]{:S(2)}, u32[]{:S(2)}) collective-permute-start(bf16[1,2,128,512]{3,2,1,0:T(8,128)(2,1)S(1)} %pad_maximum_fusion.10), channel_id=1, source_target_pairs={{0,2},{1,3},{2,0},{3,1},{4,6},{5,7},{6,4},{7,5},{8,10},{9,11},{10,... | collective-permute-start | bytes 786440 | tf_op jit(solution)/shard_map/ppermute | solution.py:24
  274.0 13.8 %collective-permute-start.44 = (bf16[128,4,64]{0,2,1:T(8,128)(2,1)S(1)}, bf16[128,4,64]{0,2,1:T(8,128)(2,1)S(1)}, u32[]{:S(2)}, u32[]{:S(2)}) collective-permute-start(bf16[128,4,64]{0,2,1:T(8,128)(2,1)S(1)} %fusion.3), channel_id=1, source_target_pairs={{16,0},{17,1},{18,2},{19,3},{20,4},{21,5},{22,6},{23,7},{24,8},{25... | collective-permute-start | bytes 196616 | tf_op jit(solution)/shard_map/ppermute | solution.py:32
  287.8 10.0 %collective-permute-start.47 = (bf16[1,1,144,512]{3,2,1,0:T(8,128)(2,1)}, bf16[1,1,144,512]{3,2,1,0:T(8,128)(2,1)S(1)}, u32[]{:S(2)}, u32[]{:S(2)}) collective-permute-start(bf16[1,1,144,512]{3,2,1,0:T(8,128)(2,1)} %add_convert_fusion.18), channel_id=1, source_target_pairs={{0,2},{1,3},{2,0},{3,1},{4,6},{5,7},{6,4},{7,5},{8,10},{9,11},{10,... | collective-permute-start | bytes 442376 | tf_op jit(solution)/shard_map/ppermute | solution.py:24
  291.0 10.3 %collective-permute-start.46 = (bf16[2,128,512]{2,1,0:T(8,128)(2,1)S(1)}, bf16[2,128,512]{2,1,0:T(8,128)(2,1)S(1)}, u32[]{:S(2)}, u32[]{:S(2)}) collective-permute-start(bf16[2,128,512]{2,1,0:T(8,128)(2,1)S(1)} %get-tuple-element.211), channel_id=1, source_target_pairs={{0,4},{4,0},{8,12},{12,8},{1,5},{5,1},{9,13},{13,9},{2,6},{6,2},{1... | collective-permute-start | bytes 786440 | tf_op jit(solution)/shard_map/ppermute | solution.py:24
  (32 other events, 130.3 us)
where the time goes:
time: 306 us; the launch traced here: 303 us
  waiting for transfers between devices  102 us (33%)
  Pallas kernels  80.5 us (26%)
  starting transfers between devices  77.5 us (25%)
  other arithmetic  21.9 us (7%)
  local copies, waits for them, and re-layouts  18.9 us (6%)
    pallas_call x6, Pallas kernels, call(): pl.pallas_call(kernel, name=name, in_specs=[spec for _, spec in ins], out...  80.5 us
    ppermute x8, waiting for transfers between devices, decoder_swap(): return lax.ppermute(block, ('section', axis), pairs)  34.6 us
    ppermute x36, starting transfers between devices, swap(): return lax.ppermute(block, axis, [(i, i ^ bit) for i in range(count)])  33.4 us
    ppermute x36, waiting for transfers between devices, swap(): return lax.ppermute(block, axis, [(i, i ^ bit) for i in range(count)])  32.7 us
    ppermute x8, starting transfers between devices, decoder_swap(): return lax.ppermute(block, ('section', axis), pairs)  23 us
    ppermute x4, waiting for transfers between devices, oneway(): return lax.ppermute(block, axis, [(source, target)])  18.8 us
    all_to_all x1, waiting for transfers between devices, on_device(): lax.all_to_all(rows_in(layer_in[0]), 'mp', 0, 0, tiled=True)  13.8 us
    unnamed x97, local copies, waits for them, and re-layouts  12.5 us
  transfers between devices with their start and end apart: 52, of which 19 were waited for; matrix products, arithmetic and copies ran while one was open for 8% of the time, Pallas kernels for 13%

commit v1 on v0

--- a/solution.py
+++ b/solution.py
@@ -16,7 +16,7 @@
 BF = jnp.bfloat16
 F32 = jnp.float32
 PAD = 16
-VMEM_MIB = {"self_fwd": 56, "feed_fwd": 22, "decoder": 56, "feed_bwd": 56, "self_bwd": 56, "last": 56}
+VMEM_MIB = {"self_fwd": 56, "feed_fwd": 22, "decoder": 46, "feed_bwd": 56, "self_bwd": 56, "last": 56}
 
 
 def swap(block, axis, bit):
@@ -751,11 +751,10 @@
     )
     mem_sum = add(mem_keep, swap(mem_send, "dp", 1))
     d_mem = oneway(mem_sum, "section", 1, 0)
-    got3 = decoder_swap(after(send3, mem_sum), "dp", 1)
-    section_out = rows_out(jnp.where(encoder, memory, after(decoded, mem_sum)))
-    d_mem, got3, section_out = together(d_mem, got3, section_out)
     bit = bits[-1]
+    got3 = decoder_swap(after(send3, d_mem), "dp", 1)
     keep3, send3 = fold(keep3, got3)
+    got3 = decoder_swap(send3, "dp", bit)
     small, d_mid, keep_u, send_u, keep_d, send_d = call(
         functools.partial(feed_bwd_kernel, pieces2, len(weights2)),
         "feed_bwd",
@@ -770,7 +769,7 @@
         input_output_aliases={9: 1, 10: 2, 11: 3, 12: 4, 13: 5},
     )
     got_u, got_d = swap(send_u, "dp", 1), swap(send_d, "dp", 1)
-    got3 = decoder_swap(after(send3, d_mem), "dp", bit)
+    section_out = rows_out(jnp.where(encoder, memory, after(decoded, small)))
 
     def self_bwd(pairs, kept, d_mid):
         return call(
@@ -794,7 +793,9 @@
     keep3, send3 = fold(keep3, got3, 1)
     got3 = decoder_swap(send3, "mp", 1)
     d_own, d_other, keep1, send1 = self_bwd(list(range(ways)), kept, after(d_mid, send_u, send_d, send3))
-    d_other, send1, got_u, got_d, got3 = together(d_other, send1, got_u, got_d, got3)
+    d_other, send1, got_u, got_d, got3, section_out = together(
+        d_other, send1, got_u, got_d, got3, section_out
+    )
     got1 = swap(send1, "dp", 1)
     d_got = swap(d_other, "dp", 1)
     keep3, got3 = fold_mp(keep3, got3, 2, decoder_swap)
@@ -842,7 +843,7 @@
     got = swap(jnp.concatenate([send_u, send_d], axis=1), "mp", 2)
     keep1, send1 = fold(keep1, got1, 1)
     got1 = swap(send1, "mp", 2)
-    got, back, in_grads = after((got, back, in_grads), send1)
+    got, back, in_grads, section_out = after((got, back, in_grads, section_out), send1)
     got_u, got_d = halves(got, 1)
     r_up, r_down, r1 = total(keep_u, got_u), total(keep_d, got_d), total(keep1, got1)
     small, r1 = r1[blk, : 6 * each].reshape(6, each), r1[:blk]

time: 306 us -> 303 us (level)
  waiting for transfers between devices: 102 us -> 96 us
  other arithmetic: 21.9 us -> 26.8 us
    ppermute x8, waiting for transfers between devices: 34.6 us -> 28.1 us  [decoder_swap(): return lax.ppermute(block, ('section', axis), pairs)]
    convert_element_type x13, other arithmetic: 7.18 us -> 12.5 us  [add(): return (a.astype(F32) + b.astype(F32)).astype(BF)]
    unnamed x97 -> x73, local copies, waits for them, and re-layouts: 12.5 us -> 12 us
  transfers between devices with their start and end apart: 52 -> 52, of which waited for: 19 -> 17; matrix products, arithmetic and copies ran while one was open for 8% -> 12% of each run, Pallas kernels for 13% -> 14%
where the time goes in v1:
time: 303 us; the launch traced here: 299 us
  waiting for transfers between devices  96 us (32%)
  Pallas kernels  78.7 us (26%)
  starting transfers between devices  78 us (26%)
  other arithmetic  26.8 us (9%)
  local copies, waits for them, and re-layouts  17 us (6%)
    pallas_call x6, Pallas kernels, call(): pl.pallas_call(kernel, name=name, in_specs=[spec for _, spec in ins], out...  78.7 us
    ppermute x36, starting transfers between devices, swap(): return lax.ppermute(block, axis, [(i, i ^ bit) for i in range(count)])  35.3 us
    ppermute x36, waiting for transfers between devices, swap(): return lax.ppermute(block, axis, [(i, i ^ bit) for i in range(count)])  32.3 us
    ppermute x8, waiting for transfers between devices, decoder_swap(): return lax.ppermute(block, ('section', axis), pairs)  28.1 us
    ppermute x8, starting transfers between devices, decoder_swap(): return lax.ppermute(block, ('section', axis), pairs)  22.4 us
    ppermute x4, waiting for transfers between devices, oneway(): return lax.ppermute(block, axis, [(source, target)])  21.8 us
    all_to_all x1, waiting for transfers between devices, on_device(): lax.all_to_all(rows_in(layer_in[0]), 'mp', 0, 0, tiled=True)  13.9 us
    convert_element_type x13, other arithmetic, add(): return (a.astype(F32) + b.astype(F32)).astype(BF)  12.5 us
  transfers between devices with their start and end apart: 52, of which 17 were waited for; matrix products, arithmetic and copies ran while one was open for 12% of the time, Pallas kernels for 14%

profile of v1, /device:TPU:3, one launch (start us, length us, event | category | flops | bytes accessed | tf_op | source)
XLA Modules:
  0.0 298.6 jit_solution(4326185315222485538)
XLA Ops:
  2.2 1.3 collective-permute-start.9
  3.5 2.4 collective-permute-start.12
  7.6 1.0 copy.53
  9.0 1.1 select_bitcast_fusion.5
  11.7 1.2 collective-permute-start.13
  14.2 4.6 %all-to-all-start = ((bf16[4,128,512]{2,1,0:T(8,128)(2,1)}), bf16[4,128,512]{2,1,0:T(8,128)(2,1)}, u32[]{:S(2)}, u32[]{:S(2)}) async-start(bf16[4,128,512]{2,1,0:T(8,128)(2,1)} %maximum_select_fusion), calls=%async_computation | async-start | bytes 1048576 | tf_op jit(solution)/shard_map/all_to_all | solution.py:632
  19.1 13.9 %all-to-all-done = bf16[4,128,512]{2,1,0:T(8,128)(2,1)} async-done(((bf16[4,128,512]{2,1,0:T(8,128)(2,1)}), bf16[4,128,512]{2,1,0:T(8,128)(2,1)}, u32[]{:S(2)}, u32[]{:S(2)}) %all-to-all-start) | async-done | bytes 524320 | tf_op jit(solution)/shard_map/all_to_all | solution.py:632
  34.0 2.2 collective-permute-start.10
  37.0 3.2 %collective-permute-done.5 = bf16[2,144,512]{2,1,0:T(8,128)(2,1)S(1)} collective-permute-done((bf16[2,144,512]{2,1,0:T(8,128)(2,1)S(1)}, bf16[2,144,512]{2,1,0:T(8,128)(2,1)S(1)}, u32[]{:S(2)}, u32[]{:S(2)}) %collective-permute-start.5) | collective-permute-done | bytes 294944 | tf_op jit(solution)/shard_map/ppermute | solution.py:24
  41.7 1.2 collective-permute-start.15
  42.9 3.1 %collective-permute-start.1 = (bf16[512,512]{1,0:T(8,128)(2,1)}, bf16[512,512]{1,0:T(8,128)(2,1)}, u32[]{:S(2)}, u32[]{:S(2)}) collective-permute-start(bf16[512,512]{1,0:T(8,128)(2,1)} %bitcast.6.x_own), channel_id=1, source_target_pairs={{0,4},{4,0},{8,12},{12,8},{1,5},{5,1},{9,13},{13,9},{2,6},{6,2},{1... | collective-permute-start | bytes 1572872 | tf_op jit(solution)/shard_map/ppermute | solution.py:24
  46.0 3.5 %all-to-all-start.1 = ((bf16[4,128,512]{2,1,0:T(8,128)(2,1)}), bf16[4,128,512]{2,1,0:T(8,128)(2,1)S(1)}, u32[]{:S(2)}, u32[]{:S(2)}) async-start(bf16[4,128,512]{2,1,0:T(8,128)(2,1)} %maximum_select_fusion.1), calls=%async_computation.1 | async-start | bytes 1048576 | tf_op jit(solution)/shard_map/all_to_all | solution.py:633
  49.5 4.7 %collective-permute-start.11 = (bf16[2,128,512]{2,1,0:T(8,128)(2,1)S(1)}, bf16[2,128,512]{2,1,0:T(8,128)(2,1)S(1)}, u32[]{:S(2)}, u32[]{:S(2)}) collective-permute-start(bf16[2,128,512]{2,1,0:T(8,128)(2,1)S(1)} %constant_dynamic-update-slice_fusion.2), channel_id=1, source_target_pairs={{16,18},{17,19},{18,16},{19,17},{20,22},{21,23},{22,20},{23,21},{2... | collective-permute-start | bytes 786440 | tf_op jit(solution)/shard_map/ppermute | solution.py:54
  54.3 2.6 collective-permute-start.7
  57.1 4.8 %collective-permute-start.8 = (bf16[4,144,512]{2,1,0:T(8,128)(2,1)}, bf16[4,144,512]{2,1,0:T(8,128)(2,1)}, u32[]{:S(2)}, u32[]{:S(2)}) collective-permute-start(bf16[4,144,512]{2,1,0:T(8,128)(2,1)} %collective-permute-done.6.refs_1_), channel_id=1, source_target_pairs={{0,4},{4,0},{8,12},{12,8},{1,5},{5,1},{9,13},{13,9},{2,6},{6,2},{1... | collective-permute-start | bytes 1769480 | tf_op jit(solution)/shard_map/ppermute | solution.py:24
  63.0 14.9 %collective-permute-done.11 = bf16[2,128,512]{2,1,0:T(8,128)(2,1)S(1)} collective-permute-done((bf16[2,128,512]{2,1,0:T(8,128)(2,1)S(1)}, bf16[2,128,512]{2,1,0:T(8,128)(2,1)S(1)}, u32[]{:S(2)}, u32[]{:S(2)}) %collective-permute-start.11) | collective-permute-done | bytes 262176 | tf_op jit(solution)/shard_map/ppermute | solution.py:54
  78.1 1.1 collective-permute-start.17
  79.2 1.1 pad_maximum_fusion.1.refs_1_.refs_3_
  80.4 13.3 %self_fwd.1 = (bf16[4,512,128]{2,1,0:T(8,128)(2,1)}, bf16[4,1024,128]{2,1,0:T(8,128)(2,1)}, bf16[4,1024,128]{2,1,0:T(8,128)(2,1)}, f32[4,512,128]{2,1,0:T(8,128)...) custom-call(s32[3]{0:T(128)} %pad_add_fusion.ints, ...), custom_call_target="tpu_custom_call" | custom-call | flops 5368709120 | bytes 8388608 | tf_op jit(solution)/shard_map/self_fwd/pallas_call | solution.py:585
  93.7 2.0 collective-permute-start.19
  96.3 2.1 collective-permute-start.24
  100.3 1.2 copy-done.13
  102.5 1.3 copy-done.12
  104.8 1.3 collective-permute-start.22
  106.1 5.2 %collective-permute-done.24 = bf16[2,2,128,512]{3,2,1,0:T(8,128)(2,1)S(1)} collective-permute-done((bf16[2,2,128,512]{3,2,1,0:T(8,128)(2,1)S(1)}, bf16[2,2,128,512]{3,2,1,0:T(8,128)(2,1)S(1)}, u32[]{:S(2)}, u32[]{:S(2)}) %collective-permute-start.24) | collective-permute-done | bytes 524320 | tf_op jit(solution)/shard_map/ppermute | solution.py:54
  111.4 10.6 %collective-permute-done.22.mem_own = bf16[512,512]{1,0:T(8,128)(2,1)S(1)} collective-permute-done((bf16[512,512]{1,0:T(8,128)(2,1)S(1)}, bf16[512,512]{1,0:T(8,128)(2,1)S(1)}, u32[]{:S(2)}, u32[]{:S(2)}) %collective-permute-start.22) | collective-permute-done | bytes 524320 | tf_op jit(solution)/shard_map/ppermute | solution.py:32
  121.9 2.8 collective-permute-start.25
  124.8 2.9 collective-permute-done.23.mem_other
  128.8 37.9 %decoder.1 = (bf16[512,512]{1,0:T(8,128)(2,1)S(1)}, f32[512,512]{1,0:T(8,128)}, bf16[512,512]{1,0:T(8,128)(2,1)S(1)}, bf16[512,512]{1,0:T(8,128)(2,1)S(1)}, f32[...) custom-call(s32[3]{0:T(128)S(1)} %copy-done.4, ...), custom_call_target="tpu_custom_call" | custom-call | flops 42949672960 | bytes 8388608 | tf_op jit(solution)/shard_map/decoder/pallas_call | solution.py:585
  167.1 1.5 collective-permute-done.26
  168.8 1.3 collective-permute-start.27
  170.1 11.2 %collective-permute-done.27.d_mem_in = bf16[512,512]{1,0:T(8,128)(2,1)S(1)} collective-permute-done((bf16[512,512]{1,0:T(8,128)(2,1)S(1)}, bf16[512,512]{1,0:T(8,128)(2,1)S(1)}, u32[]{:S(2)}, u32[]{:S(2)}) %collective-permute-start.27) | collective-permute-done | bytes 524320 | tf_op jit(solution)/shard_map/ppermute | solution.py:32
  181.3 2.8 collective-permute-start.30
  184.2 1.9 feed_bwd.1
  186.6 1.1 add_convert_fusion.3
  187.7 3.0 collective-permute-start.31
  191.6 3.5 %all-to-all-start.2 = ((bf16[4,128,512]{2,1,0:T(8,128)(2,1)}), bf16[4,128,512]{2,1,0:T(8,128)(2,1)S(1)}, u32[]{:S(2)}, u32[]{:S(2)}) async-start(bf16[4,128,512]{2,1,0:T(8,128)(2,1)} %bitcast.35), calls=%async_computation.2 | async-start | bytes 1048576 | tf_op jit(solution)/shard_map/all_to_all | solution.py:112
  195.1 7.9 %collective-permute-done.31 = bf16[1,4,128,512]{3,2,1,0:T(8,128)(2,1)S(1)} collective-permute-done((bf16[1,4,128,512]{3,2,1,0:T(8,128)(2,1)}, bf16[1,4,128,512]{3,2,1,0:T(8,128)(2,1)S(1)}, u32[]{:S(2)}, u32[]{:S(2)}) %collective-permute-start.31) | collective-permute-done | bytes 524320 | tf_op jit(solution)/shard_map/ppermute | solution.py:54
  203.8 2.4 collective-permute-start.34
  206.2 2.7 add_convert_fusion.2
  208.9 1.2 collective-permute-start.33
  210.1 1.1 add_convert_fusion.5
  211.2 1.1 collective-permute-start.32
  212.2 21.2 %self_bwd.1 = (f32[512,512]{1,0:T(8,128)}, bf16[512,512]{1,0:T(8,128)(2,1)}, bf16[2,4,128,512]{3,2,1,0:T(8,128)(2,1)}, bf16[2,4,128,512]{3,2,1,0:T(8,128)(2,1)}) custom-call(s32[3]{0:T(128)} %pad_add_fusion.ints, f32[512,512]{1,0:T(8,128)} %get-tuple-element.130.d_mid_in.d_mid, bf16[1024,128]{1,0:T(8,128)(2,1)} %fusion.code_in, ...), custom_call_target="tpu_custom_call" | custom-call | flops 10737418240 | bytes 8388608 | tf_op jit(solution)/shard_map/self_bwd/pallas_call | solution.py:585
  233.5 2.1 collective-permute-start.35
  235.7 2.4 collective-permute-done.35
  238.1 1.5 add_convert_fusion
  239.6 1.2 add_convert_fusion.13
  243.1 2.5 collective-permute-start.39
  245.8 1.8 collective-permute-start.38
  248.4 3.4 %last.1 = (bf16[512,512]{1,0:T(8,128)(2,1)}, f32[2,512]{1,0:T(2,128)}) custom-call(f32[512,512]{1,0:T(8,128)} %get-tuple-element.151.d_own, bf16[512,512]{1,0:T(8,128)(2,1)} %copy-done.30, bf16[512,512]{1,0:T(8,128)(2,1)} %bitcast.6.x_own, f32[512,512]{1,0:T(8,128)} %get-tuple-element.130.d_mid_in.d_mid, f32[8,512]{1,0:T(8,128)} %get-tuple-element.99.norms), custom_call_target="tpu_custom_call" | custom-call | flops 1073741824 | bytes 8388608 | tf_op jit(solution)/shard_map/last/pallas_call | solution.py:585
  251.8 3.5 %all-to-all-start.3 = ((bf16[4,128,512]{2,1,0:T(8,128)(2,1)}), bf16[4,128,512]{2,1,0:T(8,128)(2,1)S(1)}, u32[]{:S(2)}, u32[]{:S(2)}) async-start(bf16[4,128,512]{2,1,0:T(8,128)(2,1)} %bitcast.160), calls=%async_computation.3 | async-start | bytes 1048576 | tf_op jit(solution)/shard_map/all_to_all | solution.py:112
  256.1 4.8 %collective-permute-done.37 = bf16[1,6,128,512]{3,2,1,0:T(8,128)(2,1)} collective-permute-done((bf16[1,6,128,512]{3,2,1,0:T(8,128)(2,1)}, bf16[1,6,128,512]{3,2,1,0:T(8,128)(2,1)}, u32[]{:S(2)}, u32[]{:S(2)}) %collective-permute-start.37) | collective-permute-done | bytes 786464 | tf_op jit(solution)/shard_map/ppermute | solution.py:24
  263.0 1.3 collective-permute-start.41
  264.2 1.2 add_convert_fusion.9
  267.0 2.3 collective-permute-done.42
  269.6 2.3 collective-permute-start.40
  271.9 1.4 collective-permute-start.43
  273.3 9.7 %collective-permute-done.44 = bf16[1,2,144,512]{3,2,1,0:T(8,128)(2,1)S(1)} collective-permute-done((bf16[1,2,144,512]{3,2,1,0:T(8,128)(2,1)S(1)}, bf16[1,2,144,512]{3,2,1,0:T(8,128)(2,1)S(1)}, u32[]{:S(2)}, u32[]{:S(2)}) %collective-permute-start.44) | collective-permute-done | bytes 294944 | tf_op jit(solution)/shard_map/ppermute | solution.py:24
  283.8 1.7 add_bitcast_fusion.1
  287.0 1.6 collective-permute-start.45
  289.3 3.5 %collective-permute-done.47 = bf16[1,1,144,512]{3,2,1,0:T(8,128)(2,1)S(1)} collective-permute-done((bf16[1,1,144,512]{3,2,1,0:T(8,128)(2,1)}, bf16[1,1,144,512]{3,2,1,0:T(8,128)(2,1)S(1)}, u32[]{:S(2)}, u32[]{:S(2)}) %collective-permute-start.47) | collective-permute-done | bytes 147488 | tf_op jit(solution)/shard_map/ppermute | solution.py:24
  296.3 1.0 maximum_select_fusion.2
  297.3 1.0 maximum_select_fusion.3
  (220 shorter events, 34.0 us)
Async XLA Ops:
  0.7 11.0 %collective-permute-start.3 = (s32[2,2,1024]{2,1,0:T(2,128)}, s32[2,2,1024]{2,1,0:T(2,128)S(1)}, u32[]{:S(2)}, u32[]{:S(2)}) collective-permute-start(s32[2,2,1024]{2,1,0:T(2,128)} %param.13), channel_id=1, source_target_pairs={{0,4},{4,0},{8,12},{12,8},{1,5},{5,1},{9,13},{13,9},{2,6},{6,2},{1... | collective-permute-start | bytes 49160 | tf_op jit(solution)/shard_map/ppermute | solution.py:24
  2.2 16.6 %collective-permute-start.9 = (bf16[128,4,64]{0,2,1:T(8,128)(2,1)S(1)}, bf16[128,4,64]{0,2,1:T(8,128)(2,1)S(1)}, u32[]{:S(2)}, u32[]{:S(2)}) collective-permute-start(bf16[128,4,64]{0,2,1:T(8,128)(2,1)S(1)} %pad_maximum_fusion.13), channel_id=1, source_target_pairs={{0,16},{1,17},{2,18},{3,19},{4,20},{5,21},{6,22},{7,23},{8,24},{9,... | collective-permute-start | bytes 196616 | tf_op jit(solution)/shard_map/ppermute | solution.py:32
  3.5 15.5 %collective-permute-start.12 = (bf16[128,512]{1,0:T(8,128)(2,1)}, bf16[128,512]{1,0:T(8,128)(2,1)S(1)}, u32[]{:S(2)}, u32[]{:S(2)}) collective-permute-start(bf16[128,512]{1,0:T(8,128)(2,1)} %bitcast.165), channel_id=1, source_target_pairs={{0,2},{1,3},{2,0},{3,1},{4,6},{5,7},{6,4},{7,5},{8,10},{9,11},{10,... | collective-permute-start | bytes 393224 | tf_op jit(solution)/shard_map/ppermute | solution.py:24
  8.8 10.2 %collective-permute-start.4 = (bf16[144,512]{1,0:T(8,128)(2,1)S(1)}, bf16[144,512]{1,0:T(8,128)(2,1)S(1)}, u32[]{:S(2)}, u32[]{:S(2)}) collective-permute-start(bf16[144,512]{1,0:T(8,128)(2,1)S(1)} %concatenate.116), channel_id=1, source_target_pairs={{0,2},{1,3},{2,0},{3,1},{4,6},{5,7},{6,4},{7,5},{8,10},{9,11},{10,... | collective-permute-start | bytes 442376 | tf_op jit(solution)/shard_map/ppermute | solution.py:24
  10.1 2.9 collective-permute-start
  11.7 21.4 %collective-permute-start.13 = (bf16[1,128,1024]{2,1,0:T(8,128)(2,1)S(1)}, bf16[1,128,1024]{2,1,0:T(8,128)(2,1)S(1)}, u32[]{:S(2)}, u32[]{:S(2)}) collective-permute-start(bf16[1,128,1024]{2,1,0:T(8,128)(2,1)S(1)} %maximum_bitcast_fusion), channel_id=1, source_target_pairs={{0,8},{4,12},{8,0},{12,4},{1,9},{5,13},{9,1},{13,5},{2,10},{6,14},... | collective-permute-start | bytes 786440 | tf_op jit(solution)/shard_map/ppermute | solution.py:24
  12.9 20.2 %collective-permute-start.2 = (bf16[2,128,512]{2,1,0:T(8,128)(2,1)S(1)}, bf16[2,128,512]{2,1,0:T(8,128)(2,1)S(1)}, u32[]{:S(2)}, u32[]{:S(2)}) collective-permute-start(bf16[2,128,512]{2,1,0:T(8,128)(2,1)S(1)} %get-tuple-element.213), channel_id=1, source_target_pairs={{0,4},{4,0},{8,12},{12,8},{1,5},{5,1},{9,13},{13,9},{2,6},{6,2},{1... | collective-permute-start | bytes 786440 | tf_op jit(solution)/shard_map/ppermute | solution.py:24
  14.2 18.8 %all-to-all-start = ((bf16[4,128,512]{2,1,0:T(8,128)(2,1)}), bf16[4,128,512]{2,1,0:T(8,128)(2,1)}, u32[]{:S(2)}, u32[]{:S(2)}) async-start(bf16[4,128,512]{2,1,0:T(8,128)(2,1)} %maximum_select_fusion), calls=%async_computation | async-start | bytes 1048576 | tf_op jit(solution)/shard_map/all_to_all | solution.py:632
  33.0 7.2 %collective-permute-start.5 = (bf16[2,144,512]{2,1,0:T(8,128)(2,1)S(1)}, bf16[2,144,512]{2,1,0:T(8,128)(2,1)S(1)}, u32[]{:S(2)}, u32[]{:S(2)}) collective-permute-start(bf16[2,144,512]{2,1,0:T(8,128)(2,1)S(1)} %pad_maximum_fusion.7), channel_id=1, source_target_pairs={{0,1},{1,0},{2,3},{3,2},{4,5},{5,4},{6,7},{7,6},{8,9},{9,8},{10,11... | collective-permute-start | bytes 884744 | tf_op jit(solution)/shard_map/ppermute | solution.py:24
  33.1 94.7 %copy-start = (bf16[2,128,1024]{2,1,0:T(8,128)(2,1)}, bf16[2,128,1024]{2,1,0:T(8,128)(2,1)S(1)}, u32[]{:S(2)}) copy-start(bf16[2,128,1024]{2,1,0:T(8,128)(2,1)S(1)} %pad_maximum_fusion.4.refs_0_.refs_2_) | copy-start | bytes 1572868
  34.0 15.5 %collective-permute-start.10 = (bf16[1,128,512]{2,1,0:T(8,128)(2,1)S(1)}, bf16[1,128,512]{2,1,0:T(8,128)(2,1)S(1)}, u32[]{:S(2)}, u32[]{:S(2)}) collective-permute-start(bf16[1,128,512]{2,1,0:T(8,128)(2,1)S(1)} %copy.70), channel_id=1, source_target_pairs={{16,24},{20,28},{24,16},{28,20},{17,25},{21,29},{25,17},{29,21},{1... | collective-permute-start | bytes 393224 | tf_op jit(solution)/shard_map/ppermute | solution.py:54
  40.9 16.1 %collective-permute-start.6 = (bf16[4,144,512]{2,1,0:T(8,128)(2,1)}, bf16[4,144,512]{2,1,0:T(8,128)(2,1)}, u32[]{:S(2)}, u32[]{:S(2)}) collective-permute-start(bf16[4,144,512]{2,1,0:T(8,128)(2,1)} %constant_dynamic-update-slice_fusion.refs_0_), channel_id=1, source_target_pairs={{0,8},{4,12},{8,0},{12,4},{1,9},{5,13},{9,1},{13,5},{2,10},{6,14},... | collective-permute-start | bytes 1769480 | tf_op jit(solution)/shard_map/ppermute | solution.py:24
  41.3 13.0 %collective-permute-start.14 = (bf16[2,128,512]{2,1,0:T(8,128)(2,1)S(1)}, bf16[2,128,512]{2,1,0:T(8,128)(2,1)S(1)}, u32[]{:S(2)}, u32[]{:S(2)}) collective-permute-start(bf16[2,128,512]{2,1,0:T(8,128)(2,1)S(1)} %pad_maximum_fusion.9), channel_id=1, source_target_pairs={{0,1},{1,0},{2,3},{3,2},{4,5},{5,4},{6,7},{7,6},{8,9},{9,8},{10,11... | collective-permute-start | bytes 786440 | tf_op jit(solution)/shard_map/ppermute | solution.py:24
  41.7 15.3 %collective-permute-start.15 = (bf16[2,128,512]{2,1,0:T(8,128)(2,1)S(1)}, bf16[2,128,512]{2,1,0:T(8,128)(2,1)S(1)}, u32[]{:S(2)}, u32[]{:S(2)}) collective-permute-start(bf16[2,128,512]{2,1,0:T(8,128)(2,1)S(1)} %get-tuple-element.211), channel_id=1, source_target_pairs={{0,2},{1,3},{2,0},{3,1},{4,6},{5,7},{6,4},{7,5},{8,10},{9,11},{10,... | collective-permute-start | bytes 786440 | tf_op jit(solution)/shard_map/ppermute | solution.py:24
  42.9 35.1 %collective-permute-start.1 = (bf16[512,512]{1,0:T(8,128)(2,1)}, bf16[512,512]{1,0:T(8,128)(2,1)}, u32[]{:S(2)}, u32[]{:S(2)}) collective-permute-start(bf16[512,512]{1,0:T(8,128)(2,1)} %bitcast.6.x_own), channel_id=1, source_target_pairs={{0,4},{4,0},{8,12},{12,8},{1,5},{5,1},{9,13},{13,9},{2,6},{6,2},{1... | collective-permute-start | bytes 1572872 | tf_op jit(solution)/shard_map/ppermute | solution.py:24
  46.0 32.0 %all-to-all-start.1 = ((bf16[4,128,512]{2,1,0:T(8,128)(2,1)}), bf16[4,128,512]{2,1,0:T(8,128)(2,1)S(1)}, u32[]{:S(2)}, u32[]{:S(2)}) async-start(bf16[4,128,512]{2,1,0:T(8,128)(2,1)} %maximum_select_fusion.1), calls=%async_computation.1 | async-start | bytes 1048576 | tf_op jit(solution)/shard_map/all_to_all | solution.py:633
  49.5 28.4 %collective-permute-start.11 = (bf16[2,128,512]{2,1,0:T(8,128)(2,1)S(1)}, bf16[2,128,512]{2,1,0:T(8,128)(2,1)S(1)}, u32[]{:S(2)}, u32[]{:S(2)}) collective-permute-start(bf16[2,128,512]{2,1,0:T(8,128)(2,1)S(1)} %constant_dynamic-update-slice_fusion.2), channel_id=1, source_target_pairs={{16,18},{17,19},{18,16},{19,17},{20,22},{21,23},{22,20},{23,21},{2... | collective-permute-start | bytes 786440 | tf_op jit(solution)/shard_map/ppermute | solution.py:54
  54.3 26.0 %collective-permute-start.7 = (bf16[4,144,512]{2,1,0:T(8,128)(2,1)}, bf16[4,144,512]{2,1,0:T(8,128)(2,1)}, u32[]{:S(2)}, u32[]{:S(2)}) collective-permute-start(bf16[4,144,512]{2,1,0:T(8,128)(2,1)} %constant_dynamic-update-slice_fusion.refs_0_), channel_id=1, source_target_pairs={{0,4},{4,0},{8,12},{12,8},{1,5},{5,1},{9,13},{13,9},{2,6},{6,2},{1... | collective-permute-start | bytes 1769480 | tf_op jit(solution)/shard_map/ppermute | solution.py:24
  57.0 70.8 %copy-start.3 = (bf16[3,128,512]{2,1,0:T(8,128)(2,1)}, bf16[3,128,512]{2,1,0:T(8,128)(2,1)S(1)}, u32[]{:S(2)}) copy-start(bf16[3,128,512]{2,1,0:T(8,128)(2,1)S(1)} %pad_maximum_fusion.6.refs_2_.refs_4_) | copy-start | bytes 1179652
  57.0 22.2 %collective-permute-start.16 = (bf16[2,2,128,512]{3,2,1,0:T(8,128)(2,1)S(1)}, bf16[2,2,128,512]{3,2,1,0:T(8,128)(2,1)}, u32[]{:S(2)}, u32[]{:S(2)}) collective-permute-start(bf16[2,2,128,512]{3,2,1,0:T(8,128)(2,1)S(1)} %pad_maximum_fusion.5), channel_id=1, source_target_pairs={{0,1},{1,0},{2,3},{3,2},{4,5},{5,4},{6,7},{7,6},{8,9},{9,8},{10,11... | collective-permute-start | bytes 1572872 | tf_op jit(solution)/shard_map/ppermute | solution.py:24
  57.1 23.2 %collective-permute-start.8 = (bf16[4,144,512]{2,1,0:T(8,128)(2,1)}, bf16[4,144,512]{2,1,0:T(8,128)(2,1)}, u32[]{:S(2)}, u32[]{:S(2)}) collective-permute-start(bf16[4,144,512]{2,1,0:T(8,128)(2,1)} %collective-permute-done.6.refs_1_), channel_id=1, source_target_pairs={{0,4},{4,0},{8,12},{12,8},{1,5},{5,1},{9,13},{13,9},{2,6},{6,2},{1... | collective-permute-start | bytes 1769480 | tf_op jit(solution)/shard_map/ppermute | solution.py:24
  78.0 49.7 %copy-start.2 = (bf16[4,128,512]{2,1,0:T(8,128)(2,1)}, bf16[4,128,512]{2,1,0:T(8,128)(2,1)S(1)}, u32[]{:S(2)}) copy-start(bf16[4,128,512]{2,1,0:T(8,128)(2,1)S(1)} %all-to-all-done.1) | copy-start | bytes 1572868
  78.1 15.6 %collective-permute-start.17 = (bf16[3,128,512]{2,1,0:T(8,128)(2,1)S(1)}, bf16[3,128,512]{2,1,0:T(8,128)(2,1)S(1)}, u32[]{:S(2)}, u32[]{:S(2)}) collective-permute-start(bf16[3,128,512]{2,1,0:T(8,128)(2,1)S(1)} %pad_maximum_fusion.6.refs_2_.refs_4_), channel_id=1, source_target_pairs={{0,8},{4,12},{8,0},{12,4},{1,9},{5,13},{9,1},{13,5},{2,10},{6,14},... | collective-permute-start | bytes 1179656 | tf_op jit(solution)/shard_map/ppermute | solution.py:24
  80.3 47.4 %copy-start.1 = (bf16[3,2,128,512]{3,2,1,0:T(8,128)(2,1)}, bf16[3,2,128,512]{3,2,1,0:T(8,128)(2,1)S(1)}, u32[]{:S(2)}) copy-start(bf16[3,2,128,512]{3,2,1,0:T(8,128)(2,1)S(1)} %pad_maximum_fusion.1.refs_1_.refs_3_) | copy-start | bytes 2359300
  80.3 19.2 %copy-start.4 = (s32[3]{0:T(128)S(1)}, s32[3]{0:T(128)}, u32[]{:S(2)}) copy-start(s32[3]{0:T(128)} %pad_add_fusion.ints) | copy-start | bytes 40
  93.7 34.0 %copy-start.7 = (bf16[3,128,512]{2,1,0:T(8,128)(2,1)}, bf16[3,128,512]{2,1,0:T(8,128)(2,1)S(1)}, u32[]{:S(2)}) copy-start(bf16[3,128,512]{2,1,0:T(8,128)(2,1)S(1)} %collective-permute-done.17.refs_3_.refs_5_) | copy-start | bytes 1179652
  93.7 5.8 %collective-permute-start.19 = (bf16[3,2,128,512]{3,2,1,0:T(8,128)(2,1)S(1)}, bf16[3,2,128,512]{3,2,1,0:T(8,128)(2,1)S(1)}, u32[]{:S(2)}, u32[]{:S(2)}) collective-permute-start(bf16[3,2,128,512]{3,2,1,0:T(8,128)(2,1)S(1)} %pad_maximum_fusion.1.refs_1_.refs_3_), channel_id=1, source_target_pairs={{0,4},{4,0},{8,12},{12,8},{1,5},{5,1},{9,13},{13,9},{2,6},{6,2},{1... | collective-permute-start | bytes 2359304 | tf_op jit(solution)/shard_map/ppermute | solution.py:24
  95.7 3.8 %collective-permute-start.18 = (bf16[2,128,1024]{2,1,0:T(8,128)(2,1)S(1)}, bf16[2,128,1024]{2,1,0:T(8,128)(2,1)S(1)}, u32[]{:S(2)}, u32[]{:S(2)}) collective-permute-start(bf16[2,128,1024]{2,1,0:T(8,128)(2,1)S(1)} %pad_maximum_fusion.4.refs_0_.refs_2_), channel_id=1, source_target_pairs={{0,4},{4,0},{8,12},{12,8},{1,5},{5,1},{9,13},{13,9},{2,6},{6,2},{1... | collective-permute-start | bytes 1572872 | tf_op jit(solution)/shard_map/ppermute | solution.py:24
  95.8 3.1 %collective-permute-start.20 = (bf16[3,128,512]{2,1,0:T(8,128)(2,1)S(1)}, bf16[3,128,512]{2,1,0:T(8,128)(2,1)S(1)}, u32[]{:S(2)}, u32[]{:S(2)}) collective-permute-start(bf16[3,128,512]{2,1,0:T(8,128)(2,1)S(1)} %pad_maximum_fusion.6.refs_2_.refs_4_), channel_id=1, source_target_pairs={{0,4},{4,0},{8,12},{12,8},{1,5},{5,1},{9,13},{13,9},{2,6},{6,2},{1... | collective-permute-start | bytes 1179656 | tf_op jit(solution)/shard_map/ppermute | solution.py:24
  96.2 3.3 %collective-permute-start.21 = (bf16[3,128,512]{2,1,0:T(8,128)(2,1)S(1)}, bf16[3,128,512]{2,1,0:T(8,128)(2,1)S(1)}, u32[]{:S(2)}, u32[]{:S(2)}) collective-permute-start(bf16[3,128,512]{2,1,0:T(8,128)(2,1)S(1)} %collective-permute-done.17.refs_3_.refs_5_), channel_id=1, source_target_pairs={{0,4},{4,0},{8,12},{12,8},{1,5},{5,1},{9,13},{13,9},{2,6},{6,2},{1... | collective-permute-start | bytes 1179656 | tf_op jit(solution)/shard_map/ppermute | solution.py:24
  96.3 14.9 %collective-permute-start.24 = (bf16[2,2,128,512]{3,2,1,0:T(8,128)(2,1)S(1)}, bf16[2,2,128,512]{3,2,1,0:T(8,128)(2,1)S(1)}, u32[]{:S(2)}, u32[]{:S(2)}) collective-permute-start(bf16[2,2,128,512]{3,2,1,0:T(8,128)(2,1)S(1)} %pad_maximum_fusion.3), channel_id=1, source_target_pairs={{16,17},{17,16},{18,19},{19,18},{20,21},{21,20},{22,23},{23,22},{2... | collective-permute-start | bytes 1572872 | tf_op jit(solution)/shard_map/ppermute | solution.py:54
  98.9 28.8 %copy-start.8 = (bf16[3,128,512]{2,1,0:T(8,128)(2,1)}, bf16[3,128,512]{2,1,0:T(8,128)(2,1)S(1)}, u32[]{:S(2)}) copy-start(bf16[3,128,512]{2,1,0:T(8,128)(2,1)S(1)} %collective-permute-done.20.refs_6_.refs_8_) | copy-start | bytes 1179652
  99.5 28.3 %copy-start.9 = (bf16[3,128,512]{2,1,0:T(8,128)(2,1)}, bf16[3,128,512]{2,1,0:T(8,128)(2,1)S(1)}, u32[]{:S(2)}) copy-start(bf16[3,128,512]{2,1,0:T(8,128)(2,1)S(1)} %collective-permute-done.21.refs_7_.refs_9_) | copy-start | bytes 1179652
  99.5 28.3 %copy-start.6 = (bf16[2,128,1024]{2,1,0:T(8,128)(2,1)}, bf16[2,128,1024]{2,1,0:T(8,128)(2,1)S(1)}, u32[]{:S(2)}) copy-start(bf16[2,128,1024]{2,1,0:T(8,128)(2,1)S(1)} %collective-permute-done.18.refs_4_.refs_6_) | copy-start | bytes 1572868
  99.5 28.3 %copy-start.5 = (bf16[3,2,128,512]{3,2,1,0:T(8,128)(2,1)}, bf16[3,2,128,512]{3,2,1,0:T(8,128)(2,1)S(1)}, u32[]{:S(2)}) copy-start(bf16[3,2,128,512]{3,2,1,0:T(8,128)(2,1)S(1)} %collective-permute-done.19.refs_5_.refs_7_) | copy-start | bytes 2359300
  104.8 22.9 %copy-start.11 = (bf16[4,512,512]{2,1,0:T(8,128)(2,1)}, bf16[4,512,512]{2,1,0:T(8,128)(2,1)S(1)}, u32[]{:S(2)}) copy-start(bf16[4,512,512]{2,1,0:T(8,128)(2,1)S(1)} %get-tuple-element.111.hidden_in) | copy-start | bytes 6291460
  104.8 17.1 %collective-permute-start.22 = (bf16[512,512]{1,0:T(8,128)(2,1)S(1)}, bf16[512,512]{1,0:T(8,128)(2,1)S(1)}, u32[]{:S(2)}, u32[]{:S(2)}) collective-permute-start(bf16[512,512]{1,0:T(8,128)(2,1)S(1)} %get-tuple-element.105), channel_id=1, source_target_pairs={{0,16},{1,17},{2,18},{3,19},{4,20},{5,21},{6,22},{7,23},{8,24},{9,... | collective-permute-start | bytes 1572872 | tf_op jit(solution)/shard_map/ppermute | solution.py:32
  121.9 5.8 %collective-permute-start.25 = (bf16[4,2,128,512]{3,2,1,0:T(8,128)(2,1)S(1)}, bf16[4,2,128,512]{3,2,1,0:T(8,128)(2,1)S(1)}, u32[]{:S(2)}, u32[]{:S(2)}) collective-permute-start(bf16[4,2,128,512]{3,2,1,0:T(8,128)(2,1)S(1)} %pad_maximum_fusion.refs_0_), channel_id=1, source_target_pairs={{16,20},{20,16},{24,28},{28,24},{17,21},{21,17},{25,29},{29,25},{1... | collective-permute-start | bytes 3145736 | tf_op jit(solution)/shard_map/ppermute | solution.py:54
  124.7 3.0 %collective-permute-start.23 = (bf16[512,512]{1,0:T(8,128)(2,1)S(1)}, bf16[512,512]{1,0:T(8,128)(2,1)S(1)}, u32[]{:S(2)}, u32[]{:S(2)}) collective-permute-start(bf16[512,512]{1,0:T(8,128)(2,1)S(1)} %collective-permute-done.22.mem_own), channel_id=1, source_target_pairs={{0,4},{4,0},{8,12},{12,8},{1,5},{5,1},{9,13},{13,9},{2,6},{6,2},{1... | collective-permute-start | bytes 1572872 | tf_op jit(solution)/shard_map/ppermute | solution.py:24
  166.7 17.5 %copy-start.15 = (f32[4,512]{1,0:T(4,128)}, f32[4,512]{1,0:T(4,128)S(1)}, u32[]{:S(2)}) copy-start(f32[4,512]{1,0:T(4,128)S(1)} %get-tuple-element.113.small_in) | copy-start | bytes 24580
  166.7 2.0 collective-permute-start.26
  168.8 12.5 %collective-permute-start.27 = (bf16[512,512]{1,0:T(8,128)(2,1)S(1)}, bf16[512,512]{1,0:T(8,128)(2,1)S(1)}, u32[]{:S(2)}, u32[]{:S(2)}) collective-permute-start(bf16[512,512]{1,0:T(8,128)(2,1)S(1)} %add_convert_fusion.8), channel_id=1, source_target_pairs={{16,0},{17,1},{18,2},{19,3},{20,4},{21,5},{22,6},{23,7},{24,8},{25... | collective-permute-start | bytes 1572872 | tf_op jit(solution)/shard_map/ppermute | solution.py:32
  181.3 5.3 %collective-permute-start.30 = (bf16[2,4,128,512]{3,2,1,0:T(8,128)(2,1)}, bf16[2,4,128,512]{3,2,1,0:T(8,128)(2,1)S(1)}, u32[]{:S(2)}, u32[]{:S(2)}) collective-permute-start(bf16[2,4,128,512]{3,2,1,0:T(8,128)(2,1)} %get-tuple-element.124), channel_id=1, source_target_pairs={{16,20},{20,16},{24,28},{28,24},{17,21},{21,17},{25,29},{29,25},{1... | collective-permute-start | bytes 3145736 | tf_op jit(solution)/shard_map/ppermute | solution.py:54
  186.1 9.0 %collective-permute-start.28 = (bf16[2,4,128,512]{3,2,1,0:T(8,128)(2,1)}, bf16[2,4,128,512]{3,2,1,0:T(8,128)(2,1)S(1)}, u32[]{:S(2)}, u32[]{:S(2)}) collective-permute-start(bf16[2,4,128,512]{3,2,1,0:T(8,128)(2,1)} %get-tuple-element.120), channel_id=1, source_target_pairs={{0,4},{4,0},{8,12},{12,8},{1,5},{5,1},{9,13},{13,9},{2,6},{6,2},{1... | collective-permute-start | bytes 3145736 | tf_op jit(solution)/shard_map/ppermute | solution.py:24
  186.1 8.9 %collective-permute-start.29 = (bf16[2,4,128,512]{3,2,1,0:T(8,128)(2,1)}, bf16[2,4,128,512]{3,2,1,0:T(8,128)(2,1)}, u32[]{:S(2)}, u32[]{:S(2)}) collective-permute-start(bf16[2,4,128,512]{3,2,1,0:T(8,128)(2,1)} %get-tuple-element.121), channel_id=1, source_target_pairs={{0,4},{4,0},{8,12},{12,8},{1,5},{5,1},{9,13},{13,9},{2,6},{6,2},{1... | collective-permute-start | bytes 3145736 | tf_op jit(solution)/shard_map/ppermute | solution.py:24
  187.7 15.3 %collective-permute-start.31 = (bf16[1,4,128,512]{3,2,1,0:T(8,128)(2,1)}, bf16[1,4,128,512]{3,2,1,0:T(8,128)(2,1)S(1)}, u32[]{:S(2)}, u32[]{:S(2)}) collective-permute-start(bf16[1,4,128,512]{3,2,1,0:T(8,128)(2,1)} %get-tuple-element.195), channel_id=1, source_target_pairs={{16,24},{20,28},{24,16},{28,20},{17,25},{21,29},{25,17},{29,21},{1... | collective-permute-start | bytes 1572872 | tf_op jit(solution)/shard_map/ppermute | solution.py:54
  191.6 41.9 %all-to-all-start.2 = ((bf16[4,128,512]{2,1,0:T(8,128)(2,1)}), bf16[4,128,512]{2,1,0:T(8,128)(2,1)S(1)}, u32[]{:S(2)}, u32[]{:S(2)}) async-start(bf16[4,128,512]{2,1,0:T(8,128)(2,1)} %bitcast.35), calls=%async_computation.2 | async-start | bytes 1048576 | tf_op jit(solution)/shard_map/all_to_all | solution.py:112
  203.8 29.7 %collective-permute-start.34 = (bf16[1,2,128,512]{3,2,1,0:T(8,128)(2,1)}, bf16[1,2,128,512]{3,2,1,0:T(8,128)(2,1)}, u32[]{:S(2)}, u32[]{:S(2)}) collective-permute-start(bf16[1,2,128,512]{3,2,1,0:T(8,128)(2,1)} %get-tuple-element.203), channel_id=1, source_target_pairs={{16,17},{17,16},{18,19},{19,18},{20,21},{21,20},{22,23},{23,22},{2... | collective-permute-start | bytes 786440 | tf_op jit(solution)/shard_map/ppermute | solution.py:54
  208.9 24.6 %collective-permute-start.33 = (bf16[2,2,128,512]{3,2,1,0:T(8,128)(2,1)}, bf16[2,2,128,512]{3,2,1,0:T(8,128)(2,1)}, u32[]{:S(2)}, u32[]{:S(2)}) collective-permute-start(bf16[2,2,128,512]{3,2,1,0:T(8,128)(2,1)} %get-tuple-element.193), channel_id=1, source_target_pairs={{0,1},{1,0},{2,3},{3,2},{4,5},{5,4},{6,7},{7,6},{8,9},{9,8},{10,11... | collective-permute-start | bytes 1572872 | tf_op jit(solution)/shard_map/ppermute | solution.py:24
  211.2 22.4 %collective-permute-start.32 = (bf16[1,4,128,512]{3,2,1,0:T(8,128)(2,1)}, bf16[1,4,128,512]{3,2,1,0:T(8,128)(2,1)S(1)}, u32[]{:S(2)}, u32[]{:S(2)}) collective-permute-start(bf16[1,4,128,512]{3,2,1,0:T(8,128)(2,1)} %get-tuple-element.196), channel_id=1, source_target_pairs={{0,8},{4,12},{8,0},{12,4},{1,9},{5,13},{9,1},{13,5},{2,10},{6,14},... | collective-permute-start | bytes 1572872 | tf_op jit(solution)/shard_map/ppermute | solution.py:24
  233.5 4.6 %collective-permute-start.35 = (bf16[2,4,128,512]{3,2,1,0:T(8,128)(2,1)}, bf16[2,4,128,512]{3,2,1,0:T(8,128)(2,1)S(1)}, u32[]{:S(2)}, u32[]{:S(2)}) collective-permute-start(bf16[2,4,128,512]{3,2,1,0:T(8,128)(2,1)} %get-tuple-element.145), channel_id=1, source_target_pairs={{0,4},{4,0},{8,12},{12,8},{1,5},{5,1},{9,13},{13,9},{2,6},{6,2},{1... | collective-permute-start | bytes 3145736 | tf_op jit(solution)/shard_map/ppermute | solution.py:24
  235.6 12.0 %collective-permute-start.36 = (bf16[512,512]{1,0:T(8,128)(2,1)}, bf16[512,512]{1,0:T(8,128)(2,1)S(1)}, u32[]{:S(2)}, u32[]{:S(2)}) collective-permute-start(bf16[512,512]{1,0:T(8,128)(2,1)} %get-tuple-element.152), channel_id=1, source_target_pairs={{0,4},{4,0},{8,12},{12,8},{1,5},{5,1},{9,13},{13,9},{2,6},{6,2},{1... | collective-permute-start | bytes 1572872 | tf_op jit(solution)/shard_map/ppermute | solution.py:24
  241.8 19.1 %collective-permute-start.37 = (bf16[1,6,128,512]{3,2,1,0:T(8,128)(2,1)}, bf16[1,6,128,512]{3,2,1,0:T(8,128)(2,1)}, u32[]{:S(2)}, u32[]{:S(2)}) collective-permute-start(bf16[1,6,128,512]{3,2,1,0:T(8,128)(2,1)} %pad_maximum_fusion.2), channel_id=1, source_target_pairs={{0,8},{4,12},{8,0},{12,4},{1,9},{5,13},{9,1},{13,5},{2,10},{6,14},... | collective-permute-start | bytes 2359304 | tf_op jit(solution)/shard_map/ppermute | solution.py:24
  243.1 12.2 %collective-permute-start.39 = (bf16[1,1,128,512]{3,2,1,0:T(8,128)(2,1)S(1)}, bf16[1,1,128,512]{3,2,1,0:T(8,128)(2,1)S(1)}, u32[]{:S(2)}, u32[]{:S(2)}) collective-permute-start(bf16[1,1,128,512]{3,2,1,0:T(8,128)(2,1)S(1)} %add_convert_fusion.24), channel_id=1, source_target_pairs={{16,18},{17,19},{18,16},{19,17},{20,22},{21,23},{22,20},{23,21},{2... | collective-permute-start | bytes 393224 | tf_op jit(solution)/shard_map/ppermute | solution.py:54
  245.8 10.3 %collective-permute-start.38 = (bf16[1,2,128,512]{3,2,1,0:T(8,128)(2,1)S(1)}, bf16[1,2,128,512]{3,2,1,0:T(8,128)(2,1)S(1)}, u32[]{:S(2)}, u32[]{:S(2)}) collective-permute-start(bf16[1,2,128,512]{3,2,1,0:T(8,128)(2,1)S(1)} %get-tuple-element.201), channel_id=1, source_target_pairs={{0,1},{1,0},{2,3},{3,2},{4,5},{5,4},{6,7},{7,6},{8,9},{9,8},{10,11... | collective-permute-start | bytes 786440 | tf_op jit(solution)/shard_map/ppermute | solution.py:24
  251.8 31.9 %all-to-all-start.3 = ((bf16[4,128,512]{2,1,0:T(8,128)(2,1)}), bf16[4,128,512]{2,1,0:T(8,128)(2,1)S(1)}, u32[]{:S(2)}, u32[]{:S(2)}) async-start(bf16[4,128,512]{2,1,0:T(8,128)(2,1)} %bitcast.160), calls=%async_computation.3 | async-start | bytes 1048576 | tf_op jit(solution)/shard_map/all_to_all | solution.py:112
  263.0 3.4 %collective-permute-start.41 = (f32[2,4,6,32]{3,2,1,0:T(8,128)S(1)}, f32[2,4,6,32]{3,2,1,0:T(8,128)S(1)}, u32[]{:S(2)}, u32[]{:S(2)}) collective-permute-start(f32[2,4,6,32]{3,2,1,0:T(8,128)S(1)} %pad_maximum_fusion.15), channel_id=1, source_target_pairs={{0,4},{4,0},{8,12},{12,8},{1,5},{5,1},{9,13},{13,9},{2,6},{6,2},{1... | collective-permute-start | bytes 18440 | tf_op jit(solution)/shard_map/ppermute | solution.py:24
  266.4 2.9 collective-permute-start.42
  269.5 13.6 %collective-permute-start.44 = (bf16[1,2,144,512]{3,2,1,0:T(8,128)(2,1)S(1)}, bf16[1,2,144,512]{3,2,1,0:T(8,128)(2,1)S(1)}, u32[]{:S(2)}, u32[]{:S(2)}) collective-permute-start(bf16[1,2,144,512]{3,2,1,0:T(8,128)(2,1)S(1)} %pad_maximum_fusion.8), channel_id=1, source_target_pairs={{0,1},{1,0},{2,3},{3,2},{4,5},{5,4},{6,7},{7,6},{8,9},{9,8},{10,11... | collective-permute-start | bytes 884744 | tf_op jit(solution)/shard_map/ppermute | solution.py:24
  269.6 14.2 %collective-permute-start.40 = (bf16[1,2,128,512]{3,2,1,0:T(8,128)(2,1)S(1)}, bf16[1,2,128,512]{3,2,1,0:T(8,128)(2,1)S(1)}, u32[]{:S(2)}, u32[]{:S(2)}) collective-permute-start(bf16[1,2,128,512]{3,2,1,0:T(8,128)(2,1)S(1)} %pad_maximum_fusion.10), channel_id=1, source_target_pairs={{0,2},{1,3},{2,0},{3,1},{4,6},{5,7},{6,4},{7,5},{8,10},{9,11},{10,... | collective-permute-start | bytes 786440 | tf_op jit(solution)/shard_map/ppermute | solution.py:24
  271.9 11.8 %collective-permute-start.43 = (bf16[128,4,64]{0,2,1:T(8,128)(2,1)S(1)}, bf16[128,4,64]{0,2,1:T(8,128)(2,1)S(1)}, u32[]{:S(2)}, u32[]{:S(2)}) collective-permute-start(bf16[128,4,64]{0,2,1:T(8,128)(2,1)S(1)} %fusion.3), channel_id=1, source_target_pairs={{16,0},{17,1},{18,2},{19,3},{20,4},{21,5},{22,6},{23,7},{24,8},{25... | collective-permute-start | bytes 196616 | tf_op jit(solution)/shard_map/ppermute | solution.py:32
  283.7 9.1 %collective-permute-start.47 = (bf16[1,1,144,512]{3,2,1,0:T(8,128)(2,1)}, bf16[1,1,144,512]{3,2,1,0:T(8,128)(2,1)S(1)}, u32[]{:S(2)}, u32[]{:S(2)}) collective-permute-start(bf16[1,1,144,512]{3,2,1,0:T(8,128)(2,1)} %add_convert_fusion.18), channel_id=1, source_target_pairs={{0,2},{1,3},{2,0},{3,1},{4,6},{5,7},{6,4},{7,5},{8,10},{9,11},{10,... | collective-permute-start | bytes 442376 | tf_op jit(solution)/shard_map/ppermute | solution.py:24
  287.0 9.3 %collective-permute-start.45 = (bf16[2,128,512]{2,1,0:T(8,128)(2,1)S(1)}, bf16[2,128,512]{2,1,0:T(8,128)(2,1)S(1)}, u32[]{:S(2)}, u32[]{:S(2)}) collective-permute-start(bf16[2,128,512]{2,1,0:T(8,128)(2,1)S(1)} %get-tuple-element.209), channel_id=1, source_target_pairs={{0,4},{4,0},{8,12},{12,8},{1,5},{5,1},{9,13},{13,9},{2,6},{6,2},{1... | collective-permute-start | bytes 786440 | tf_op jit(solution)/shard_map/ppermute | solution.py:24
  288.6 8.8 %collective-permute-start.46 = (bf16[2,128,512]{2,1,0:T(8,128)(2,1)S(1)}, bf16[2,128,512]{2,1,0:T(8,128)(2,1)S(1)}, u32[]{:S(2)}, u32[]{:S(2)}) collective-permute-start(bf16[2,128,512]{2,1,0:T(8,128)(2,1)S(1)} %get-tuple-element.207), channel_id=1, source_target_pairs={{0,4},{4,0},{8,12},{12,8},{1,5},{5,1},{9,13},{13,9},{2,6},{6,2},{1... | collective-permute-start | bytes 786440 | tf_op jit(solution)/shard_map/ppermute | solution.py:24
  (20 other events, 120.3 us)

commit v2 on v1

--- a/solution.py
+++ b/solution.py
@@ -637,11 +637,11 @@
     for bit in bits:
         own3 = jnp.concatenate([own3, decoder_swap(own3, "dp", bit)])
     w1 = doubled([(all1, 0)], bits)
-    up_pair, own2 = after((up_pair, own2), all1)
+    up_pair, own2 = after(up_pair, all1), after(own2, x_own)
     up_rest = jnp.concatenate([up_pair[1:], swap(up_pair, "mp", 1)])
     down_own = own2[:, :, unit:]
     down_pair = jnp.stack([down_own, swap(down_own, "mp", 2)])
-    up_rest, down_pair = after((up_rest, down_pair), *[w for w, _ in w1])
+    w1 = [(after(w, up_rest), a) for w, a in w1]
     w1 = doubled(w1, core_bit)
     x_other = swap(x_own, "dp", 1)
 
@@ -689,7 +689,6 @@
 
     state, state_low = ((half, width), F32, AN), ((half, width), BF, AN)
 
-    x_other, cots = together(x_other, cots)
     up_rests = doubled([(up_rest, 0)], bits)
     down_rest = jnp.concatenate([down_pair[1:], swap(down_pair, "mp", 1)])
     pair3 = jnp.stack([own3, decoder_swap(own3, "mp", 2)])
@@ -704,7 +703,9 @@
         + [dma((count,)), dma((3,)), dma((ways + 2, 4)), dma((count,))],
         5 << 30,
     )
-    mid, pair3, own2, down_rest, *arrays = together(mid, pair3, own2, down_rest, *[w for w, _ in up_rests])
+    mid, cots, pair3, own2, down_rest, *arrays = together(
+        mid, cots, pair3, own2, down_rest, *[w for w, _ in up_rests]
+    )
     up_rests = [(w, a) for w, (_, a) in zip(arrays, up_rests)]
     weights2 = [w for w, _ in doubled([(own2, 0), (down_rest, 0)] + up_rests, core_bit)]
     pieces2 = []

time: 303 us -> 304 us (level)
  other arithmetic: 26.8 us -> 30 us
    ppermute x36, waiting for transfers between devices: 32.3 us -> 48.3 us  [swap(): return lax.ppermute(block, axis, [(i, i ^ bit) for i in range(count)])]
    ppermute x8, waiting for transfers between devices: 28.1 us -> 14.1 us  [decoder_swap(): return lax.ppermute(block, ('section', axis), pairs)]
    ppermute x36, starting transfers between devices: 35.3 us -> 31.8 us  [swap(): return lax.ppermute(block, axis, [(i, i ^ bit) for i in range(count)])]
    ppermute x4, waiting for transfers between devices: 21.8 us -> 18.6 us  [oneway(): return lax.ppermute(block, axis, [(source, target)])]
    unnamed x73 -> x77, local copies, waits for them, and re-layouts: 12 us -> 12 us
  transfers between devices with their start and end apart: 52 -> 52, of which waited for: 17 -> 21; matrix products, arithmetic and copies ran while one was open for 12% -> 14% of each run, Pallas kernels for 14% -> 14%
where the time goes in v2:
time: 304 us; the launch traced here: 298 us
  waiting for transfers between devices  94.6 us (31%)
  Pallas kernels  78.6 us (26%)
  starting transfers between devices  75.9 us (25%)
  other arithmetic  30 us (10%)
  local copies, waits for them, and re-layouts  17 us (6%)
    pallas_call x6, Pallas kernels, call(): pl.pallas_call(kernel, name=name, in_specs=[spec for _, spec in ins], out...  78.6 us
    ppermute x36, waiting for transfers between devices, swap(): return lax.ppermute(block, axis, [(i, i ^ bit) for i in range(count)])  48.3 us
    ppermute x36, starting transfers between devices, swap(): return lax.ppermute(block, axis, [(i, i ^ bit) for i in range(count)])  31.8 us
    ppermute x8, starting transfers between devices, decoder_swap(): return lax.ppermute(block, ('section', axis), pairs)  21.7 us
    ppermute x4, waiting for transfers between devices, oneway(): return lax.ppermute(block, axis, [(source, target)])  18.6 us
    ppermute x8, waiting for transfers between devices, decoder_swap(): return lax.ppermute(block, ('section', axis), pairs)  14.1 us
    all_to_all x1, waiting for transfers between devices, on_device(): lax.all_to_all(rows_in(layer_in[0]), 'mp', 0, 0, tiled=True)  13.6 us
    convert_element_type x13, other arithmetic, add(): return (a.astype(F32) + b.astype(F32)).astype(BF)  12.4 us
  transfers between devices with their start and end apart: 52, of which 21 were waited for; matrix products, arithmetic and copies ran while one was open for 14% of the time, Pallas kernels for 14%

profile of v2, /device:TPU:3, one launch (start us, length us, event | category | flops | bytes accessed | tf_op | source)
XLA Modules:
  0.0 298.0 jit_solution(18158966467949800389)
XLA Ops:
  2.2 1.3 collective-permute-start.11
  3.5 2.4 collective-permute-start.5
  10.9 1.3 collective-permute-start.14
  14.6 1.1 collective-permute-done
  17.0 4.6 %all-to-all-start = ((bf16[4,128,512]{2,1,0:T(8,128)(2,1)}), bf16[4,128,512]{2,1,0:T(8,128)(2,1)}, u32[]{:S(2)}, u32[]{:S(2)}) async-start(bf16[4,128,512]{2,1,0:T(8,128)(2,1)} %maximum_select_fusion), calls=%async_computation | async-start | bytes 1048576 | tf_op jit(solution)/shard_map/all_to_all | solution.py:632
  22.2 13.6 %all-to-all-done = bf16[4,128,512]{2,1,0:T(8,128)(2,1)} async-done(((bf16[4,128,512]{2,1,0:T(8,128)(2,1)}), bf16[4,128,512]{2,1,0:T(8,128)(2,1)}, u32[]{:S(2)}, u32[]{:S(2)}) %all-to-all-start) | async-done | bytes 524320 | tf_op jit(solution)/shard_map/all_to_all | solution.py:632
  36.6 2.1 collective-permute-start.12
  38.8 1.5 collective-permute-start.15
  40.3 4.5 %collective-permute-done.4 = bf16[2,144,512]{2,1,0:T(8,128)(2,1)S(1)} collective-permute-done((bf16[2,144,512]{2,1,0:T(8,128)(2,1)S(1)}, bf16[2,144,512]{2,1,0:T(8,128)(2,1)S(1)}, u32[]{:S(2)}, u32[]{:S(2)}) %collective-permute-start.4) | collective-permute-done | bytes 294944 | tf_op jit(solution)/shard_map/ppermute | solution.py:24
  45.7 2.7 collective-permute-start.1
  48.4 3.6 %collective-permute-done.15 = bf16[2,128,512]{2,1,0:T(8,128)(2,1)S(1)} collective-permute-done((bf16[2,128,512]{2,1,0:T(8,128)(2,1)S(1)}, bf16[2,128,512]{2,1,0:T(8,128)(2,1)S(1)}, u32[]{:S(2)}, u32[]{:S(2)}) %collective-permute-start.15) | collective-permute-done | bytes 262176 | tf_op jit(solution)/shard_map/ppermute | solution.py:24
  52.1 1.9 collective-permute-start.13
  54.1 1.6 collective-permute-done.6
  55.7 2.4 collective-permute-done.7.refs_1_
  58.1 3.5 %collective-permute-start.8 = (bf16[4,144,512]{2,1,0:T(8,128)(2,1)}, bf16[4,144,512]{2,1,0:T(8,128)(2,1)}, u32[]{:S(2)}, u32[]{:S(2)}) collective-permute-start(bf16[4,144,512]{2,1,0:T(8,128)(2,1)} %constant_dynamic-update-slice_fusion.refs_0_), channel_id=1, source_target_pairs={{0,4},{4,0},{8,12},{12,8},{1,5},{5,1},{9,13},{13,9},{2,6},{6,2},{1... | collective-permute-start | bytes 1769480 | tf_op jit(solution)/shard_map/ppermute | solution.py:24
  61.6 1.9 maximum_select_fusion.1
  63.5 4.0 %all-to-all-start.1 = ((bf16[4,128,512]{2,1,0:T(8,128)(2,1)}), bf16[4,128,512]{2,1,0:T(8,128)(2,1)S(1)}, u32[]{:S(2)}, u32[]{:S(2)}) async-start(bf16[4,128,512]{2,1,0:T(8,128)(2,1)} %maximum_select_fusion.1), calls=%async_computation.1 | async-start | bytes 1048576 | tf_op jit(solution)/shard_map/all_to_all | solution.py:633
  68.3 1.8 pad_maximum_fusion.3
  70.6 6.0 %collective-permute-done.16 = bf16[2,2,128,512]{3,2,1,0:T(8,128)(2,1)} collective-permute-done((bf16[2,2,128,512]{3,2,1,0:T(8,128)(2,1)S(1)}, bf16[2,2,128,512]{3,2,1,0:T(8,128)(2,1)}, u32[]{:S(2)}, u32[]{:S(2)}) %collective-permute-start.16) | collective-permute-done | bytes 524320 | tf_op jit(solution)/shard_map/ppermute | solution.py:24
  76.6 1.1 pad_maximum_fusion.1.refs_1_.refs_3_
  77.8 13.3 %self_fwd.1 = (bf16[4,512,128]{2,1,0:T(8,128)(2,1)}, bf16[4,1024,128]{2,1,0:T(8,128)(2,1)}, bf16[4,1024,128]{2,1,0:T(8,128)(2,1)}, f32[4,512,128]{2,1,0:T(8,128)...) custom-call(s32[3]{0:T(128)} %pad_add_fusion.ints, ...), custom_call_target="tpu_custom_call" | custom-call | flops 5368709120 | bytes 8388608 | tf_op jit(solution)/shard_map/self_fwd/pallas_call | solution.py:585
  91.1 4.9 %collective-permute-start.19 = (bf16[3,2,128,512]{3,2,1,0:T(8,128)(2,1)S(1)}, bf16[3,2,128,512]{3,2,1,0:T(8,128)(2,1)S(1)}, u32[]{:S(2)}, u32[]{:S(2)}) collective-permute-start(bf16[3,2,128,512]{3,2,1,0:T(8,128)(2,1)S(1)} %pad_maximum_fusion.1.refs_1_.refs_3_), channel_id=1, source_target_pairs={{0,4},{4,0},{8,12},{12,8},{1,5},{5,1},{9,13},{13,9},{2,6},{6,2},{1... | collective-permute-start | bytes 2359304 | tf_op jit(solution)/shard_map/ppermute | solution.py:24
  96.6 1.9 collective-permute-start.24
  100.6 1.2 copy-done.14
  102.8 1.4 copy-done.13
  104.1 1.4 collective-permute-start.22
  105.5 6.2 %collective-permute-done.24 = bf16[2,2,128,512]{3,2,1,0:T(8,128)(2,1)S(1)} collective-permute-done((bf16[2,2,128,512]{3,2,1,0:T(8,128)(2,1)}, bf16[2,2,128,512]{3,2,1,0:T(8,128)(2,1)S(1)}, u32[]{:S(2)}, u32[]{:S(2)}) %collective-permute-start.24) | collective-permute-done | bytes 524320 | tf_op jit(solution)/shard_map/ppermute | solution.py:54
  111.9 7.4 %collective-permute-done.22.mem_own = bf16[512,512]{1,0:T(8,128)(2,1)S(1)} collective-permute-done((bf16[512,512]{1,0:T(8,128)(2,1)S(1)}, bf16[512,512]{1,0:T(8,128)(2,1)S(1)}, u32[]{:S(2)}, u32[]{:S(2)}) %collective-permute-start.22) | collective-permute-done | bytes 524320 | tf_op jit(solution)/shard_map/ppermute | solution.py:32
  119.3 3.1 %collective-permute-start.25 = (bf16[4,2,128,512]{3,2,1,0:T(8,128)(2,1)S(1)}, bf16[4,2,128,512]{3,2,1,0:T(8,128)(2,1)S(1)}, u32[]{:S(2)}, u32[]{:S(2)}) collective-permute-start(bf16[4,2,128,512]{3,2,1,0:T(8,128)(2,1)S(1)} %pad_maximum_fusion.refs_0_), channel_id=1, source_target_pairs={{16,20},{20,16},{24,28},{28,24},{17,21},{21,17},{25,29},{29,25},{1... | collective-permute-start | bytes 3145736 | tf_op jit(solution)/shard_map/ppermute | solution.py:54
  122.5 2.9 collective-permute-done.23.mem_other
  126.5 37.9 %decoder.1 = (bf16[512,512]{1,0:T(8,128)(2,1)S(1)}, f32[512,512]{1,0:T(8,128)}, bf16[512,512]{1,0:T(8,128)(2,1)S(1)}, bf16[512,512]{1,0:T(8,128)(2,1)S(1)}, f32[...) custom-call(s32[3]{0:T(128)S(1)} %copy-done.4, ...), custom_call_target="tpu_custom_call" | custom-call | flops 42949672960 | bytes 8388608 | tf_op jit(solution)/shard_map/decoder/pallas_call | solution.py:585
  164.8 1.5 collective-permute-done.26
  166.5 1.3 collective-permute-start.27
  167.8 11.2 %collective-permute-done.27.d_mem_in = bf16[512,512]{1,0:T(8,128)(2,1)S(1)} collective-permute-done((bf16[512,512]{1,0:T(8,128)(2,1)S(1)}, bf16[512,512]{1,0:T(8,128)(2,1)S(1)}, u32[]{:S(2)}, u32[]{:S(2)}) %collective-permute-start.27) | collective-permute-done | bytes 524320 | tf_op jit(solution)/shard_map/ppermute | solution.py:32
  179.1 2.8 collective-permute-start.30
  181.9 1.9 feed_bwd.1
  184.3 1.1 add_convert_fusion.3
  185.4 5.7 %collective-permute-start.31 = (bf16[1,4,128,512]{3,2,1,0:T(8,128)(2,1)}, bf16[1,4,128,512]{3,2,1,0:T(8,128)(2,1)S(1)}, u32[]{:S(2)}, u32[]{:S(2)}) collective-permute-start(bf16[1,4,128,512]{3,2,1,0:T(8,128)(2,1)} %get-tuple-element.193), channel_id=1, source_target_pairs={{16,24},{20,28},{24,16},{28,20},{17,25},{21,29},{25,17},{29,21},{1... | collective-permute-start | bytes 1572872 | tf_op jit(solution)/shard_map/ppermute | solution.py:54
  191.9 3.5 %all-to-all-start.2 = ((bf16[4,128,512]{2,1,0:T(8,128)(2,1)}), bf16[4,128,512]{2,1,0:T(8,128)(2,1)S(1)}, u32[]{:S(2)}, u32[]{:S(2)}) async-start(bf16[4,128,512]{2,1,0:T(8,128)(2,1)} %bitcast.35), calls=%async_computation.2 | async-start | bytes 1048576 | tf_op jit(solution)/shard_map/all_to_all | solution.py:112
  195.4 7.9 %collective-permute-done.31 = bf16[1,4,128,512]{3,2,1,0:T(8,128)(2,1)S(1)} collective-permute-done((bf16[1,4,128,512]{3,2,1,0:T(8,128)(2,1)}, bf16[1,4,128,512]{3,2,1,0:T(8,128)(2,1)S(1)}, u32[]{:S(2)}, u32[]{:S(2)}) %collective-permute-start.31) | collective-permute-done | bytes 524320 | tf_op jit(solution)/shard_map/ppermute | solution.py:54
  204.2 2.3 collective-permute-start.34
  206.5 2.7 add_convert_fusion.2
  209.1 1.2 collective-permute-start.33
  210.4 1.1 add_convert_fusion.5
  211.5 1.1 collective-permute-start.32
  212.6 21.2 %self_bwd.1 = (f32[512,512]{1,0:T(8,128)}, bf16[512,512]{1,0:T(8,128)(2,1)}, bf16[2,4,128,512]{3,2,1,0:T(8,128)(2,1)}, bf16[2,4,128,512]{3,2,1,0:T(8,128)(2,1)}) custom-call(s32[3]{0:T(128)} %pad_add_fusion.ints, f32[512,512]{1,0:T(8,128)} %get-tuple-element.128.d_mid_in.d_mid, bf16[1024,128]{1,0:T(8,128)(2,1)} %fusion.code_in, ...), custom_call_target="tpu_custom_call" | custom-call | flops 10737418240 | bytes 8388608 | tf_op jit(solution)/shard_map/self_bwd/pallas_call | solution.py:585
  233.9 2.1 collective-permute-start.35
  236.1 2.4 collective-permute-done.35
  238.5 1.5 add_convert_fusion
  240.0 1.2 add_convert_fusion.13
  243.1 1.9 collective-permute-start.39
  245.2 1.1 collective-permute-start.38
  247.1 3.4 %last.1 = (bf16[512,512]{1,0:T(8,128)(2,1)}, f32[2,512]{1,0:T(2,128)}) custom-call(f32[512,512]{1,0:T(8,128)} %get-tuple-element.149.d_own, bf16[512,512]{1,0:T(8,128)(2,1)} %copy-done.32, bf16[512,512]{1,0:T(8,128)(2,1)} %bitcast.6.x_own, f32[512,512]{1,0:T(8,128)} %get-tuple-element.128.d_mid_in.d_mid, f32[8,512]{1,0:T(8,128)} %get-tuple-element.97.norms), custom_call_target="tpu_custom_call" | custom-call | flops 1073741824 | bytes 8388608 | tf_op jit(solution)/shard_map/last/pallas_call | solution.py:585
  250.6 3.8 %all-to-all-start.3 = ((bf16[4,128,512]{2,1,0:T(8,128)(2,1)}), bf16[4,128,512]{2,1,0:T(8,128)(2,1)S(1)}, u32[]{:S(2)}, u32[]{:S(2)}) async-start(bf16[4,128,512]{2,1,0:T(8,128)(2,1)} %bitcast.162), calls=%async_computation.3 | async-start | bytes 1048576 | tf_op jit(solution)/shard_map/all_to_all | solution.py:112
  255.3 5.9 %collective-permute-done.37 = bf16[1,6,128,512]{3,2,1,0:T(8,128)(2,1)} collective-permute-done((bf16[1,6,128,512]{3,2,1,0:T(8,128)(2,1)}, bf16[1,6,128,512]{3,2,1,0:T(8,128)(2,1)}, u32[]{:S(2)}, u32[]{:S(2)}) %collective-permute-start.37) | collective-permute-done | bytes 786464 | tf_op jit(solution)/shard_map/ppermute | solution.py:24
  263.3 1.3 collective-permute-start.41
  264.6 1.2 add_convert_fusion.9
  267.0 2.4 collective-permute-done.42
  269.9 1.2 collective-permute-start.40
  271.1 2.5 collective-permute-start.43
  273.6 8.4 %collective-permute-done.44 = bf16[1,2,144,512]{3,2,1,0:T(8,128)(2,1)S(1)} collective-permute-done((bf16[1,2,144,512]{3,2,1,0:T(8,128)(2,1)S(1)}, bf16[1,2,144,512]{3,2,1,0:T(8,128)(2,1)S(1)}, u32[]{:S(2)}, u32[]{:S(2)}) %collective-permute-start.44) | collective-permute-done | bytes 294944 | tf_op jit(solution)/shard_map/ppermute | solution.py:24
  282.9 1.7 add_bitcast_fusion.1
  286.1 2.3 collective-permute-start.45
  289.2 3.1 %collective-permute-done.47 = bf16[1,1,144,512]{3,2,1,0:T(8,128)(2,1)S(1)} collective-permute-done((bf16[1,1,144,512]{3,2,1,0:T(8,128)(2,1)}, bf16[1,1,144,512]{3,2,1,0:T(8,128)(2,1)S(1)}, u32[]{:S(2)}, u32[]{:S(2)}) %collective-permute-start.47) | collective-permute-done | bytes 147488 | tf_op jit(solution)/shard_map/ppermute | solution.py:24
  (223 shorter events, 37.6 us)
Async XLA Ops:
  0.7 13.0 %collective-permute-start.2 = (s32[2,2,1024]{2,1,0:T(2,128)}, s32[2,2,1024]{2,1,0:T(2,128)S(1)}, u32[]{:S(2)}, u32[]{:S(2)}) collective-permute-start(s32[2,2,1024]{2,1,0:T(2,128)} %param.13), channel_id=1, source_target_pairs={{0,4},{4,0},{8,12},{12,8},{1,5},{5,1},{9,13},{13,9},{2,6},{6,2},{1... | collective-permute-start | bytes 49160 | tf_op jit(solution)/shard_map/ppermute | solution.py:24
  2.2 19.7 %collective-permute-start.11 = (bf16[128,4,64]{0,2,1:T(8,128)(2,1)S(1)}, bf16[128,4,64]{0,2,1:T(8,128)(2,1)S(1)}, u32[]{:S(2)}, u32[]{:S(2)}) collective-permute-start(bf16[128,4,64]{0,2,1:T(8,128)(2,1)S(1)} %pad_maximum_fusion.13), channel_id=1, source_target_pairs={{0,16},{1,17},{2,18},{3,19},{4,20},{5,21},{6,22},{7,23},{8,24},{9,... | collective-permute-start | bytes 196616 | tf_op jit(solution)/shard_map/ppermute | solution.py:32
  3.5 42.1 %collective-permute-start.5 = (bf16[128,512]{1,0:T(8,128)(2,1)}, bf16[128,512]{1,0:T(8,128)(2,1)S(1)}, u32[]{:S(2)}, u32[]{:S(2)}) collective-permute-start(bf16[128,512]{1,0:T(8,128)(2,1)} %bitcast.167), channel_id=1, source_target_pairs={{0,2},{1,3},{2,0},{3,1},{4,6},{5,7},{6,4},{7,5},{8,10},{9,11},{10,... | collective-permute-start | bytes 393224 | tf_op jit(solution)/shard_map/ppermute | solution.py:24
  8.8 13.3 %collective-permute-start.3 = (bf16[144,512]{1,0:T(8,128)(2,1)S(1)}, bf16[144,512]{1,0:T(8,128)(2,1)S(1)}, u32[]{:S(2)}, u32[]{:S(2)}) collective-permute-start(bf16[144,512]{1,0:T(8,128)(2,1)S(1)} %concatenate.114), channel_id=1, source_target_pairs={{0,2},{1,3},{2,0},{3,1},{4,6},{5,7},{6,4},{7,5},{8,10},{9,11},{10,... | collective-permute-start | bytes 442376 | tf_op jit(solution)/shard_map/ppermute | solution.py:24
  10.9 11.3 %collective-permute-start.14 = (bf16[1,128,1024]{2,1,0:T(8,128)(2,1)S(1)}, bf16[1,128,1024]{2,1,0:T(8,128)(2,1)S(1)}, u32[]{:S(2)}, u32[]{:S(2)}) collective-permute-start(bf16[1,128,1024]{2,1,0:T(8,128)(2,1)S(1)} %maximum_bitcast_fusion), channel_id=1, source_target_pairs={{0,8},{4,12},{8,0},{12,4},{1,9},{5,13},{9,1},{13,5},{2,10},{6,14},... | collective-permute-start | bytes 786440 | tf_op jit(solution)/shard_map/ppermute | solution.py:24
  13.6 2.1 collective-permute-start
  15.7 45.9 %collective-permute-start.10 = (bf16[2,128,512]{2,1,0:T(8,128)(2,1)}, bf16[2,128,512]{2,1,0:T(8,128)(2,1)}, u32[]{:S(2)}, u32[]{:S(2)}) collective-permute-start(bf16[2,128,512]{2,1,0:T(8,128)(2,1)} %get-tuple-element.211), channel_id=1, source_target_pairs={{0,4},{4,0},{8,12},{12,8},{1,5},{5,1},{9,13},{13,9},{2,6},{6,2},{1... | collective-permute-start | bytes 786440 | tf_op jit(solution)/shard_map/ppermute | solution.py:24
  17.0 18.9 %all-to-all-start = ((bf16[4,128,512]{2,1,0:T(8,128)(2,1)}), bf16[4,128,512]{2,1,0:T(8,128)(2,1)}, u32[]{:S(2)}, u32[]{:S(2)}) async-start(bf16[4,128,512]{2,1,0:T(8,128)(2,1)} %maximum_select_fusion), calls=%async_computation | async-start | bytes 1048576 | tf_op jit(solution)/shard_map/all_to_all | solution.py:632
  21.9 23.6 %copy-start.25 = (bf16[1,128,512]{2,1,0:T(8,128)(2,1)S(1)}, bf16[1,128,512]{2,1,0:T(8,128)(2,1)}, u32[]{:S(2)}) copy-start(bf16[1,128,512]{2,1,0:T(8,128)(2,1)} %param.17) | copy-start | bytes 393220
  22.2 103.2 %copy-start = (bf16[2,128,1024]{2,1,0:T(8,128)(2,1)}, bf16[2,128,1024]{2,1,0:T(8,128)(2,1)S(1)}, u32[]{:S(2)}) copy-start(bf16[2,128,1024]{2,1,0:T(8,128)(2,1)S(1)} %pad_maximum_fusion.4.refs_0_.refs_2_) | copy-start | bytes 1572868
  35.8 9.0 %collective-permute-start.4 = (bf16[2,144,512]{2,1,0:T(8,128)(2,1)S(1)}, bf16[2,144,512]{2,1,0:T(8,128)(2,1)S(1)}, u32[]{:S(2)}, u32[]{:S(2)}) collective-permute-start(bf16[2,144,512]{2,1,0:T(8,128)(2,1)S(1)} %pad_maximum_fusion.7), channel_id=1, source_target_pairs={{0,1},{1,0},{2,3},{3,2},{4,5},{5,4},{6,7},{7,6},{8,9},{9,8},{10,11... | collective-permute-start | bytes 884744 | tf_op jit(solution)/shard_map/ppermute | solution.py:24
  36.6 9.1 %collective-permute-start.12 = (bf16[1,128,512]{2,1,0:T(8,128)(2,1)S(1)}, bf16[1,128,512]{2,1,0:T(8,128)(2,1)S(1)}, u32[]{:S(2)}, u32[]{:S(2)}) collective-permute-start(bf16[1,128,512]{2,1,0:T(8,128)(2,1)S(1)} %copy.70), channel_id=1, source_target_pairs={{16,24},{20,28},{24,16},{28,20},{17,25},{21,29},{25,17},{29,21},{1... | collective-permute-start | bytes 393224 | tf_op jit(solution)/shard_map/ppermute | solution.py:54
  38.8 13.3 %collective-permute-start.15 = (bf16[2,128,512]{2,1,0:T(8,128)(2,1)S(1)}, bf16[2,128,512]{2,1,0:T(8,128)(2,1)S(1)}, u32[]{:S(2)}, u32[]{:S(2)}) collective-permute-start(bf16[2,128,512]{2,1,0:T(8,128)(2,1)S(1)} %get-tuple-element.209), channel_id=1, source_target_pairs={{0,2},{1,3},{2,0},{3,1},{4,6},{5,7},{6,4},{7,5},{8,10},{9,11},{10,... | collective-permute-start | bytes 786440 | tf_op jit(solution)/shard_map/ppermute | solution.py:24
  45.6 12.5 %collective-permute-start.7 = (bf16[4,144,512]{2,1,0:T(8,128)(2,1)}, bf16[4,144,512]{2,1,0:T(8,128)(2,1)}, u32[]{:S(2)}, u32[]{:S(2)}) collective-permute-start(bf16[4,144,512]{2,1,0:T(8,128)(2,1)} %constant_dynamic-update-slice_fusion.refs_0_), channel_id=1, source_target_pairs={{0,8},{4,12},{8,0},{12,4},{1,9},{5,13},{9,1},{13,5},{2,10},{6,14},... | collective-permute-start | bytes 1769480 | tf_op jit(solution)/shard_map/ppermute | solution.py:24
  45.6 10.0 %collective-permute-start.6 = (bf16[2,128,512]{2,1,0:T(8,128)(2,1)S(1)}, bf16[2,128,512]{2,1,0:T(8,128)(2,1)S(1)}, u32[]{:S(2)}, u32[]{:S(2)}) collective-permute-start(bf16[2,128,512]{2,1,0:T(8,128)(2,1)S(1)} %pad_maximum_fusion.9), channel_id=1, source_target_pairs={{0,1},{1,0},{2,3},{3,2},{4,5},{5,4},{6,7},{7,6},{8,9},{9,8},{10,11... | collective-permute-start | bytes 786440 | tf_op jit(solution)/shard_map/ppermute | solution.py:24
  45.7 32.1 %collective-permute-start.1 = (bf16[512,512]{1,0:T(8,128)(2,1)}, bf16[512,512]{1,0:T(8,128)(2,1)}, u32[]{:S(2)}, u32[]{:S(2)}) collective-permute-start(bf16[512,512]{1,0:T(8,128)(2,1)} %bitcast.6.x_own), channel_id=1, source_target_pairs={{0,4},{4,0},{8,12},{12,8},{1,5},{5,1},{9,13},{13,9},{2,6},{6,2},{1... | collective-permute-start | bytes 1572872 | tf_op jit(solution)/shard_map/ppermute | solution.py:24
  52.1 16.2 %collective-permute-start.13 = (bf16[2,128,512]{2,1,0:T(8,128)(2,1)S(1)}, bf16[2,128,512]{2,1,0:T(8,128)(2,1)}, u32[]{:S(2)}, u32[]{:S(2)}) collective-permute-start(bf16[2,128,512]{2,1,0:T(8,128)(2,1)S(1)} %constant_dynamic-update-slice_fusion.2), channel_id=1, source_target_pairs={{16,18},{17,19},{18,16},{19,17},{20,22},{21,23},{22,20},{23,21},{2... | collective-permute-start | bytes 786440 | tf_op jit(solution)/shard_map/ppermute | solution.py:54
  55.6 21.0 %collective-permute-start.16 = (bf16[2,2,128,512]{3,2,1,0:T(8,128)(2,1)S(1)}, bf16[2,2,128,512]{3,2,1,0:T(8,128)(2,1)}, u32[]{:S(2)}, u32[]{:S(2)}) collective-permute-start(bf16[2,2,128,512]{3,2,1,0:T(8,128)(2,1)S(1)} %pad_maximum_fusion.5), channel_id=1, source_target_pairs={{0,1},{1,0},{2,3},{3,2},{4,5},{5,4},{6,7},{7,6},{8,9},{9,8},{10,11... | collective-permute-start | bytes 1572872 | tf_op jit(solution)/shard_map/ppermute | solution.py:24
  55.7 69.7 %copy-start.3 = (bf16[3,128,512]{2,1,0:T(8,128)(2,1)}, bf16[3,128,512]{2,1,0:T(8,128)(2,1)S(1)}, u32[]{:S(2)}) copy-start(bf16[3,128,512]{2,1,0:T(8,128)(2,1)S(1)} %pad_maximum_fusion.6.refs_2_.refs_4_) | copy-start | bytes 1179652
  58.1 19.7 %collective-permute-start.8 = (bf16[4,144,512]{2,1,0:T(8,128)(2,1)}, bf16[4,144,512]{2,1,0:T(8,128)(2,1)}, u32[]{:S(2)}, u32[]{:S(2)}) collective-permute-start(bf16[4,144,512]{2,1,0:T(8,128)(2,1)} %constant_dynamic-update-slice_fusion.refs_0_), channel_id=1, source_target_pairs={{0,4},{4,0},{8,12},{12,8},{1,5},{5,1},{9,13},{13,9},{2,6},{6,2},{1... | collective-permute-start | bytes 1769480 | tf_op jit(solution)/shard_map/ppermute | solution.py:24
  61.6 16.2 %collective-permute-start.9 = (bf16[4,144,512]{2,1,0:T(8,128)(2,1)}, bf16[4,144,512]{2,1,0:T(8,128)(2,1)}, u32[]{:S(2)}, u32[]{:S(2)}) collective-permute-start(bf16[4,144,512]{2,1,0:T(8,128)(2,1)} %collective-permute-done.7.refs_1_), channel_id=1, source_target_pairs={{0,4},{4,0},{8,12},{12,8},{1,5},{5,1},{9,13},{13,9},{2,6},{6,2},{1... | collective-permute-start | bytes 1769480 | tf_op jit(solution)/shard_map/ppermute | solution.py:24
  63.5 27.6 %all-to-all-start.1 = ((bf16[4,128,512]{2,1,0:T(8,128)(2,1)}), bf16[4,128,512]{2,1,0:T(8,128)(2,1)S(1)}, u32[]{:S(2)}, u32[]{:S(2)}) async-start(bf16[4,128,512]{2,1,0:T(8,128)(2,1)} %maximum_select_fusion.1), calls=%async_computation.1 | async-start | bytes 1048576 | tf_op jit(solution)/shard_map/all_to_all | solution.py:633
  70.1 21.0 %collective-permute-start.17 = (bf16[3,128,512]{2,1,0:T(8,128)(2,1)S(1)}, bf16[3,128,512]{2,1,0:T(8,128)(2,1)S(1)}, u32[]{:S(2)}, u32[]{:S(2)}) collective-permute-start(bf16[3,128,512]{2,1,0:T(8,128)(2,1)S(1)} %pad_maximum_fusion.6.refs_2_.refs_4_), channel_id=1, source_target_pairs={{0,8},{4,12},{8,0},{12,4},{1,9},{5,13},{9,1},{13,5},{2,10},{6,14},... | collective-permute-start | bytes 1179656 | tf_op jit(solution)/shard_map/ppermute | solution.py:24
  77.8 47.7 %copy-start.1 = (bf16[3,2,128,512]{3,2,1,0:T(8,128)(2,1)}, bf16[3,2,128,512]{3,2,1,0:T(8,128)(2,1)S(1)}, u32[]{:S(2)}) copy-start(bf16[3,2,128,512]{3,2,1,0:T(8,128)(2,1)S(1)} %pad_maximum_fusion.1.refs_1_.refs_3_) | copy-start | bytes 2359300
  91.1 34.3 %copy-start.2 = (bf16[4,128,512]{2,1,0:T(8,128)(2,1)}, bf16[4,128,512]{2,1,0:T(8,128)(2,1)S(1)}, u32[]{:S(2)}) copy-start(bf16[4,128,512]{2,1,0:T(8,128)(2,1)S(1)} %all-to-all-done.1) | copy-start | bytes 1572868
  91.1 34.3 %copy-start.7 = (bf16[3,128,512]{2,1,0:T(8,128)(2,1)}, bf16[3,128,512]{2,1,0:T(8,128)(2,1)S(1)}, u32[]{:S(2)}) copy-start(bf16[3,128,512]{2,1,0:T(8,128)(2,1)S(1)} %collective-permute-done.17.refs_3_.refs_5_) | copy-start | bytes 1179652
  91.1 8.7 %collective-permute-start.19 = (bf16[3,2,128,512]{3,2,1,0:T(8,128)(2,1)S(1)}, bf16[3,2,128,512]{3,2,1,0:T(8,128)(2,1)S(1)}, u32[]{:S(2)}, u32[]{:S(2)}) collective-permute-start(bf16[3,2,128,512]{3,2,1,0:T(8,128)(2,1)S(1)} %pad_maximum_fusion.1.refs_1_.refs_3_), channel_id=1, source_target_pairs={{0,4},{4,0},{8,12},{12,8},{1,5},{5,1},{9,13},{13,9},{2,6},{6,2},{1... | collective-permute-start | bytes 2359304 | tf_op jit(solution)/shard_map/ppermute | solution.py:24
  96.0 3.8 %collective-permute-start.18 = (bf16[2,128,1024]{2,1,0:T(8,128)(2,1)S(1)}, bf16[2,128,1024]{2,1,0:T(8,128)(2,1)S(1)}, u32[]{:S(2)}, u32[]{:S(2)}) collective-permute-start(bf16[2,128,1024]{2,1,0:T(8,128)(2,1)S(1)} %pad_maximum_fusion.4.refs_0_.refs_2_), channel_id=1, source_target_pairs={{0,4},{4,0},{8,12},{12,8},{1,5},{5,1},{9,13},{13,9},{2,6},{6,2},{1... | collective-permute-start | bytes 1572872 | tf_op jit(solution)/shard_map/ppermute | solution.py:24
  96.1 3.1 %collective-permute-start.20 = (bf16[3,128,512]{2,1,0:T(8,128)(2,1)S(1)}, bf16[3,128,512]{2,1,0:T(8,128)(2,1)S(1)}, u32[]{:S(2)}, u32[]{:S(2)}) collective-permute-start(bf16[3,128,512]{2,1,0:T(8,128)(2,1)S(1)} %pad_maximum_fusion.6.refs_2_.refs_4_), channel_id=1, source_target_pairs={{0,4},{4,0},{8,12},{12,8},{1,5},{5,1},{9,13},{13,9},{2,6},{6,2},{1... | collective-permute-start | bytes 1179656 | tf_op jit(solution)/shard_map/ppermute | solution.py:24
  96.5 3.3 %collective-permute-start.21 = (bf16[3,128,512]{2,1,0:T(8,128)(2,1)S(1)}, bf16[3,128,512]{2,1,0:T(8,128)(2,1)S(1)}, u32[]{:S(2)}, u32[]{:S(2)}) collective-permute-start(bf16[3,128,512]{2,1,0:T(8,128)(2,1)S(1)} %collective-permute-done.17.refs_3_.refs_5_), channel_id=1, source_target_pairs={{0,4},{4,0},{8,12},{12,8},{1,5},{5,1},{9,13},{13,9},{2,6},{6,2},{1... | collective-permute-start | bytes 1179656 | tf_op jit(solution)/shard_map/ppermute | solution.py:24
  96.6 15.2 %collective-permute-start.24 = (bf16[2,2,128,512]{3,2,1,0:T(8,128)(2,1)}, bf16[2,2,128,512]{3,2,1,0:T(8,128)(2,1)S(1)}, u32[]{:S(2)}, u32[]{:S(2)}) collective-permute-start(bf16[2,2,128,512]{3,2,1,0:T(8,128)(2,1)} %pad_maximum_fusion.3), channel_id=1, source_target_pairs={{16,17},{17,16},{18,19},{19,18},{20,21},{21,20},{22,23},{23,22},{2... | collective-permute-start | bytes 1572872 | tf_op jit(solution)/shard_map/ppermute | solution.py:54
  99.2 26.2 %copy-start.8 = (bf16[3,128,512]{2,1,0:T(8,128)(2,1)}, bf16[3,128,512]{2,1,0:T(8,128)(2,1)S(1)}, u32[]{:S(2)}) copy-start(bf16[3,128,512]{2,1,0:T(8,128)(2,1)S(1)} %collective-permute-done.20.refs_6_.refs_8_) | copy-start | bytes 1179652
  99.8 25.6 %copy-start.9 = (bf16[3,128,512]{2,1,0:T(8,128)(2,1)}, bf16[3,128,512]{2,1,0:T(8,128)(2,1)S(1)}, u32[]{:S(2)}) copy-start(bf16[3,128,512]{2,1,0:T(8,128)(2,1)S(1)} %collective-permute-done.21.refs_7_.refs_9_) | copy-start | bytes 1179652
  99.8 25.7 %copy-start.6 = (bf16[2,128,1024]{2,1,0:T(8,128)(2,1)}, bf16[2,128,1024]{2,1,0:T(8,128)(2,1)S(1)}, u32[]{:S(2)}) copy-start(bf16[2,128,1024]{2,1,0:T(8,128)(2,1)S(1)} %collective-permute-done.18.refs_4_.refs_6_) | copy-start | bytes 1572868
  99.8 25.7 %copy-start.5 = (bf16[3,2,128,512]{3,2,1,0:T(8,128)(2,1)}, bf16[3,2,128,512]{3,2,1,0:T(8,128)(2,1)S(1)}, u32[]{:S(2)}) copy-start(bf16[3,2,128,512]{3,2,1,0:T(8,128)(2,1)S(1)} %collective-permute-done.19.refs_5_.refs_7_) | copy-start | bytes 2359300
  104.1 60.2 %copy-start.15 = (f32[512,512]{1,0:T(8,128)}, f32[512,512]{1,0:T(8,128)S(1)}, u32[]{:S(2)}) copy-start(f32[512,512]{1,0:T(8,128)S(1)} %get-tuple-element.102.encoded_in) | copy-start | bytes 3145732
  104.1 22.4 %copy-start.11 = (f32[8,512]{1,0:T(8,128)S(1)}, f32[8,512]{1,0:T(8,128)}, u32[]{:S(2)}) copy-start(f32[8,512]{1,0:T(8,128)} %get-tuple-element.97.norms) | copy-start | bytes 49156
  104.1 15.2 %collective-permute-start.22 = (bf16[512,512]{1,0:T(8,128)(2,1)S(1)}, bf16[512,512]{1,0:T(8,128)(2,1)S(1)}, u32[]{:S(2)}, u32[]{:S(2)}) collective-permute-start(bf16[512,512]{1,0:T(8,128)(2,1)S(1)} %get-tuple-element.103), channel_id=1, source_target_pairs={{0,16},{1,17},{2,18},{3,19},{4,20},{5,21},{6,22},{7,23},{8,24},{9,... | collective-permute-start | bytes 1572872 | tf_op jit(solution)/shard_map/ppermute | solution.py:32
  119.3 6.1 %collective-permute-start.25 = (bf16[4,2,128,512]{3,2,1,0:T(8,128)(2,1)S(1)}, bf16[4,2,128,512]{3,2,1,0:T(8,128)(2,1)S(1)}, u32[]{:S(2)}, u32[]{:S(2)}) collective-permute-start(bf16[4,2,128,512]{3,2,1,0:T(8,128)(2,1)S(1)} %pad_maximum_fusion.refs_0_), channel_id=1, source_target_pairs={{16,20},{20,16},{24,28},{28,24},{17,21},{21,17},{25,29},{29,25},{1... | collective-permute-start | bytes 3145736 | tf_op jit(solution)/shard_map/ppermute | solution.py:54
  122.4 3.0 %collective-permute-start.23 = (bf16[512,512]{1,0:T(8,128)(2,1)S(1)}, bf16[512,512]{1,0:T(8,128)(2,1)S(1)}, u32[]{:S(2)}, u32[]{:S(2)}) collective-permute-start(bf16[512,512]{1,0:T(8,128)(2,1)S(1)} %collective-permute-done.22.mem_own), channel_id=1, source_target_pairs={{0,4},{4,0},{8,12},{12,8},{1,5},{5,1},{9,13},{13,9},{2,6},{6,2},{1... | collective-permute-start | bytes 1572872 | tf_op jit(solution)/shard_map/ppermute | solution.py:24
  164.4 2.0 collective-permute-start.26
  166.5 12.5 %collective-permute-start.27 = (bf16[512,512]{1,0:T(8,128)(2,1)S(1)}, bf16[512,512]{1,0:T(8,128)(2,1)S(1)}, u32[]{:S(2)}, u32[]{:S(2)}) collective-permute-start(bf16[512,512]{1,0:T(8,128)(2,1)S(1)} %add_convert_fusion.8), channel_id=1, source_target_pairs={{16,0},{17,1},{18,2},{19,3},{20,4},{21,5},{22,6},{23,7},{24,8},{25... | collective-permute-start | bytes 1572872 | tf_op jit(solution)/shard_map/ppermute | solution.py:32
  179.1 5.3 %collective-permute-start.30 = (bf16[2,4,128,512]{3,2,1,0:T(8,128)(2,1)}, bf16[2,4,128,512]{3,2,1,0:T(8,128)(2,1)S(1)}, u32[]{:S(2)}, u32[]{:S(2)}) collective-permute-start(bf16[2,4,128,512]{3,2,1,0:T(8,128)(2,1)} %get-tuple-element.122), channel_id=1, source_target_pairs={{16,20},{20,16},{24,28},{28,24},{17,21},{21,17},{25,29},{29,25},{1... | collective-permute-start | bytes 3145736 | tf_op jit(solution)/shard_map/ppermute | solution.py:54
  183.8 11.7 %collective-permute-start.28 = (bf16[2,4,128,512]{3,2,1,0:T(8,128)(2,1)}, bf16[2,4,128,512]{3,2,1,0:T(8,128)(2,1)S(1)}, u32[]{:S(2)}, u32[]{:S(2)}) collective-permute-start(bf16[2,4,128,512]{3,2,1,0:T(8,128)(2,1)} %get-tuple-element.118), channel_id=1, source_target_pairs={{0,4},{4,0},{8,12},{12,8},{1,5},{5,1},{9,13},{13,9},{2,6},{6,2},{1... | collective-permute-start | bytes 3145736 | tf_op jit(solution)/shard_map/ppermute | solution.py:24
  183.8 11.6 %collective-permute-start.29 = (bf16[2,4,128,512]{3,2,1,0:T(8,128)(2,1)}, bf16[2,4,128,512]{3,2,1,0:T(8,128)(2,1)}, u32[]{:S(2)}, u32[]{:S(2)}) collective-permute-start(bf16[2,4,128,512]{3,2,1,0:T(8,128)(2,1)} %get-tuple-element.119), channel_id=1, source_target_pairs={{0,4},{4,0},{8,12},{12,8},{1,5},{5,1},{9,13},{13,9},{2,6},{6,2},{1... | collective-permute-start | bytes 3145736 | tf_op jit(solution)/shard_map/ppermute | solution.py:24
  185.4 17.9 %collective-permute-start.31 = (bf16[1,4,128,512]{3,2,1,0:T(8,128)(2,1)}, bf16[1,4,128,512]{3,2,1,0:T(8,128)(2,1)S(1)}, u32[]{:S(2)}, u32[]{:S(2)}) collective-permute-start(bf16[1,4,128,512]{3,2,1,0:T(8,128)(2,1)} %get-tuple-element.193), channel_id=1, source_target_pairs={{16,24},{20,28},{24,16},{28,20},{17,25},{21,29},{25,17},{29,21},{1... | collective-permute-start | bytes 1572872 | tf_op jit(solution)/shard_map/ppermute | solution.py:54
  191.9 41.9 %all-to-all-start.2 = ((bf16[4,128,512]{2,1,0:T(8,128)(2,1)}), bf16[4,128,512]{2,1,0:T(8,128)(2,1)S(1)}, u32[]{:S(2)}, u32[]{:S(2)}) async-start(bf16[4,128,512]{2,1,0:T(8,128)(2,1)} %bitcast.35), calls=%async_computation.2 | async-start | bytes 1048576 | tf_op jit(solution)/shard_map/all_to_all | solution.py:112
  204.2 29.7 %collective-permute-start.34 = (bf16[1,2,128,512]{3,2,1,0:T(8,128)(2,1)}, bf16[1,2,128,512]{3,2,1,0:T(8,128)(2,1)}, u32[]{:S(2)}, u32[]{:S(2)}) collective-permute-start(bf16[1,2,128,512]{3,2,1,0:T(8,128)(2,1)} %get-tuple-element.201), channel_id=1, source_target_pairs={{16,17},{17,16},{18,19},{19,18},{20,21},{21,20},{22,23},{23,22},{2... | collective-permute-start | bytes 786440 | tf_op jit(solution)/shard_map/ppermute | solution.py:54
  209.1 24.7 %collective-permute-start.33 = (bf16[2,2,128,512]{3,2,1,0:T(8,128)(2,1)}, bf16[2,2,128,512]{3,2,1,0:T(8,128)(2,1)}, u32[]{:S(2)}, u32[]{:S(2)}) collective-permute-start(bf16[2,2,128,512]{3,2,1,0:T(8,128)(2,1)} %get-tuple-element.191), channel_id=1, source_target_pairs={{0,1},{1,0},{2,3},{3,2},{4,5},{5,4},{6,7},{7,6},{8,9},{9,8},{10,11... | collective-permute-start | bytes 1572872 | tf_op jit(solution)/shard_map/ppermute | solution.py:24
  211.5 22.4 %collective-permute-start.32 = (bf16[1,4,128,512]{3,2,1,0:T(8,128)(2,1)}, bf16[1,4,128,512]{3,2,1,0:T(8,128)(2,1)S(1)}, u32[]{:S(2)}, u32[]{:S(2)}) collective-permute-start(bf16[1,4,128,512]{3,2,1,0:T(8,128)(2,1)} %get-tuple-element.194), channel_id=1, source_target_pairs={{0,8},{4,12},{8,0},{12,4},{1,9},{5,13},{9,1},{13,5},{2,10},{6,14},... | collective-permute-start | bytes 1572872 | tf_op jit(solution)/shard_map/ppermute | solution.py:24
  233.9 4.6 %collective-permute-start.35 = (bf16[2,4,128,512]{3,2,1,0:T(8,128)(2,1)}, bf16[2,4,128,512]{3,2,1,0:T(8,128)(2,1)S(1)}, u32[]{:S(2)}, u32[]{:S(2)}) collective-permute-start(bf16[2,4,128,512]{3,2,1,0:T(8,128)(2,1)} %get-tuple-element.143), channel_id=1, source_target_pairs={{0,4},{4,0},{8,12},{12,8},{1,5},{5,1},{9,13},{13,9},{2,6},{6,2},{1... | collective-permute-start | bytes 3145736 | tf_op jit(solution)/shard_map/ppermute | solution.py:24
  236.0 10.3 %collective-permute-start.36 = (bf16[512,512]{1,0:T(8,128)(2,1)}, bf16[512,512]{1,0:T(8,128)(2,1)S(1)}, u32[]{:S(2)}, u32[]{:S(2)}) collective-permute-start(bf16[512,512]{1,0:T(8,128)(2,1)} %get-tuple-element.150), channel_id=1, source_target_pairs={{0,4},{4,0},{8,12},{12,8},{1,5},{5,1},{9,13},{13,9},{2,6},{6,2},{1... | collective-permute-start | bytes 1572872 | tf_op jit(solution)/shard_map/ppermute | solution.py:24
  242.2 19.1 %collective-permute-start.37 = (bf16[1,6,128,512]{3,2,1,0:T(8,128)(2,1)}, bf16[1,6,128,512]{3,2,1,0:T(8,128)(2,1)}, u32[]{:S(2)}, u32[]{:S(2)}) collective-permute-start(bf16[1,6,128,512]{3,2,1,0:T(8,128)(2,1)} %pad_maximum_fusion.2), channel_id=1, source_target_pairs={{0,8},{4,12},{8,0},{12,4},{1,9},{5,13},{9,1},{13,5},{2,10},{6,14},... | collective-permute-start | bytes 2359304 | tf_op jit(solution)/shard_map/ppermute | solution.py:24
  243.1 11.2 %collective-permute-start.39 = (bf16[1,1,128,512]{3,2,1,0:T(8,128)(2,1)S(1)}, bf16[1,1,128,512]{3,2,1,0:T(8,128)(2,1)S(1)}, u32[]{:S(2)}, u32[]{:S(2)}) collective-permute-start(bf16[1,1,128,512]{3,2,1,0:T(8,128)(2,1)S(1)} %add_convert_fusion.24), channel_id=1, source_target_pairs={{16,18},{17,19},{18,16},{19,17},{20,22},{21,23},{22,20},{23,21},{2... | collective-permute-start | bytes 393224 | tf_op jit(solution)/shard_map/ppermute | solution.py:54
  245.2 10.1 %collective-permute-start.38 = (bf16[1,2,128,512]{3,2,1,0:T(8,128)(2,1)S(1)}, bf16[1,2,128,512]{3,2,1,0:T(8,128)(2,1)S(1)}, u32[]{:S(2)}, u32[]{:S(2)}) collective-permute-start(bf16[1,2,128,512]{3,2,1,0:T(8,128)(2,1)S(1)} %get-tuple-element.199), channel_id=1, source_target_pairs={{0,1},{1,0},{2,3},{3,2},{4,5},{5,4},{6,7},{7,6},{8,9},{9,8},{10,11... | collective-permute-start | bytes 786440 | tf_op jit(solution)/shard_map/ppermute | solution.py:24
  250.6 32.3 %all-to-all-start.3 = ((bf16[4,128,512]{2,1,0:T(8,128)(2,1)}), bf16[4,128,512]{2,1,0:T(8,128)(2,1)S(1)}, u32[]{:S(2)}, u32[]{:S(2)}) async-start(bf16[4,128,512]{2,1,0:T(8,128)(2,1)} %bitcast.162), calls=%async_computation.3 | async-start | bytes 1048576 | tf_op jit(solution)/shard_map/all_to_all | solution.py:112
  263.3 3.4 %collective-permute-start.41 = (f32[2,4,6,32]{3,2,1,0:T(8,128)S(1)}, f32[2,4,6,32]{3,2,1,0:T(8,128)S(1)}, u32[]{:S(2)}, u32[]{:S(2)}) collective-permute-start(f32[2,4,6,32]{3,2,1,0:T(8,128)S(1)} %pad_maximum_fusion.15), channel_id=1, source_target_pairs={{0,4},{4,0},{8,12},{12,8},{1,5},{5,1},{9,13},{13,9},{2,6},{6,2},{1... | collective-permute-start | bytes 18440 | tf_op jit(solution)/shard_map/ppermute | solution.py:24
  266.7 2.7 collective-permute-start.42
  269.5 12.5 %collective-permute-start.44 = (bf16[1,2,144,512]{3,2,1,0:T(8,128)(2,1)S(1)}, bf16[1,2,144,512]{3,2,1,0:T(8,128)(2,1)S(1)}, u32[]{:S(2)}, u32[]{:S(2)}) collective-permute-start(bf16[1,2,144,512]{3,2,1,0:T(8,128)(2,1)S(1)} %pad_maximum_fusion.8), channel_id=1, source_target_pairs={{0,1},{1,0},{2,3},{3,2},{4,5},{5,4},{6,7},{7,6},{8,9},{9,8},{10,11... | collective-permute-start | bytes 884744 | tf_op jit(solution)/shard_map/ppermute | solution.py:24
  269.9 13.0 %collective-permute-start.40 = (bf16[1,2,128,512]{3,2,1,0:T(8,128)(2,1)S(1)}, bf16[1,2,128,512]{3,2,1,0:T(8,128)(2,1)S(1)}, u32[]{:S(2)}, u32[]{:S(2)}) collective-permute-start(bf16[1,2,128,512]{3,2,1,0:T(8,128)(2,1)S(1)} %pad_maximum_fusion.10), channel_id=1, source_target_pairs={{0,2},{1,3},{2,0},{3,1},{4,6},{5,7},{6,4},{7,5},{8,10},{9,11},{10,... | collective-permute-start | bytes 786440 | tf_op jit(solution)/shard_map/ppermute | solution.py:24
  271.1 11.8 %collective-permute-start.43 = (bf16[128,4,64]{0,2,1:T(8,128)(2,1)S(1)}, bf16[128,4,64]{0,2,1:T(8,128)(2,1)S(1)}, u32[]{:S(2)}, u32[]{:S(2)}) collective-permute-start(bf16[128,4,64]{0,2,1:T(8,128)(2,1)S(1)} %fusion.3), channel_id=1, source_target_pairs={{16,0},{17,1},{18,2},{19,3},{20,4},{21,5},{22,6},{23,7},{24,8},{25... | collective-permute-start | bytes 196616 | tf_op jit(solution)/shard_map/ppermute | solution.py:32
  282.7 9.6 %collective-permute-start.47 = (bf16[1,1,144,512]{3,2,1,0:T(8,128)(2,1)}, bf16[1,1,144,512]{3,2,1,0:T(8,128)(2,1)S(1)}, u32[]{:S(2)}, u32[]{:S(2)}) collective-permute-start(bf16[1,1,144,512]{3,2,1,0:T(8,128)(2,1)} %add_convert_fusion.18), channel_id=1, source_target_pairs={{0,2},{1,3},{2,0},{3,1},{4,6},{5,7},{6,4},{7,5},{8,10},{9,11},{10,... | collective-permute-start | bytes 442376 | tf_op jit(solution)/shard_map/ppermute | solution.py:24
  286.1 9.7 %collective-permute-start.45 = (bf16[2,128,512]{2,1,0:T(8,128)(2,1)S(1)}, bf16[2,128,512]{2,1,0:T(8,128)(2,1)S(1)}, u32[]{:S(2)}, u32[]{:S(2)}) collective-permute-start(bf16[2,128,512]{2,1,0:T(8,128)(2,1)S(1)} %get-tuple-element.207), channel_id=1, source_target_pairs={{0,4},{4,0},{8,12},{12,8},{1,5},{5,1},{9,13},{13,9},{2,6},{6,2},{1... | collective-permute-start | bytes 786440 | tf_op jit(solution)/shard_map/ppermute | solution.py:24
  288.5 8.3 %collective-permute-start.46 = (bf16[2,128,512]{2,1,0:T(8,128)(2,1)S(1)}, bf16[2,128,512]{2,1,0:T(8,128)(2,1)S(1)}, u32[]{:S(2)}, u32[]{:S(2)}) collective-permute-start(bf16[2,128,512]{2,1,0:T(8,128)(2,1)S(1)} %get-tuple-element.205), channel_id=1, source_target_pairs={{0,4},{4,0},{8,12},{12,8},{1,5},{5,1},{9,13},{13,9},{2,6},{6,2},{1... | collective-permute-start | bytes 786440 | tf_op jit(solution)/shard_map/ppermute | solution.py:24
  (22 other events, 166.0 us)
